TPU v7x, 32 devices: a whole 2x2x4 slice. The times are simulated.
32 devices in a mesh: seq: 8 (over z, y), head: 4 (over x, core).
Axes of the slice: x: 2, y: 2, z: 4, core: 2. Of those that a mesh axis runs over, the one named last changes fastest.
Arguments:
- queries: bfloat16 [2048, 4096], P('seq', 'head'), may hold values from -6 to 6
- keys: bfloat16 [2048, 512], P(('seq', 'head')), may hold values from -6 to 6
- values: bfloat16 [2048, 512], P(('seq', 'head')), may hold values from -6 to 6
- d_out: bfloat16 [2048, 4096], P('seq', 'head'), may hold values from -6 to 6
- rand_blocks: int32 [32, 8], P('seq'), may hold values from 0 to 31, as said below
- glob_blocks: int32 [2], replicated, may hold values from 0 to 31
Outputs:
- attn_out: bfloat16 [2048, 4096], P('seq', 'head')
- d_queries: bfloat16 [2048, 4096], P('seq', 'head')
- d_keys: bfloat16 [2048, 512], P(('seq', 'head'))
- d_values: bfloat16 [2048, 512], P(('seq', 'head'))
Inputs may be any that keep to these rules, and one draw needn't show every extreme that they name: `rand_blocks`: block b lies on index b // 4 of seq. Among the 32 entries of the query blocks of one index of seq, at most 4 name blocks of any one index, and some index of seq reaches 4 for some owner in every draw.
All inputs are finite; a program needn't handle non-finite values.
Results may differ from a plain program's by a relative error of at most 0.012.
Values may be sent and summed in bfloat16 or wider, within the bound.
No kernel may reach another device: no remote copies, remote signals or barrier semaphores. Data moves between devices by JAX's collectives and lax.ppermute only.
A program may use at most 64 MiB of HBM per device.

v0:
```python
import jax
import jax.numpy as jnp
from jax import lax
from jax.sharding import PartitionSpec as P

DH = 128
KVH = 4
BLOCK = 64
GLOB = 2
RAND = 8


NEG_FILL = -1e30


def padded_2(cells, sides, width):
    for axis, dim in sides:
        count = lax.axis_size(axis)
        ends = count - 1
        head = lax.slice_in_dim(cells, 0, width, axis=dim)
        tail = lax.slice_in_dim(cells, cells.shape[dim] - width, cells.shape[dim], axis=dim)
        cells = jnp.concatenate(
            [
                lax.ppermute(tail, axis, [(i, (i + 1) % count) for i in range(ends)]),
                cells,
                lax.ppermute(head, axis, [((i + 1) % count, i) for i in range(ends)]),
            ],
            axis=dim,
        )
    return cells


def broadcast(block, axis, source):
    block = jnp.where(lax.axis_index(axis) == source, block, jnp.zeros_like(block))
    return lax.psum(block, axis)


def key_rows(library, spots):
    chosen = library[spots]
    flat = chosen.reshape(chosen.shape[0] * chosen.shape[1], chosen.shape[2])
    return (flat[:, :DH], flat[:, DH:])


def masked_scores(query_block, keys_here, allowed_row):
    factor = DH ** (-0.5)
    scores = (
        jnp.einsum("thd,kd->htk", query_block, keys_here, preferred_element_type=jnp.float32)
        * factor
    )
    widened = jnp.repeat(allowed_row, keys_here.shape[0] // allowed_row.shape[0])
    return jnp.where(widened[None, None, :], scores, NEG_FILL)


def body(queries, keys, values, d_out, rand_blocks, glob_blocks):
    seq_count = lax.axis_size("seq")
    here = lax.axis_index("seq")
    short = keys.shape[0]
    stacked = jnp.concatenate(
        [keys.reshape(short, KVH, DH), values.reshape(short, KVH, DH)], axis=2
    )
    mine = lax.all_to_all(stacked, "head", split_axis=1, concat_axis=0, tiled=True)
    tok_count = mine.shape[0]
    blocks_here = tok_count // BLOCK
    flat_pairs = mine.reshape(tok_count, 2 * DH)
    own_blocks = flat_pairs.reshape(blocks_here, BLOCK, 2 * DH)
    padded = padded_2(flat_pairs, (("seq", 0),), BLOCK)
    window = padded.reshape(blocks_here + 2, BLOCK, 2 * DH)
    global_parts = []
    for number in range(GLOB):
        target = glob_blocks[number]
        piece = lax.dynamic_index_in_dim(own_blocks, target % blocks_here, 0, keepdims=False)
        global_parts.append(broadcast(piece, "seq", target // blocks_here))
    global_pairs = jnp.stack(global_parts)
    entries = rand_blocks.reshape(-1)
    entry_count = entries.shape[0]
    capacity = -(-entry_count // seq_count)
    position_count = seq_count * capacity
    owners = entries // blocks_here
    inner_index = entries % blocks_here
    order = jnp.arange(entry_count, dtype=jnp.int32)
    earlier = (owners[:, None] == owners[None, :]) & (order[:, None] > order[None, :])
    ranks = jnp.sum(earlier.astype(jnp.int32), axis=1)
    slots = owners * capacity + ranks
    placing = slots[None, :] == jnp.arange(position_count, dtype=jnp.int32)[:, None]
    wanted = jnp.sum(jnp.where(placing, inner_index[None, :], 0), axis=1).reshape(
        seq_count, capacity
    )
    incoming = lax.all_to_all(wanted, "seq", split_axis=0, concat_axis=0, tiled=True).reshape(
        position_count
    )
    served = own_blocks[incoming].reshape(seq_count, capacity, BLOCK, 2 * DH)
    fetched = lax.all_to_all(served, "seq", split_axis=0, concat_axis=0, tiled=True).reshape(
        position_count, BLOCK, 2 * DH
    )
    block_ids = jnp.arange(blocks_here, dtype=jnp.int32)
    window_ids = jnp.stack([block_ids, block_ids + 1, block_ids + 2], axis=1)
    global_ids = jnp.broadcast_to(
        blocks_here + 2 + jnp.arange(GLOB, dtype=jnp.int32), (blocks_here, GLOB)
    )
    random_ids = blocks_here + 2 + GLOB + slots.reshape(blocks_here, RAND)
    positions = jnp.concatenate([window_ids, global_ids, random_ids], axis=1)
    allowed = jnp.concatenate(
        [
            jnp.logical_not((block_ids == 0) & (here == 0))[:, None],
            jnp.ones((blocks_here, 1), jnp.bool_),
            jnp.logical_not((block_ids == blocks_here - 1) & (here == seq_count - 1))[:, None],
            jnp.ones((blocks_here, GLOB + RAND), jnp.bool_),
        ],
        axis=1,
    )
    library = jnp.concatenate([window, global_pairs, fetched], axis=0)
    heads_here = queries.shape[1] // DH
    query_blocks = queries.reshape(blocks_here, BLOCK, heads_here, DH)
    grad_blocks = d_out.reshape(blocks_here, BLOCK, heads_here, DH)

    def forward_step(inputs):
        query_block, spots, allowed_row = inputs
        keys_here, values_here = key_rows(library, spots)
        scores = masked_scores(query_block, keys_here, allowed_row)
        peak = jnp.max(scores, axis=-1, keepdims=True)
        logsum = peak + jnp.log(jnp.sum(jnp.exp(scores - peak), axis=-1, keepdims=True))
        probs16 = jnp.exp(scores - logsum).astype(jnp.bfloat16)
        result = jnp.einsum("htk,kd->thd", probs16, values_here, preferred_element_type=jnp.float32)
        return (result.astype(jnp.bfloat16), logsum)

    out_blocks, logsums = lax.map(forward_step, (query_blocks, positions, allowed))
    refetched = lax.all_to_all(served, "seq", split_axis=0, concat_axis=0, tiled=True).reshape(
        position_count, BLOCK, 2 * DH
    )
    library_back = jnp.concatenate([window, global_pairs, refetched], axis=0)

    def backward_step(inputs):
        query_block, gradient_tile, out_block, logsum, spots, allowed_row = inputs
        keys_here, values_here = key_rows(library_back, spots)
        factor = DH ** (-0.5)
        scores = masked_scores(query_block, keys_here, allowed_row)
        probs = jnp.exp(scores - logsum)
        probs16 = probs.astype(jnp.bfloat16)
        delta = jnp.sum(gradient_tile.astype(jnp.float32) * out_block.astype(jnp.float32), axis=-1)
        dprobs = jnp.einsum(
            "thd,kd->htk", gradient_tile, values_here, preferred_element_type=jnp.float32
        )
        dscores = (probs * (dprobs - jnp.transpose(delta)[:, :, None])).astype(jnp.bfloat16)
        dquery = (
            jnp.einsum("htk,kd->thd", dscores, keys_here, preferred_element_type=jnp.float32)
            * factor
        )
        dkey = (
            jnp.einsum("htk,thd->kd", dscores, query_block, preferred_element_type=jnp.float32)
            * factor
        )
        dvalue = jnp.einsum(
            "htk,thd->kd", probs16, gradient_tile, preferred_element_type=jnp.float32
        )
        terms = jnp.concatenate([dkey, dvalue], axis=1).reshape(spots.shape[0], BLOCK, 2 * DH)
        return (dquery.astype(jnp.bfloat16), terms)

    dquery_blocks, terms = lax.map(
        backward_step, (query_blocks, grad_blocks, out_blocks, logsums, positions, allowed)
    )
    attn_out = out_blocks.reshape(tok_count, heads_here * DH)
    d_queries = dquery_blocks.reshape(tok_count, heads_here * DH)
    prev_terms = terms[:, 0]
    self_terms = terms[:, 1]
    next_terms = terms[:, 2]
    zero_block = jnp.zeros((1, BLOCK, 2 * DH), jnp.float32)
    grads = (
        self_terms
        + jnp.concatenate([prev_terms[1:], zero_block], axis=0)
        + jnp.concatenate([zero_block, next_terms[:-1]], axis=0)
    )
    rims = jnp.concatenate([prev_terms[0], next_terms[-1]], axis=0).astype(jnp.bfloat16)
    arrived = padded_2(rims, (("seq", 0),), BLOCK)
    from_left = arrived[:BLOCK].astype(jnp.float32)
    from_right = arrived[3 * BLOCK :].astype(jnp.float32)
    edge_first = jnp.concatenate(
        [from_left[None], jnp.zeros((blocks_here - 1, BLOCK, 2 * DH), jnp.float32)], axis=0
    )
    edge_last = jnp.concatenate(
        [jnp.zeros((blocks_here - 1, BLOCK, 2 * DH), jnp.float32), from_right[None]], axis=0
    )
    grads = grads + edge_first + edge_last
    global_terms = jnp.sum(terms[:, 3 : 3 + GLOB], axis=0)
    global_total = lax.psum(global_terms, "seq")
    global_hits = ((glob_blocks // blocks_here)[:, None] == here) & (
        (glob_blocks % blocks_here)[:, None] == block_ids[None, :]
    )
    grads = grads + jnp.sum(
        jnp.where(global_hits[:, :, None, None], global_total[:, None], 0.0), axis=0
    )
    random_terms = terms[:, 3 + GLOB :].reshape(entry_count, BLOCK * 2 * DH).astype(jnp.bfloat16)
    outgoing = jnp.dot(
        placing.astype(jnp.bfloat16), random_terms, preferred_element_type=jnp.float32
    ).astype(jnp.bfloat16)
    returned = lax.all_to_all(
        outgoing.reshape(seq_count, capacity, BLOCK, 2 * DH),
        "seq",
        split_axis=0,
        concat_axis=0,
        tiled=True,
    )
    landing = (incoming[None, :] == block_ids[:, None]).astype(jnp.bfloat16)
    grads = grads + jnp.dot(
        landing,
        returned.reshape(position_count, BLOCK * 2 * DH),
        preferred_element_type=jnp.float32,
    ).reshape(blocks_here, BLOCK, 2 * DH)
    packed = grads.astype(jnp.bfloat16).reshape(tok_count, 1, 2 * DH)
    restored = lax.all_to_all(packed, "head", split_axis=0, concat_axis=1, tiled=True)
    d_keys = restored[:, :, :DH].reshape(short, KVH * DH)
    d_values = restored[:, :, DH:].reshape(short, KVH * DH)
    return (attn_out, d_queries, d_keys, d_values)


def solution(mesh):
    in_specs = (
        P("seq", "head"),
        P(("seq", "head"), None),
        P(("seq", "head"), None),
        P("seq", "head"),
        P("seq", None),
        P(),
    )
    out_specs = (
        P("seq", "head"),
        P("seq", "head"),
        P(("seq", "head"), None),
        P(("seq", "head"), None),
    )
    return jax.shard_map(body, mesh=mesh, in_specs=in_specs, out_specs=out_specs, check_vma=False)
```

profile of v0, /device:TPU:0, one launch (start us, length us, event | category | flops | bytes accessed | tf_op | source)
XLA Modules:
  0.0 269.6 jit_solution(16533609476727897413)
XLA Ops:
  9.0 7.3 %all-to-all-start.1 = ((s32[8,1,4]{2,1,0:T(1,128)}), s32[8,1,4]{2,1,0:T(1,128)S(1)}, u32[]{:S(2)}, u32[]{:S(2)}) async-start(s32[8,1,4]{2,1,0:T(1,128)} %bitcast.41), calls=%async_computation.1 | async-start | bytes 8192 | tf_op jit(solution)/shard_map/all_to_all | solution.py:88
  17.8 4.8 %all-to-all-done.1 = s32[8,1,4]{2,1,0:T(1,128)S(1)} async-done(((s32[8,1,4]{2,1,0:T(1,128)}), s32[8,1,4]{2,1,0:T(1,128)S(1)}, u32[]{:S(2)}, u32[]{:S(2)}) %all-to-all-start.1) | async-done | bytes 160 | tf_op jit(solution)/shard_map/all_to_all | solution.py:88
  22.7 3.3 %all-to-all-start = ((bf16[64,4,256]{2,0,1:T(8,128)(2,1)}), bf16[64,4,256]{2,0,1:T(8,128)(2,1)S(1)}, u32[]{:S(2)}, u32[]{:S(2)}) async-start(bf16[64,4,256]{2,0,1:T(8,128)(2,1)} %pad_maximum_fusion.3), calls=%async_computation | async-start | bytes 262144 | tf_op jit(solution)/shard_map/all_to_all | solution.py:61
  27.3 3.3 %all-to-all-done = bf16[64,4,256]{2,0,1:T(8,128)(2,1)S(1)} async-done(((bf16[64,4,256]{2,0,1:T(8,128)(2,1)}), bf16[64,4,256]{2,0,1:T(8,128)(2,1)S(1)}, u32[]{:S(2)}, u32[]{:S(2)}) %all-to-all-start) | async-done | bytes 131104 | tf_op jit(solution)/shard_map/all_to_all | solution.py:61
  30.6 1.6 gather_fusion.2
  32.2 3.6 %all-to-all-start.2 = ((bf16[8,4,64,256]{3,2,1,0:T(8,128)(2,1)}), bf16[8,4,64,256]{3,2,1,0:T(8,128)(2,1)S(1)}, u32[]{:S(2)}, u32[]{:S(2)}) async-start(bf16[8,4,64,256]{3,2,1,0:T(8,128)(2,1)} %bitcast.43), calls=%async_computation.2 | async-start | bytes 2097152 | tf_op jit(solution)/shard_map/all_to_all | solution.py:92
  42.1 1.9 copy.94
  44.3 3.8 %collective-permute-start = (bf16[64,256]{1,0:T(8,128)(2,1)S(1)}, bf16[64,256]{1,0:T(8,128)(2,1)S(1)}, u32[]{:S(2)}, u32[]{:S(2)}) collective-permute-start(bf16[64,256]{1,0:T(8,128)(2,1)S(1)} %get-tuple-element.213), channel_id=1, source_target_pairs={{0,4},{4,8},{8,12},{12,16},{16,20},{20,24},{24,28},{1,5},{5,9},{9,... | collective-permute-start | bytes 98312 | tf_op jit(solution)/shard_map/ppermute | solution.py:24
  48.0 1.3 collective-permute-start.1
  50.0 4.2 %collective-permute-done.1 = bf16[64,256]{1,0:T(8,128)(2,1)S(1)} collective-permute-done((bf16[64,256]{1,0:T(8,128)(2,1)S(1)}, bf16[64,256]{1,0:T(8,128)(2,1)S(1)}, u32[]{:S(2)}, u32[]{:S(2)}) %collective-permute-start.1) | collective-permute-done | bytes 32800 | tf_op jit(solution)/shard_map/ppermute | solution.py:26
  54.2 66.0 %all-reduce.10.cloned.1.call-done = (bf16[1,64,256]{2,1,0:T(8,128)(2,1)}, bf16[1,64,256]{2,1,0:T(8,128)(2,1)}) async-done(((bf16[1,64,256]{2,1,0:T(8,128)(2,1)}, bf16[1,64,256]{2,1,0:T(8,128)(2,1)}), (bf16[1,64,256]{2,1,0:T(8,128)(2,1)}, bf16[1,64,256]{2,1,0:T(8,128)(2,1)})) %all-reduce.10.cloned.1.call-update) | async-done | bytes 65552 | tf_op jit(solution)/shard_map/psum | solution.py:35
  121.1 11.8 %while.24 = (s32[]{:T(128)}, bf16[4,64,8,128]{3,1,2,0:T(8,128)(2,1)}, f32[4,8,64,1]{2,1,3,0:T(8,128)S(1)}, s32[4,13]{1,0:T(4,128)S(1)}, bf16[40,64,256]{2,1,0:T(...) while((s32[]{:T(128)}, bf16[4,64,8,128]{3,1,2,0:T(8,128)(2,1)}, ...), condition=%wide.region_7.8_spmd, body=%wide.region_4.7_spmd.sunk | while | flops 221151776 | bytes 6817576 | solution.py:126
  132.9 27.1 %while.25 = (s32[]{:T(128)}, bf16[4,64,8,128]{3,2,1,0:T(8,128)(2,1)}, f32[4,13,64,256]{3,2,1,0:T(8,128)}, s32[4,13]{1,0:T(4,128)S(1)}, bf16[40,64,256]{2,1,0:T(8...) while((s32[]{:T(128)}, ...), condition=%wide.region_10.11_spmd, body=%wide.region_8.10_spmd.sunk | while | flops 548954624 | bytes 15144784 | solution.py:158
  160.0 2.2 convert.16
  163.8 1.2 copy.97
  165.1 4.7 %all-to-all-start.3 = ((bf16[8,4,64,256]{3,2,1,0:T(8,128)(2,1)}), bf16[8,4,64,256]{3,2,1,0:T(8,128)(2,1)}, u32[]{:S(2)}, u32[]{:S(2)}) async-start(bf16[8,4,64,256]{3,2,1,0:T(8,128)(2,1)} %bitcast.299), calls=%async_computation.3 | async-start | bytes 2097152 | tf_op jit(solution)/shard_map/all_to_all | solution.py:195
  170.0 3.9 %copy.70 = f32[4,13,64,256]{3,0,2,1:T(4,128)} copy(f32[4,13,64,256]{3,2,1,0:T(8,128)S(1)} %copy-done.1) | data formatting | bytes 6815744 | tf_op jit(solution)/shard_map/while | solution.py:158
  175.4 3.9 %collective-permute-start.2 = (bf16[64,256]{1,0:T(8,128)(2,1)S(1)}, bf16[64,256]{1,0:T(8,128)(2,1)S(1)}, u32[]{:S(2)}, u32[]{:S(2)}) collective-permute-start(bf16[64,256]{1,0:T(8,128)(2,1)S(1)} %get-tuple-element.209), channel_id=1, source_target_pairs={{0,4},{4,8},{8,12},{12,16},{16,20},{20,24},{24,28},{1,5},{5,9},{9,... | collective-permute-start | bytes 98312 | tf_op jit(solution)/shard_map/ppermute | solution.py:24
  179.3 1.3 collective-permute-start.3
  181.8 3.3 %collective-permute-done.3 = bf16[64,256]{1,0:T(8,128)(2,1)S(1)} collective-permute-done((bf16[64,256]{1,0:T(8,128)(2,1)S(1)}, bf16[64,256]{1,0:T(8,128)(2,1)S(1)}, u32[]{:S(2)}, u32[]{:S(2)}) %collective-permute-start.3) | collective-permute-done | bytes 32800 | tf_op jit(solution)/shard_map/ppermute | solution.py:26
  185.2 63.0 %all-reduce.8.cloned.1.call-done = f32[2,64,256]{2,1,0:T(8,128)} async-done(((f32[2,64,256]{2,1,0:T(8,128)}), f32[2,64,256]{2,1,0:T(8,128)}) %all-reduce.8.cloned.1.call-update) | async-done | bytes 131088 | tf_op jit(solution)/shard_map/psum | solution.py:184
  249.2 2.3 fusion.30
  253.4 3.3 %all-to-all-start.4 = ((bf16[4,2,8192]{2,1,0:T(2,128)(2,1)}), bf16[4,2,8192]{2,1,0:T(2,128)(2,1)S(1)}, u32[]{:S(2)}, u32[]{:S(2)}) async-start(bf16[4,2,8192]{2,1,0:T(2,128)(2,1)} %reshape.459), calls=%async_computation.4 | async-start | bytes 262144 | tf_op jit(solution)/shard_map/all_to_all | solution.py:209
  258.9 2.4 all-to-all-done.4
  (193 shorter events, 57.0 us)
Async XLA Ops:
  7.2 9.1 %copy-start = (bf16[64,512]{1,0:T(8,128)(2,1)S(1)}, bf16[64,512]{1,0:T(8,128)(2,1)}, u32[]{:S(2)}) copy-start(bf16[64,512]{1,0:T(8,128)(2,1)} %param.11) | copy-start | bytes 196612
  9.0 13.7 %all-to-all-start.1 = ((s32[8,1,4]{2,1,0:T(1,128)}), s32[8,1,4]{2,1,0:T(1,128)S(1)}, u32[]{:S(2)}, u32[]{:S(2)}) async-start(s32[8,1,4]{2,1,0:T(1,128)} %bitcast.41), calls=%async_computation.1 | async-start | bytes 8192 | tf_op jit(solution)/shard_map/all_to_all | solution.py:88
  22.7 7.9 %all-to-all-start = ((bf16[64,4,256]{2,0,1:T(8,128)(2,1)}), bf16[64,4,256]{2,0,1:T(8,128)(2,1)S(1)}, u32[]{:S(2)}, u32[]{:S(2)}) async-start(bf16[64,4,256]{2,0,1:T(8,128)(2,1)} %pad_maximum_fusion.3), calls=%async_computation | async-start | bytes 262144 | tf_op jit(solution)/shard_map/all_to_all | solution.py:61
  30.6 5.2 %copy-start.7 = (s32[2]{0:T(128)S(1)}, s32[2]{0:T(128)}, u32[]{:S(2)}) copy-start(s32[2]{0:T(128)} %param.15) | copy-start | bytes 28
  30.6 11.3 %copy-start.4 = (bf16[256,1024]{1,0:T(8,128)(2,1)S(1)}, bf16[256,1024]{1,0:T(8,128)(2,1)}, u32[]{:S(2)}) copy-start(bf16[256,1024]{1,0:T(8,128)(2,1)} %param.10) | copy-start | bytes 1572868
  32.2 88.0 %all-to-all-start.2 = ((bf16[8,4,64,256]{3,2,1,0:T(8,128)(2,1)}), bf16[8,4,64,256]{3,2,1,0:T(8,128)(2,1)S(1)}, u32[]{:S(2)}, u32[]{:S(2)}) async-start(bf16[8,4,64,256]{3,2,1,0:T(8,128)(2,1)} %bitcast.43), calls=%async_computation.2 | async-start | bytes 2097152 | tf_op jit(solution)/shard_map/all_to_all | solution.py:92
  35.7 8.3 %copy-start.6 = (s32[4,8]{1,0:T(4,128)S(1)}, s32[4,8]{1,0:T(4,128)}, u32[]{:S(2)}) copy-start(s32[4,8]{1,0:T(4,128)} %param.14) | copy-start | bytes 388
  35.7 84.5 %all-reduce.10.cloned.1.call-start = ((), (), s32[]{:S(2)}) async-start(), calls=%async_computation.6 | async-start | bytes 131072 | tf_op jit(solution)/shard_map/psum | solution.py:35
  44.3 5.7 %collective-permute-start = (bf16[64,256]{1,0:T(8,128)(2,1)S(1)}, bf16[64,256]{1,0:T(8,128)(2,1)S(1)}, u32[]{:S(2)}, u32[]{:S(2)}) collective-permute-start(bf16[64,256]{1,0:T(8,128)(2,1)S(1)} %get-tuple-element.213), channel_id=1, source_target_pairs={{0,4},{4,8},{8,12},{12,16},{16,20},{20,24},{24,28},{1,5},{5,9},{9,... | collective-permute-start | bytes 98312 | tf_op jit(solution)/shard_map/ppermute | solution.py:24
  48.0 6.2 %collective-permute-start.1 = (bf16[64,256]{1,0:T(8,128)(2,1)S(1)}, bf16[64,256]{1,0:T(8,128)(2,1)S(1)}, u32[]{:S(2)}, u32[]{:S(2)}) collective-permute-start(bf16[64,256]{1,0:T(8,128)(2,1)S(1)} %get-tuple-element.214), channel_id=1, source_target_pairs={{4,0},{8,4},{12,8},{16,12},{20,16},{24,20},{28,24},{5,1},{9,5},{13... | collective-permute-start | bytes 98312 | tf_op jit(solution)/shard_map/ppermute | solution.py:26
  162.2 1.2 copy-start.2
  163.8 6.2 %copy-start.1 = (f32[4,13,64,256]{3,2,1,0:T(8,128)S(1)}, f32[4,13,64,256]{3,2,1,0:T(8,128)}, u32[]{:S(2)}) copy-start(f32[4,13,64,256]{3,2,1,0:T(8,128)} %get-tuple-element.98) | copy-start | bytes 10223620
  165.1 84.1 %all-to-all-start.3 = ((bf16[8,4,64,256]{3,2,1,0:T(8,128)(2,1)}), bf16[8,4,64,256]{3,2,1,0:T(8,128)(2,1)}, u32[]{:S(2)}, u32[]{:S(2)}) async-start(bf16[8,4,64,256]{3,2,1,0:T(8,128)(2,1)} %bitcast.299), calls=%async_computation.3 | async-start | bytes 2097152 | tf_op jit(solution)/shard_map/all_to_all | solution.py:195
  169.8 78.4 %all-reduce.8.cloned.1.call-start = ((), (), s32[]{:S(2)}) async-start(), calls=%async_computation.5 | async-start | bytes 262144 | tf_op jit(solution)/shard_map/psum | solution.py:184
  175.4 6.3 %collective-permute-start.2 = (bf16[64,256]{1,0:T(8,128)(2,1)S(1)}, bf16[64,256]{1,0:T(8,128)(2,1)S(1)}, u32[]{:S(2)}, u32[]{:S(2)}) collective-permute-start(bf16[64,256]{1,0:T(8,128)(2,1)S(1)} %get-tuple-element.209), channel_id=1, source_target_pairs={{0,4},{4,8},{8,12},{12,16},{16,20},{20,24},{24,28},{1,5},{5,9},{9,... | collective-permute-start | bytes 98312 | tf_op jit(solution)/shard_map/ppermute | solution.py:24
  179.3 5.8 %collective-permute-start.3 = (bf16[64,256]{1,0:T(8,128)(2,1)S(1)}, bf16[64,256]{1,0:T(8,128)(2,1)S(1)}, u32[]{:S(2)}, u32[]{:S(2)}) collective-permute-start(bf16[64,256]{1,0:T(8,128)(2,1)S(1)} %get-tuple-element.210), channel_id=1, source_target_pairs={{4,0},{8,4},{12,8},{16,12},{20,16},{24,20},{28,24},{5,1},{9,5},{13... | collective-permute-start | bytes 98312 | tf_op jit(solution)/shard_map/ppermute | solution.py:26
  249.2 7.5 %copy-start.3 = (bf16[4,64,8,128]{3,1,2,0:T(8,128)(2,1)S(1)}, bf16[4,64,8,128]{3,1,2,0:T(8,128)(2,1)}, u32[]{:S(2)}) copy-start(bf16[4,64,8,128]{3,1,2,0:T(8,128)(2,1)} %get-tuple-element.407) | copy-start | bytes 1572868
  251.5 6.5 %copy-start.5 = (bf16[4,64,8,128]{3,2,1,0:T(8,128)(2,1)S(1)}, bf16[4,64,8,128]{3,2,1,0:T(8,128)(2,1)}, u32[]{:S(2)}) copy-start(bf16[4,64,8,128]{3,2,1,0:T(8,128)(2,1)} %get-tuple-element.97) | copy-start | bytes 1572868
  253.4 7.9 %all-to-all-start.4 = ((bf16[4,2,8192]{2,1,0:T(2,128)(2,1)}), bf16[4,2,8192]{2,1,0:T(2,128)(2,1)S(1)}, u32[]{:S(2)}, u32[]{:S(2)}) async-start(bf16[4,2,8192]{2,1,0:T(2,128)(2,1)} %reshape.459), calls=%async_computation.4 | async-start | bytes 262144 | tf_op jit(solution)/shard_map/all_to_all | solution.py:209
Sparse Core Ops, SparseCore 0:
  50.1 70.0 all-reduce.9
  174.8 73.3 all-reduce.7
where the time goes:
time: 271 us; the launch traced here: 270 us
  waiting for transfers between devices  147 us (54%)
  local copies, waits for them, and re-layouts  37.5 us (14%)
  starting transfers between devices  32.5 us (12%)
  between operations  19.6 us (7%)
  matrix products  18.3 us (7%)
  other arithmetic  14.3 us (5%)
    psum x1, waiting for transfers between devices, broadcast(): return lax.psum(block, axis)  66 us
    psum x1, waiting for transfers between devices, body(): global_total = lax.psum(global_terms, 'seq')  63 us
    ppermute x2, starting transfers between devices, padded_2(): lax.ppermute(tail, axis, [(i, (i + 1) % count) for i in range(ends)])  7.62 us
    ppermute x2, waiting for transfers between devices, padded_2(): lax.ppermute(head, axis, [((i + 1) % count, i) for i in range(ends)])  7.45 us
    all_to_all x1, starting transfers between devices, body(): lax.all_to_all(wanted, 'seq', split_axis=0, concat_axis=0, tiled=True)  7.28 us
    unnamed x27, local copies, waits for them, and re-layouts  7.14 us
  transfers between devices with their start and end apart: 11, of which 7 were waited for; matrix products, arithmetic and copies ran while one was open for 6% of the time, Pallas kernels for 0%

commit v1 on v0

--- a/solution.py
+++ b/solution.py
@@ -1,6 +1,10 @@
+import math
+
 import jax
 import jax.numpy as jnp
 from jax import lax
+from jax.experimental import pallas as pl
+from jax.experimental.pallas import tpu as pltpu
 from jax.sharding import PartitionSpec as P
 
 DH = 128
@@ -36,7 +40,12 @@
 
 
 def key_rows(library, spots):
-    chosen = library[spots]
+    chosen = jnp.stack(
+        [
+            lax.dynamic_index_in_dim(library, spots[i], 0, keepdims=False)
+            for i in range(spots.shape[0])
+        ]
+    )
     flat = chosen.reshape(chosen.shape[0] * chosen.shape[1], chosen.shape[2])
     return (flat[:, :DH], flat[:, DH:])
 
@@ -51,7 +60,7 @@
     return jnp.where(widened[None, None, :], scores, NEG_FILL)
 
 
-def body(queries, keys, values, d_out, rand_blocks, glob_blocks):
+def request_body(queries, keys, values, d_out, rand_blocks, glob_blocks):
     seq_count = lax.axis_size("seq")
     here = lax.axis_index("seq")
     short = keys.shape[0]
@@ -88,11 +97,20 @@
     incoming = lax.all_to_all(wanted, "seq", split_axis=0, concat_axis=0, tiled=True).reshape(
         position_count
     )
-    served = own_blocks[incoming].reshape(seq_count, capacity, BLOCK, 2 * DH)
+    block_ids = jnp.arange(blocks_here, dtype=jnp.int32)
+    picking = (incoming[:, None] == block_ids[None, :]).astype(jnp.bfloat16)
+    served = (
+        jnp.dot(
+            picking,
+            own_blocks.reshape(blocks_here, BLOCK * 2 * DH),
+            preferred_element_type=jnp.float32,
+        )
+        .astype(jnp.bfloat16)
+        .reshape(seq_count, capacity, BLOCK, 2 * DH)
+    )
     fetched = lax.all_to_all(served, "seq", split_axis=0, concat_axis=0, tiled=True).reshape(
         position_count, BLOCK, 2 * DH
     )
-    block_ids = jnp.arange(blocks_here, dtype=jnp.int32)
     window_ids = jnp.stack([block_ids, block_ids + 1, block_ids + 2], axis=1)
     global_ids = jnp.broadcast_to(
         blocks_here + 2 + jnp.arange(GLOB, dtype=jnp.int32), (blocks_here, GLOB)
@@ -212,6 +230,225 @@
     return (attn_out, d_queries, d_keys, d_values)
 
 
+def flips(count, bits):
+    return [(i, i ^ bits) for i in range(count)]
+
+
+def head_columns(head, offset):
+    return pl.ds(pl.multiple_of((head ^ offset) * DH, DH), DH)
+
+
+def pack_kernel(keys_ref, values_ref, *piece_refs):
+    head = lax.axis_index("head")
+    short = keys_ref.shape[0]
+    for offset, piece in enumerate(piece_refs):
+        columns = head_columns(head, offset)
+        piece[:short, :] = keys_ref[:, columns]
+        piece[short:, :] = values_ref[:, columns]
+
+
+def unpack_kernel(*refs):
+    piece_refs, (keys_ref, values_ref) = refs[:-2], refs[-2:]
+    head = lax.axis_index("head")
+    short = keys_ref.shape[0]
+    for offset, piece in enumerate(piece_refs):
+        columns = head_columns(head, offset)
+        keys_ref[:, columns] = piece[:short, :]
+        values_ref[:, columns] = piece[short:, :]
+
+
+def dot(left, right, left_dim, right_dim):
+    return lax.dot_general(
+        left,
+        right,
+        (((left_dim,), (right_dim,)), ((), ())),
+        preferred_element_type=jnp.float32,
+    )
+
+
+def attention_kernel(seq_count, chunk_heads, *refs):
+    rand_ref, glob_ref, query_ref, grad_ref = refs[:4]
+    part_refs = refs[4 : 4 + seq_count]
+    out_ref, dquery_ref, keep_ref, ship_ref = refs[4 + seq_count : 8 + seq_count]
+    library, total, key_rows_ref, value_rows_ref, sems = refs[8 + seq_count :]
+    blocks_here = part_refs[0].shape[0]
+    all_blocks = seq_count * blocks_here
+    heads_here = query_ref.shape[1] // DH
+    step = pl.program_id(0)
+    here = lax.axis_index("seq")
+    head = lax.axis_index("head")
+
+    @pl.when(step == 0)
+    def _():
+        copies = [
+            pltpu.make_async_copy(
+                part, library.at[pl.ds(k * blocks_here, blocks_here)], sems.at[k]
+            )
+            for k, part in enumerate(part_refs)
+        ]
+        for copy in copies:
+            copy.start()
+        total[...] = jnp.zeros_like(total)
+        for copy in copies:
+            copy.wait()
+
+    block = here * blocks_here + step
+    names = [jnp.maximum(block - 1, 0), block, jnp.minimum(block + 1, all_blocks - 1)]
+    names += [glob_ref[i] for i in range(GLOB)]
+    names += [rand_ref[step, i] for i in range(RAND)]
+    spots = []
+    for name in names:
+        owner = lax.div(name, blocks_here)
+        inner = lax.rem(name, blocks_here)
+        spots.append((owner ^ here) * blocks_here + (inner ^ head))
+    for number, spot in enumerate(spots):
+        rows = pl.ds(number * BLOCK, BLOCK)
+        key_rows_ref[rows, :] = library[spot, :BLOCK, :]
+        value_rows_ref[rows, :] = library[spot, BLOCK:, :]
+    first_bias = jnp.where(block == 0, NEG_FILL, 0.0)
+    last_bias = jnp.where(block == all_blocks - 1, NEG_FILL, 0.0)
+    factor = DH ** (-0.5)
+    scale = factor * math.log2(math.e)
+    dkey = None
+    for start in range(0, heads_here, chunk_heads):
+        chunk = range(start, start + chunk_heads)
+        query = jnp.concatenate([query_ref[:, h * DH : (h + 1) * DH] for h in chunk], axis=0)
+        grad = jnp.concatenate([grad_ref[:, h * DH : (h + 1) * DH] for h in chunk], axis=0)
+        scores = dot(key_rows_ref[...], query, 1, 1)
+        scores = jnp.concatenate(
+            [
+                scores[:BLOCK] + first_bias,
+                scores[BLOCK : 2 * BLOCK],
+                scores[2 * BLOCK : 3 * BLOCK] + last_bias,
+                scores[3 * BLOCK :],
+            ],
+            axis=0,
+        )
+        peak = jnp.max(scores, axis=0, keepdims=True)
+        weights = jnp.exp2((scores - peak) * scale)
+        probs = weights * (1.0 / jnp.sum(weights, axis=0, keepdims=True))
+        probs16 = probs.astype(jnp.bfloat16)
+        result = dot(value_rows_ref[...], probs16, 0, 0).astype(jnp.bfloat16)
+        grad_across = jnp.transpose(grad.astype(jnp.float32))
+        delta = jnp.sum(grad_across * result.astype(jnp.float32), axis=0, keepdims=True)
+        dprobs = dot(value_rows_ref[...], grad, 1, 1)
+        dscores = (probs * (dprobs - delta)).astype(jnp.bfloat16)
+        dquery = dot(key_rows_ref[...], dscores, 0, 0) * factor
+        result_down = jnp.transpose(result.astype(jnp.float32)).astype(jnp.bfloat16)
+        dquery_down = jnp.transpose(dquery).astype(jnp.bfloat16)
+        for number, h in enumerate(chunk):
+            rows = slice(number * BLOCK, (number + 1) * BLOCK)
+            out_ref[:, h * DH : (h + 1) * DH] = result_down[rows]
+            dquery_ref[:, h * DH : (h + 1) * DH] = dquery_down[rows]
+        key_term = dot(dscores, query, 1, 0) * factor
+        value_term = dot(probs16, grad, 1, 0)
+        dkey = key_term if dkey is None else dkey + key_term
+        dvalue = value_term if start == 0 else dvalue + value_term
+    for number, spot in enumerate(spots):
+        rows = slice(number * BLOCK, (number + 1) * BLOCK)
+        total[spot, :BLOCK, :] += dkey[rows]
+        total[spot, BLOCK:, :] += dvalue[rows]
+
+    @pl.when(step == pl.num_programs(0) - 1)
+    def _():
+        for pair in range(seq_count // 2):
+            near = pl.ds(2 * pair * blocks_here, blocks_here)
+            far = pl.ds((2 * pair + 1) * blocks_here, blocks_here)
+            keep_ref[pair] = total[near]
+            ship_ref[pair] = total[far].astype(jnp.bfloat16)
+
+
+def attention(rand_blocks, glob_blocks, queries, d_out, parts):
+    seq_count = len(parts)
+    blocks_here, pair_rows, _ = parts[0].shape
+    entries = 3 + GLOB + RAND
+    tok_count, width = queries.shape
+    heads_here = width // DH
+    tile = pl.BlockSpec((BLOCK, width), lambda i: (i, 0))
+    smem = pl.BlockSpec(memory_space=pltpu.SMEM)
+    half = (seq_count // 2, blocks_here, pair_rows, DH)
+    whole = pl.BlockSpec(half, lambda i: (0, 0, 0, 0))
+    all_blocks = seq_count * blocks_here
+    pairs = tok_count * heads_here * entries * BLOCK
+    return pl.pallas_call(
+        lambda *refs: attention_kernel(seq_count, math.gcd(heads_here, 4), *refs),
+        grid=(blocks_here,),
+        in_specs=[smem, smem, tile, tile] + [pl.BlockSpec(memory_space=pl.ANY)] * seq_count,
+        out_specs=[tile, tile, whole, whole],
+        out_shape=[
+            jax.ShapeDtypeStruct(queries.shape, jnp.bfloat16),
+            jax.ShapeDtypeStruct(queries.shape, jnp.bfloat16),
+            jax.ShapeDtypeStruct(half, jnp.float32),
+            jax.ShapeDtypeStruct(half, jnp.bfloat16),
+        ],
+        scratch_shapes=[
+            pltpu.VMEM((all_blocks, pair_rows, DH), jnp.bfloat16),
+            pltpu.VMEM((all_blocks, pair_rows, DH), jnp.float32),
+            pltpu.VMEM((entries * BLOCK, DH), jnp.bfloat16),
+            pltpu.VMEM((entries * BLOCK, DH), jnp.bfloat16),
+            pltpu.SemaphoreType.DMA((seq_count,)),
+        ],
+        compiler_params=pltpu.CompilerParams(vmem_limit_bytes=40 * 1024 * 1024),
+        cost_estimate=pl.CostEstimate(
+            flops=12 * pairs * DH, bytes_accessed=8 * tok_count * width, transcendentals=pairs
+        ),
+    )(rand_blocks, glob_blocks, queries, d_out, *parts)
+
+
+def whole_body(queries, keys, values, d_out, rand_blocks, glob_blocks):
+    seq_count = lax.axis_size("seq")
+    head_count = lax.axis_size("head")
+    short = keys.shape[0]
+    piece = jax.ShapeDtypeStruct((2 * short, DH), jnp.bfloat16)
+    pieces = pl.pallas_call(pack_kernel, out_shape=[piece] * head_count)(keys, values)
+    own = jnp.stack(
+        [pieces[0]]
+        + [
+            lax.ppermute(pieces[k], "head", flips(head_count, k)) for k in range(1, head_count)
+        ]
+    )
+    parts = {0: own}
+    for k in range(seq_count - 2, 0, -2):
+        parts[k] = lax.ppermute(own, "seq", flips(seq_count, k))
+    for k in range(0, seq_count, 2):
+        parts[k + 1] = lax.ppermute(parts[k], "seq", flips(seq_count, 1))
+    attn_out, d_queries, keep, ship = attention(
+        rand_blocks, glob_blocks, queries, d_out, [parts[k] for k in range(seq_count)]
+    )
+    pairs = seq_count // 2
+    half = max(pairs // 2, 1)
+    sums = {}
+    for low in range(pairs - half, -1, -half):
+        arrived = lax.ppermute(ship[low : low + half], "seq", flips(seq_count, 1))
+        for number in range(half):
+            pair = low + number
+            sums[pair] = keep[pair] + arrived[number].astype(jnp.float32)
+    total = sums[0]
+    for pair in range(pairs - 1, 0, -1):
+        total = total + lax.ppermute(
+            sums[pair].astype(jnp.bfloat16), "seq", flips(seq_count, 2 * pair)
+        ).astype(jnp.float32)
+    packed = total.astype(jnp.bfloat16)
+    back = [packed[0]] + [
+        lax.ppermute(packed[k], "head", flips(head_count, k)) for k in range(1, head_count)
+    ]
+    flat = jax.ShapeDtypeStruct(keys.shape, jnp.bfloat16)
+    d_keys, d_values = pl.pallas_call(unpack_kernel, out_shape=[flat, flat])(*back)
+    return (attn_out, d_queries, d_keys, d_values)
+
+
+def body(queries, keys, values, d_out, rand_blocks, glob_blocks):
+    seq_count = lax.axis_size("seq")
+    head_count = lax.axis_size("head")
+    blocks_here = rand_blocks.shape[0]
+    capacity = -(-rand_blocks.size // seq_count)
+    powers = all(n & (n - 1) == 0 for n in (seq_count, head_count))
+    fits = keys.shape[0] == BLOCK and blocks_here == head_count
+    if capacity >= blocks_here and seq_count > 1 and powers and fits:
+        return whole_body(queries, keys, values, d_out, rand_blocks, glob_blocks)
+    return request_body(queries, keys, values, d_out, rand_blocks, glob_blocks)
+
+
 def solution(mesh):
     in_specs = (
         P("seq", "head"),

time: 271 us -> 79 us (0.29)
  waiting for transfers between devices: 147 us -> 36.5 us
  local copies, waits for them, and re-layouts: 37.5 us -> 3.37 us
  between operations: 19.6 us -> 0.69 us
  matrix products: 18.3 us -> 0 us
  Pallas kernels: 0 us -> 16 us
  other arithmetic: 14.3 us -> 1.01 us
  starting transfers between devices: 32.5 us -> 21 us
    psum x2 -> x0, waiting for transfers between devices: 129 us -> none  [the longest x1 66 us: broadcast(): return lax.psum(block, axis)]
    ppermute x4 -> x18, waiting for transfers between devices: 7.46 us -> 36.5 us  [the longest x2 10.3 us: whole_body(): arrived = lax.ppermute(ship[low:low + half], 'seq', flips(seq_count, 1))]
    all_to_all x5 -> x0, starting transfers between devices: 22.2 us -> none  [the longest x1 7.28 us: body(): lax.all_to_all(wanted, 'seq', split_axis=0, concat_axis=0, tiled=True)]
    dot_general x30 -> x0, matrix products: 18.3 us -> none  [the longest x4 4.71 us: forward_step(): jnp.einsum('htk,kd->thd', probs16, values_here, preferred_element_type=jn...]
    pallas_call x0 -> x3, Pallas kernels: none -> 16 us  [the longest x1 13 us: attention(): pl.pallas_call(lambda *refs: attention_kernel(seq_count, math.gcd(heads_h...]
    ppermute x4 -> x18, starting transfers between devices: 10.2 us -> 21 us  [the longest x4 5.07 us: whole_body(): parts[k + 1] = lax.ppermute(parts[k], 'seq', flips(seq_count, 1))]
    all_to_all x5 -> x0, waiting for transfers between devices: 10.6 us -> none  [the longest x1 4.84 us: body(): lax.all_to_all(wanted, 'seq', split_axis=0, concat_axis=0, tiled=True)]
    reduce_sum x12 -> x0, other arithmetic: 7.98 us -> none  [the longest x4 4.2 us: backward_step(): jnp.sum(gradient_tile.astype(jnp.float32) * out_block.astype(jnp.float32)...]
  transfers between devices with their start and end apart: 11 -> 18, of which waited for: 7 -> 12; matrix products, arithmetic and copies ran while one was open for 6% -> 0% of each run, Pallas kernels for 0% -> 0%
where the time goes in v1:
time: 79 us; the launch traced here: 78.6 us
  waiting for transfers between devices  36.5 us (46%)
  starting transfers between devices  21 us (27%)
  Pallas kernels  16 us (20%)
  local copies, waits for them, and re-layouts  3.37 us (4%)
  other arithmetic  1.01 us (1%)
    pallas_call x1, Pallas kernels, attention(): pl.pallas_call(lambda *refs: attention_kernel(seq_count, math.gcd(heads_h...  13 us
    ppermute x2, waiting for transfers between devices, whole_body(): arrived = lax.ppermute(ship[low:low + half], 'seq', flips(seq_count, 1))  10.3 us
    ppermute x3, waiting for transfers between devices, whole_body(): parts[k] = lax.ppermute(own, 'seq', flips(seq_count, k))  7.64 us
    ppermute x3, waiting for transfers between devices, whole_body(): lax.ppermute(sums[pair].astype(jnp.bfloat16), 'seq', flips(seq_count, 2 *...  7.42 us
    ppermute x4, waiting for transfers between devices, whole_body(): parts[k + 1] = lax.ppermute(parts[k], 'seq', flips(seq_count, 1))  5.59 us
    ppermute x4, starting transfers between devices, whole_body(): parts[k + 1] = lax.ppermute(parts[k], 'seq', flips(seq_count, 1))  5.07 us
    ppermute x3, starting transfers between devices, whole_body(): lax.ppermute(sums[pair].astype(jnp.bfloat16), 'seq', flips(seq_count, 2 *...  4.45 us
    ppermute x3, starting transfers between devices, whole_body(): parts[k] = lax.ppermute(own, 'seq', flips(seq_count, k))  4.45 us
  transfers between devices with their start and end apart: 18, of which 12 were waited for; matrix products, arithmetic and copies ran while one was open for 0% of the time, Pallas kernels for 0%

profile of v1, /device:TPU:0, one launch (start us, length us, event | category | flops | bytes accessed | tf_op | source)
XLA Modules:
  0.0 78.6 jit_solution(16620868485306208959)
XLA Ops:
  0.6 1.5 %shard_map.93 = (bf16[128,128]{1,0:T(8,128)(2,1)}, bf16[128,128]{1,0:T(8,128)(2,1)}, bf16[128,128]{1,0:T(8,128)(2,1)}, bf16[128,128]{1,0:T(8,128)(2,1)}) custom-call(bf16[64,512]{1,0:T(8,128)(2,1)} %keys_ref.1, bf16[64,512]{1,0:T(8,128)(2,1)} %values_ref.1), custom_call_target="tpu_custom_call" | custom-call | tf_op jit(solution)/shard_map/pallas_call | solution.py:403
  2.6 2.5 %collective-permute-start.1 = (bf16[128,128]{1,0:T(8,128)(2,1)}, bf16[128,128]{1,0:T(8,128)(2,1)S(1)}, u32[]{:S(2)}, u32[]{:S(2)}) collective-permute-start(bf16[128,128]{1,0:T(8,128)(2,1)} %get-tuple-element.16), channel_id=1, source_target_pairs={{0,2},{1,3},{2,0},{3,1},{4,6},{5,7},{6,4},{7,5},{8,10},{9,11},{10,... | collective-permute-start | bytes 98312 | tf_op jit(solution)/shard_map/ppermute | solution.py:407
  5.3 2.1 %collective-permute-done.1 = bf16[128,128]{1,0:T(8,128)(2,1)S(1)} collective-permute-done((bf16[128,128]{1,0:T(8,128)(2,1)}, bf16[128,128]{1,0:T(8,128)(2,1)S(1)}, u32[]{:S(2)}, u32[]{:S(2)}) %collective-permute-start.1) | collective-permute-done | bytes 32800 | tf_op jit(solution)/shard_map/ppermute | solution.py:407
  7.4 1.3 %collective-permute-done.2 = bf16[128,128]{1,0:T(8,128)(2,1)S(1)} collective-permute-done((bf16[128,128]{1,0:T(8,128)(2,1)}, bf16[128,128]{1,0:T(8,128)(2,1)S(1)}, u32[]{:S(2)}, u32[]{:S(2)}) %collective-permute-start.2) | collective-permute-done | bytes 32800 | tf_op jit(solution)/shard_map/ppermute | solution.py:407
  9.5 3.7 %collective-permute-start.8 = (bf16[4,128,128]{2,1,0:T(8,128)(2,1)S(1)}, bf16[4,128,128]{2,1,0:T(8,128)(2,1)S(1)}, u32[]{:S(2)}, u32[]{:S(2)}) collective-permute-start(bf16[4,128,128]{2,1,0:T(8,128)(2,1)S(1)} %pad_maximum_fusion.refs_4_), channel_id=1, source_target_pairs={{0,24},{4,28},{8,16},{12,20},{16,8},{20,12},{24,0},{28,4},{1,25},{... | collective-permute-start | bytes 393224 | tf_op jit(solution)/shard_map/ppermute | solution.py:412
  13.9 1.5 %collective-permute-start.3 = (bf16[4,128,128]{2,1,0:T(8,128)(2,1)S(1)}, bf16[4,128,128]{2,1,0:T(8,128)(2,1)S(1)}, u32[]{:S(2)}, u32[]{:S(2)}) collective-permute-start(bf16[4,128,128]{2,1,0:T(8,128)(2,1)S(1)} %pad_maximum_fusion.refs_4_), channel_id=1, source_target_pairs={{0,4},{4,0},{8,12},{12,8},{16,20},{20,16},{24,28},{28,24},{1,5},{5... | collective-permute-start | bytes 393224 | tf_op jit(solution)/shard_map/ppermute | solution.py:414
  15.5 2.3 %collective-permute-done.8.refs_10_ = bf16[4,128,128]{2,1,0:T(8,128)(2,1)S(1)} collective-permute-done((bf16[4,128,128]{2,1,0:T(8,128)(2,1)S(1)}, bf16[4,128,128]{2,1,0:T(8,128)(2,1)S(1)}, u32[]{:S(2)}, u32[]{:S(2)}) %collective-permute-start.8) | collective-permute-done | bytes 131104 | tf_op jit(solution)/shard_map/ppermute | solution.py:412
  17.8 1.5 %collective-permute-start.9 = (bf16[4,128,128]{2,1,0:T(8,128)(2,1)S(1)}, bf16[4,128,128]{2,1,0:T(8,128)(2,1)S(1)}, u32[]{:S(2)}, u32[]{:S(2)}) collective-permute-start(bf16[4,128,128]{2,1,0:T(8,128)(2,1)S(1)} %collective-permute-done.8.refs_10_), channel_id=1, source_target_pairs={{0,4},{4,0},{8,12},{12,8},{16,20},{20,16},{24,28},{28,24},{1,5},{5... | collective-permute-start | bytes 393224 | tf_op jit(solution)/shard_map/ppermute | solution.py:414
  19.3 5.3 %collective-permute-done.6.refs_8_ = bf16[4,128,128]{2,1,0:T(8,128)(2,1)S(1)} collective-permute-done((bf16[4,128,128]{2,1,0:T(8,128)(2,1)S(1)}, bf16[4,128,128]{2,1,0:T(8,128)(2,1)S(1)}, u32[]{:S(2)}, u32[]{:S(2)}) %collective-permute-start.6) | collective-permute-done | bytes 131104 | tf_op jit(solution)/shard_map/ppermute | solution.py:412
  24.6 1.5 %collective-permute-start.7 = (bf16[4,128,128]{2,1,0:T(8,128)(2,1)S(1)}, bf16[4,128,128]{2,1,0:T(8,128)(2,1)S(1)}, u32[]{:S(2)}, u32[]{:S(2)}) collective-permute-start(bf16[4,128,128]{2,1,0:T(8,128)(2,1)S(1)} %collective-permute-done.6.refs_8_), channel_id=1, source_target_pairs={{0,4},{4,0},{8,12},{12,8},{16,20},{20,16},{24,28},{28,24},{1,5},{5... | collective-permute-start | bytes 393224 | tf_op jit(solution)/shard_map/ppermute | solution.py:414
  26.6 4.2 %collective-permute-done.7.refs_9_ = bf16[4,128,128]{2,1,0:T(8,128)(2,1)S(1)} collective-permute-done((bf16[4,128,128]{2,1,0:T(8,128)(2,1)S(1)}, bf16[4,128,128]{2,1,0:T(8,128)(2,1)S(1)}, u32[]{:S(2)}, u32[]{:S(2)}) %collective-permute-start.7) | collective-permute-done | bytes 131104 | tf_op jit(solution)/shard_map/ppermute | solution.py:414
  30.8 1.4 %collective-permute-done.5.refs_7_ = bf16[4,128,128]{2,1,0:T(8,128)(2,1)S(1)} collective-permute-done((bf16[4,128,128]{2,1,0:T(8,128)(2,1)S(1)}, bf16[4,128,128]{2,1,0:T(8,128)(2,1)S(1)}, u32[]{:S(2)}, u32[]{:S(2)}) %collective-permute-start.5) | collective-permute-done | bytes 131104 | tf_op jit(solution)/shard_map/ppermute | solution.py:414
  32.2 1.0 %copy-done = bf16[256,1024]{1,0:T(8,128)(2,1)S(1)} copy-done((bf16[256,1024]{1,0:T(8,128)(2,1)S(1)}, bf16[256,1024]{1,0:T(8,128)(2,1)}, u32[]{:S(2)}) %copy-start) | copy-done | bytes 524312
  34.3 13.0 %shard_map.94 = (bf16[256,1024]{1,0:T(8,128)(2,1)}, bf16[256,1024]{1,0:T(8,128)(2,1)}, f32[4,4,128,128]{3,2,1,0:T(8,128)S(1)}, bf16[4,4,128,128]{3,2,1,0:T(8,128)(2,1)S(1)}) custom-call(s32[4,8]{1,0:T(4,128)S(1)} %copy-done.2, s32[2]{0:T(128)S(1)} %copy-done.3, bf16[256,1024]{1,0:T(8,128)(2,1)S(1)} %copy-done, bf16[256,1024]{1,0:T(8,128)(2,1)S(1)} %copy-done.1, ...), custom_call_target="tpu_custom_call" | custom-call | flops 2617245696 | bytes 2097152 | tf_op jit(solution)/shard_map/pallas_call | solution.py:373
  47.3 1.6 %collective-permute-start.11 = (bf16[2,4,128,128]{3,2,1,0:T(8,128)(2,1)S(1)}, bf16[2,4,128,128]{3,2,1,0:T(8,128)(2,1)S(1)}, u32[]{:S(2)}, u32[]{:S(2)}) collective-permute-start(bf16[2,4,128,128]{3,2,1,0:T(8,128)(2,1)S(1)} %get-tuple-element.27), channel_id=1, source_target_pairs={{0,4},{4,0},{8,12},{12,8},{16,20},{20,16},{24,28},{28,24},{1,5},{5... | collective-permute-start | bytes 786440 | tf_op jit(solution)/shard_map/ppermute | solution.py:422
  49.4 7.2 %collective-permute-done.11 = bf16[2,4,128,128]{3,2,1,0:T(8,128)(2,1)S(1)} collective-permute-done((bf16[2,4,128,128]{3,2,1,0:T(8,128)(2,1)S(1)}, bf16[2,4,128,128]{3,2,1,0:T(8,128)(2,1)S(1)}, u32[]{:S(2)}, u32[]{:S(2)}) %collective-permute-start.11) | collective-permute-done | bytes 262176 | tf_op jit(solution)/shard_map/ppermute | solution.py:422
  56.6 3.1 %collective-permute-done.10 = bf16[2,4,128,128]{3,2,1,0:T(8,128)(2,1)S(1)} collective-permute-done((bf16[2,4,128,128]{3,2,1,0:T(8,128)(2,1)S(1)}, bf16[2,4,128,128]{3,2,1,0:T(8,128)(2,1)S(1)}, u32[]{:S(2)}, u32[]{:S(2)}) %collective-permute-start.10) | collective-permute-done | bytes 262176 | tf_op jit(solution)/shard_map/ppermute | solution.py:422
  59.9 2.5 %collective-permute-start.12 = (bf16[4,128,128]{2,1,0:T(8,128)(2,1)S(1)}, bf16[4,128,128]{2,1,0:T(8,128)(2,1)S(1)}, u32[]{:S(2)}, u32[]{:S(2)}) collective-permute-start(bf16[4,128,128]{2,1,0:T(8,128)(2,1)S(1)} %get-tuple-element.24), channel_id=1, source_target_pairs={{0,24},{4,28},{8,16},{12,20},{16,8},{20,12},{24,0},{28,4},{1,25},{... | collective-permute-start | bytes 393224 | tf_op jit(solution)/shard_map/ppermute | solution.py:428
  62.4 1.9 %collective-permute-start.14 = (bf16[4,128,128]{2,1,0:T(8,128)(2,1)S(1)}, bf16[4,128,128]{2,1,0:T(8,128)(2,1)S(1)}, u32[]{:S(2)}, u32[]{:S(2)}) collective-permute-start(bf16[4,128,128]{2,1,0:T(8,128)(2,1)S(1)} %get-tuple-element.26), channel_id=1, source_target_pairs={{0,8},{4,12},{8,0},{12,4},{16,24},{20,28},{24,16},{28,20},{1,9},{5... | collective-permute-start | bytes 393224 | tf_op jit(solution)/shard_map/ppermute | solution.py:428
  64.3 3.4 %collective-permute-done.12 = bf16[4,128,128]{2,1,0:T(8,128)(2,1)S(1)} collective-permute-done((bf16[4,128,128]{2,1,0:T(8,128)(2,1)S(1)}, bf16[4,128,128]{2,1,0:T(8,128)(2,1)S(1)}, u32[]{:S(2)}, u32[]{:S(2)}) %collective-permute-start.12) | collective-permute-done | bytes 131104 | tf_op jit(solution)/shard_map/ppermute | solution.py:428
  67.7 4.0 %collective-permute-done.13 = bf16[4,128,128]{2,1,0:T(8,128)(2,1)S(1)} collective-permute-done((bf16[4,128,128]{2,1,0:T(8,128)(2,1)S(1)}, bf16[4,128,128]{2,1,0:T(8,128)(2,1)S(1)}, u32[]{:S(2)}, u32[]{:S(2)}) %collective-permute-start.13) | collective-permute-done | bytes 131104 | tf_op jit(solution)/shard_map/ppermute | solution.py:428
  73.1 1.2 %collective-permute-start.15 = (bf16[128,128]{1,0:T(8,128)(2,1)S(1)}, bf16[128,128]{1,0:T(8,128)(2,1)S(1)}, u32[]{:S(2)}, u32[]{:S(2)}) collective-permute-start(bf16[128,128]{1,0:T(8,128)(2,1)S(1)} %get-tuple-element.31), channel_id=1, source_target_pairs={{0,1},{1,0},{2,3},{3,2},{4,5},{5,4},{6,7},{7,6},{8,9},{9,8},{10,11... | collective-permute-start | bytes 98312 | tf_op jit(solution)/shard_map/ppermute | solution.py:433
  74.3 1.5 %collective-permute-done.17.refs_3_ = bf16[128,128]{1,0:T(8,128)(2,1)S(1)} collective-permute-done((bf16[128,128]{1,0:T(8,128)(2,1)S(1)}, bf16[128,128]{1,0:T(8,128)(2,1)S(1)}, u32[]{:S(2)}, u32[]{:S(2)}) %collective-permute-start.17) | collective-permute-done | bytes 32800 | tf_op jit(solution)/shard_map/ppermute | solution.py:433
  77.1 1.5 %shard_map.95 = (bf16[64,512]{1,0:T(8,128)(2,1)}, bf16[64,512]{1,0:T(8,128)(2,1)}) custom-call(bf16[128,128]{1,0:T(8,128)(2,1)} %get-tuple-element.32.refs_0_, bf16[128,128]{1,0:T(8,128)(2,1)} %copy-done.6, bf16[128,128]{1,0:T(8,128)(2,1)} %copy-done.5, bf16[128,128]{1,0:T(8,128)(2,1)} %copy-done.4), custom_call_target="tpu_custom_call" | custom-call | tf_op jit(solution)/shard_map/pallas_call | solution.py:436
  (34 shorter events, 7.1 us)
Async XLA Ops:
  2.2 3.1 %collective-permute-start = (bf16[128,128]{1,0:T(8,128)(2,1)}, bf16[128,128]{1,0:T(8,128)(2,1)S(1)}, u32[]{:S(2)}, u32[]{:S(2)}) collective-permute-start(bf16[128,128]{1,0:T(8,128)(2,1)} %get-tuple-element.15), channel_id=1, source_target_pairs={{0,1},{1,0},{2,3},{3,2},{4,5},{5,4},{6,7},{7,6},{8,9},{9,8},{10,11... | collective-permute-start | bytes 98312 | tf_op jit(solution)/shard_map/ppermute | solution.py:407
  2.6 4.8 %collective-permute-start.1 = (bf16[128,128]{1,0:T(8,128)(2,1)}, bf16[128,128]{1,0:T(8,128)(2,1)S(1)}, u32[]{:S(2)}, u32[]{:S(2)}) collective-permute-start(bf16[128,128]{1,0:T(8,128)(2,1)} %get-tuple-element.16), channel_id=1, source_target_pairs={{0,2},{1,3},{2,0},{3,1},{4,6},{5,7},{6,4},{7,5},{8,10},{9,11},{10,... | collective-permute-start | bytes 98312 | tf_op jit(solution)/shard_map/ppermute | solution.py:407
  5.1 3.6 %collective-permute-start.2 = (bf16[128,128]{1,0:T(8,128)(2,1)}, bf16[128,128]{1,0:T(8,128)(2,1)S(1)}, u32[]{:S(2)}, u32[]{:S(2)}) collective-permute-start(bf16[128,128]{1,0:T(8,128)(2,1)} %get-tuple-element.17), channel_id=1, source_target_pairs={{0,3},{1,2},{2,1},{3,0},{4,7},{5,6},{6,5},{7,4},{8,11},{9,10},{10,... | collective-permute-start | bytes 98312 | tf_op jit(solution)/shard_map/ppermute | solution.py:407
  8.7 23.6 %copy-start.2 = (s32[4,8]{1,0:T(4,128)S(1)}, s32[4,8]{1,0:T(4,128)}, u32[]{:S(2)}) copy-start(s32[4,8]{1,0:T(4,128)} %refs_0_.1) | copy-start | bytes 388
  8.7 23.6 %copy-start.3 = (s32[2]{0:T(128)S(1)}, s32[2]{0:T(128)}, u32[]{:S(2)}) copy-start(s32[2]{0:T(128)} %refs_1_.1) | copy-start | bytes 28
  9.5 8.3 %collective-permute-start.8 = (bf16[4,128,128]{2,1,0:T(8,128)(2,1)S(1)}, bf16[4,128,128]{2,1,0:T(8,128)(2,1)S(1)}, u32[]{:S(2)}, u32[]{:S(2)}) collective-permute-start(bf16[4,128,128]{2,1,0:T(8,128)(2,1)S(1)} %pad_maximum_fusion.refs_4_), channel_id=1, source_target_pairs={{0,24},{4,28},{8,16},{12,20},{16,8},{20,12},{24,0},{28,4},{1,25},{... | collective-permute-start | bytes 393224 | tf_op jit(solution)/shard_map/ppermute | solution.py:412
  13.1 11.5 %collective-permute-start.6 = (bf16[4,128,128]{2,1,0:T(8,128)(2,1)S(1)}, bf16[4,128,128]{2,1,0:T(8,128)(2,1)S(1)}, u32[]{:S(2)}, u32[]{:S(2)}) collective-permute-start(bf16[4,128,128]{2,1,0:T(8,128)(2,1)S(1)} %pad_maximum_fusion.refs_4_), channel_id=1, source_target_pairs={{0,16},{4,20},{8,24},{12,28},{16,0},{20,4},{24,8},{28,12},{1,17},{... | collective-permute-start | bytes 393224 | tf_op jit(solution)/shard_map/ppermute | solution.py:412
  13.1 13.0 %collective-permute-start.4 = (bf16[4,128,128]{2,1,0:T(8,128)(2,1)S(1)}, bf16[4,128,128]{2,1,0:T(8,128)(2,1)S(1)}, u32[]{:S(2)}, u32[]{:S(2)}) collective-permute-start(bf16[4,128,128]{2,1,0:T(8,128)(2,1)S(1)} %pad_maximum_fusion.refs_4_), channel_id=1, source_target_pairs={{0,8},{4,12},{8,0},{12,4},{16,24},{20,28},{24,16},{28,20},{1,9},{5... | collective-permute-start | bytes 393224 | tf_op jit(solution)/shard_map/ppermute | solution.py:412
  13.9 12.7 %collective-permute-start.3 = (bf16[4,128,128]{2,1,0:T(8,128)(2,1)S(1)}, bf16[4,128,128]{2,1,0:T(8,128)(2,1)S(1)}, u32[]{:S(2)}, u32[]{:S(2)}) collective-permute-start(bf16[4,128,128]{2,1,0:T(8,128)(2,1)S(1)} %pad_maximum_fusion.refs_4_), channel_id=1, source_target_pairs={{0,4},{4,0},{8,12},{12,8},{16,20},{20,16},{24,28},{28,24},{1,5},{5... | collective-permute-start | bytes 393224 | tf_op jit(solution)/shard_map/ppermute | solution.py:414
  17.8 8.9 %collective-permute-start.9 = (bf16[4,128,128]{2,1,0:T(8,128)(2,1)S(1)}, bf16[4,128,128]{2,1,0:T(8,128)(2,1)S(1)}, u32[]{:S(2)}, u32[]{:S(2)}) collective-permute-start(bf16[4,128,128]{2,1,0:T(8,128)(2,1)S(1)} %collective-permute-done.8.refs_10_), channel_id=1, source_target_pairs={{0,4},{4,0},{8,12},{12,8},{16,20},{20,16},{24,28},{28,24},{1,5},{5... | collective-permute-start | bytes 393224 | tf_op jit(solution)/shard_map/ppermute | solution.py:414
  24.6 6.2 %collective-permute-start.7 = (bf16[4,128,128]{2,1,0:T(8,128)(2,1)S(1)}, bf16[4,128,128]{2,1,0:T(8,128)(2,1)S(1)}, u32[]{:S(2)}, u32[]{:S(2)}) collective-permute-start(bf16[4,128,128]{2,1,0:T(8,128)(2,1)S(1)} %collective-permute-done.6.refs_8_), channel_id=1, source_target_pairs={{0,4},{4,0},{8,12},{12,8},{16,20},{20,16},{24,28},{28,24},{1,5},{5... | collective-permute-start | bytes 393224 | tf_op jit(solution)/shard_map/ppermute | solution.py:414
  26.1 6.1 %collective-permute-start.5 = (bf16[4,128,128]{2,1,0:T(8,128)(2,1)S(1)}, bf16[4,128,128]{2,1,0:T(8,128)(2,1)S(1)}, u32[]{:S(2)}, u32[]{:S(2)}) collective-permute-start(bf16[4,128,128]{2,1,0:T(8,128)(2,1)S(1)} %collective-permute-done.4.refs_6_), channel_id=1, source_target_pairs={{0,4},{4,0},{8,12},{12,8},{16,20},{20,16},{24,28},{28,24},{1,5},{5... | collective-permute-start | bytes 393224 | tf_op jit(solution)/shard_map/ppermute | solution.py:414
  32.2 1.0 %copy-start = (bf16[256,1024]{1,0:T(8,128)(2,1)S(1)}, bf16[256,1024]{1,0:T(8,128)(2,1)}, u32[]{:S(2)}) copy-start(bf16[256,1024]{1,0:T(8,128)(2,1)} %refs_2_.1) | copy-start | bytes 1572868
  33.3 1.0 %copy-start.1 = (bf16[256,1024]{1,0:T(8,128)(2,1)S(1)}, bf16[256,1024]{1,0:T(8,128)(2,1)}, u32[]{:S(2)}) copy-start(bf16[256,1024]{1,0:T(8,128)(2,1)} %refs_3_.1) | copy-start | bytes 1572868
  47.3 9.3 %collective-permute-start.11 = (bf16[2,4,128,128]{3,2,1,0:T(8,128)(2,1)S(1)}, bf16[2,4,128,128]{3,2,1,0:T(8,128)(2,1)S(1)}, u32[]{:S(2)}, u32[]{:S(2)}) collective-permute-start(bf16[2,4,128,128]{3,2,1,0:T(8,128)(2,1)S(1)} %get-tuple-element.27), channel_id=1, source_target_pairs={{0,4},{4,0},{8,12},{12,8},{16,20},{20,16},{24,28},{28,24},{1,5},{5... | collective-permute-start | bytes 786440 | tf_op jit(solution)/shard_map/ppermute | solution.py:422
  48.9 10.8 %collective-permute-start.10 = (bf16[2,4,128,128]{3,2,1,0:T(8,128)(2,1)S(1)}, bf16[2,4,128,128]{3,2,1,0:T(8,128)(2,1)S(1)}, u32[]{:S(2)}, u32[]{:S(2)}) collective-permute-start(bf16[2,4,128,128]{3,2,1,0:T(8,128)(2,1)S(1)} %get-tuple-element.28), channel_id=1, source_target_pairs={{0,4},{4,0},{8,12},{12,8},{16,20},{20,16},{24,28},{28,24},{1,5},{5... | collective-permute-start | bytes 786440 | tf_op jit(solution)/shard_map/ppermute | solution.py:422
  59.9 7.8 %collective-permute-start.12 = (bf16[4,128,128]{2,1,0:T(8,128)(2,1)S(1)}, bf16[4,128,128]{2,1,0:T(8,128)(2,1)S(1)}, u32[]{:S(2)}, u32[]{:S(2)}) collective-permute-start(bf16[4,128,128]{2,1,0:T(8,128)(2,1)S(1)} %get-tuple-element.24), channel_id=1, source_target_pairs={{0,24},{4,28},{8,16},{12,20},{16,8},{20,12},{24,0},{28,4},{1,25},{... | collective-permute-start | bytes 393224 | tf_op jit(solution)/shard_map/ppermute | solution.py:428
  62.4 9.3 %collective-permute-start.13 = (bf16[4,128,128]{2,1,0:T(8,128)(2,1)S(1)}, bf16[4,128,128]{2,1,0:T(8,128)(2,1)S(1)}, u32[]{:S(2)}, u32[]{:S(2)}) collective-permute-start(bf16[4,128,128]{2,1,0:T(8,128)(2,1)S(1)} %get-tuple-element.25), channel_id=1, source_target_pairs={{0,16},{4,20},{8,24},{12,28},{16,0},{20,4},{24,8},{28,12},{1,17},{... | collective-permute-start | bytes 393224 | tf_op jit(solution)/shard_map/ppermute | solution.py:428
  62.4 9.3 %collective-permute-start.14 = (bf16[4,128,128]{2,1,0:T(8,128)(2,1)S(1)}, bf16[4,128,128]{2,1,0:T(8,128)(2,1)S(1)}, u32[]{:S(2)}, u32[]{:S(2)}) collective-permute-start(bf16[4,128,128]{2,1,0:T(8,128)(2,1)S(1)} %get-tuple-element.26), channel_id=1, source_target_pairs={{0,8},{4,12},{8,0},{12,4},{16,24},{20,28},{24,16},{28,20},{1,9},{5... | collective-permute-start | bytes 393224 | tf_op jit(solution)/shard_map/ppermute | solution.py:428
  72.4 3.3 %collective-permute-start.17 = (bf16[128,128]{1,0:T(8,128)(2,1)S(1)}, bf16[128,128]{1,0:T(8,128)(2,1)S(1)}, u32[]{:S(2)}, u32[]{:S(2)}) collective-permute-start(bf16[128,128]{1,0:T(8,128)(2,1)S(1)} %get-tuple-element.29), channel_id=1, source_target_pairs={{0,3},{1,2},{2,1},{3,0},{4,7},{5,6},{6,5},{7,4},{8,11},{9,10},{10,... | collective-permute-start | bytes 98312 | tf_op jit(solution)/shard_map/ppermute | solution.py:433
  72.4 4.0 %collective-permute-start.16 = (bf16[128,128]{1,0:T(8,128)(2,1)S(1)}, bf16[128,128]{1,0:T(8,128)(2,1)S(1)}, u32[]{:S(2)}, u32[]{:S(2)}) collective-permute-start(bf16[128,128]{1,0:T(8,128)(2,1)S(1)} %get-tuple-element.30), channel_id=1, source_target_pairs={{0,2},{1,3},{2,0},{3,1},{4,6},{5,7},{6,4},{7,5},{8,10},{9,11},{10,... | collective-permute-start | bytes 98312 | tf_op jit(solution)/shard_map/ppermute | solution.py:433
  73.1 3.4 %collective-permute-start.15 = (bf16[128,128]{1,0:T(8,128)(2,1)S(1)}, bf16[128,128]{1,0:T(8,128)(2,1)S(1)}, u32[]{:S(2)}, u32[]{:S(2)}) collective-permute-start(bf16[128,128]{1,0:T(8,128)(2,1)S(1)} %get-tuple-element.31), channel_id=1, source_target_pairs={{0,1},{1,0},{2,3},{3,2},{4,5},{5,4},{6,7},{7,6},{8,9},{9,8},{10,11... | collective-permute-start | bytes 98312 | tf_op jit(solution)/shard_map/ppermute | solution.py:433
  75.8 0.7 copy-start.4
  76.5 0.6 copy-start.6
  (1 other events, 0.6 us)

commit v2 on v0

--- a/solution.py
+++ b/solution.py
@@ -1,6 +1,10 @@
+import math
+
 import jax
 import jax.numpy as jnp
 from jax import lax
+from jax.experimental import pallas as pl
+from jax.experimental.pallas import tpu as pltpu
 from jax.sharding import PartitionSpec as P
 
 DH = 128
@@ -36,7 +40,12 @@
 
 
 def key_rows(library, spots):
-    chosen = library[spots]
+    chosen = jnp.stack(
+        [
+            lax.dynamic_index_in_dim(library, spots[i], 0, keepdims=False)
+            for i in range(spots.shape[0])
+        ]
+    )
     flat = chosen.reshape(chosen.shape[0] * chosen.shape[1], chosen.shape[2])
     return (flat[:, :DH], flat[:, DH:])
 
@@ -51,7 +60,7 @@
     return jnp.where(widened[None, None, :], scores, NEG_FILL)
 
 
-def body(queries, keys, values, d_out, rand_blocks, glob_blocks):
+def request_body(queries, keys, values, d_out, rand_blocks, glob_blocks):
     seq_count = lax.axis_size("seq")
     here = lax.axis_index("seq")
     short = keys.shape[0]
@@ -88,11 +97,20 @@
     incoming = lax.all_to_all(wanted, "seq", split_axis=0, concat_axis=0, tiled=True).reshape(
         position_count
     )
-    served = own_blocks[incoming].reshape(seq_count, capacity, BLOCK, 2 * DH)
+    block_ids = jnp.arange(blocks_here, dtype=jnp.int32)
+    picking = (incoming[:, None] == block_ids[None, :]).astype(jnp.bfloat16)
+    served = (
+        jnp.dot(
+            picking,
+            own_blocks.reshape(blocks_here, BLOCK * 2 * DH),
+            preferred_element_type=jnp.float32,
+        )
+        .astype(jnp.bfloat16)
+        .reshape(seq_count, capacity, BLOCK, 2 * DH)
+    )
     fetched = lax.all_to_all(served, "seq", split_axis=0, concat_axis=0, tiled=True).reshape(
         position_count, BLOCK, 2 * DH
     )
-    block_ids = jnp.arange(blocks_here, dtype=jnp.int32)
     window_ids = jnp.stack([block_ids, block_ids + 1, block_ids + 2], axis=1)
     global_ids = jnp.broadcast_to(
         blocks_here + 2 + jnp.arange(GLOB, dtype=jnp.int32), (blocks_here, GLOB)
@@ -212,6 +230,337 @@
     return (attn_out, d_queries, d_keys, d_values)
 
 
+def flips(count, bits):
+    return [(i, i ^ bits) for i in range(count)]
+
+
+def head_columns(head, offset):
+    return pl.ds(pl.multiple_of((head ^ offset) * DH, DH), DH)
+
+
+def pack_kernel(seq_count, head_count, *refs):
+    rand_from, glob_from, keys_ref, values_ref, query_ref, grad_ref = refs[:6]
+    piece_refs = refs[6 : 6 + head_count]
+    spots_ref, query_out, grad_out, rand_ref, glob_ref, sems = refs[6 + head_count :]
+    here = lax.axis_index("seq")
+    head = lax.axis_index("head")
+    short = keys_ref.shape[0]
+    copies = [(rand_from, rand_ref), (glob_from, glob_ref)]
+    for offset, piece in enumerate(piece_refs):
+        columns = head_columns(head, offset)
+        copies.append((keys_ref.at[:, columns], piece.at[pl.ds(0, short)]))
+        copies.append((values_ref.at[:, columns], piece.at[pl.ds(short, short)]))
+    copies += [(query_ref, query_out), (grad_ref, grad_out)]
+    copies = [pltpu.make_async_copy(a, b, sems.at[n]) for n, (a, b) in enumerate(copies)]
+    for copy in copies:
+        copy.start()
+    copies[0].wait()
+    copies[1].wait()
+    blocks_here = rand_ref.shape[0]
+    last = seq_count * blocks_here - 1
+    for step in range(blocks_here):
+        block = here * blocks_here + step
+        names = [jnp.maximum(block - 1, 0), block, jnp.minimum(block + 1, last)]
+        names += [glob_ref[i] for i in range(GLOB)]
+        names += [rand_ref[step, i] for i in range(RAND)]
+        for number, name in enumerate(names):
+            owner = lax.div(name, blocks_here) ^ here
+            slot = lax.rem(owner, 2) * (seq_count // 2) + lax.div(owner, 2)
+            spots_ref[step, number] = slot * blocks_here + (lax.rem(name, blocks_here) ^ head)
+    for copy in copies[2:]:
+        copy.wait()
+
+
+def unpack_kernel(*refs):
+    piece_refs, (keys_ref, values_ref) = refs[:-2], refs[-2:]
+    head = lax.axis_index("head")
+    short = keys_ref.shape[0]
+    for offset, piece in enumerate(piece_refs):
+        columns = head_columns(head, offset)
+        keys_ref[:, columns] = piece[:short, :]
+        values_ref[:, columns] = piece[short:, :]
+
+
+def dot(left, right, left_dim, right_dim):
+    return lax.dot_general(
+        left,
+        right,
+        (((left_dim,), (right_dim,)), ((), ())),
+        preferred_element_type=jnp.float32,
+    )
+
+
+def load_parts(part_refs, library, sems):
+    copies, at = [], 0
+    for part in part_refs:
+        size = part.shape[0]
+        copies.append(
+            pltpu.make_async_copy(part, library.at[pl.ds(at, size)], sems.at[len(copies)])
+        )
+        at += size
+    return copies
+
+
+def listed_spots(spots_ref, step):
+    return [spots_ref[step, number] for number in range(spots_ref.shape[1])]
+
+
+def begin(step, part_refs, library, total, sems):
+    @pl.when(step == 0)
+    def _():
+        copies = load_parts(part_refs, library, sems)
+        for copy in copies:
+            copy.start()
+        total[...] = jnp.zeros_like(total)
+        for copy in copies:
+            copy.wait()
+
+
+def add_terms(total, spots, terms):
+    for number, spot in enumerate(spots):
+        total[spot] += terms[number * BLOCK : (number + 1) * BLOCK]
+
+
+def finish(step, total, keep_ref, ship_ref):
+    pairs, size = keep_ref.shape[:2]
+
+    @pl.when(step == pl.num_programs(0) - 1)
+    def _():
+        for pair in range(pairs):
+            keep_ref[pair] = total[pl.ds(pair * size, size)]
+            ship_ref[pair] = total[pl.ds((pairs + pair) * size, size)].astype(jnp.bfloat16)
+
+
+def stacked_heads(ref, chunk):
+    return jnp.concatenate([ref[:, h * DH : (h + 1) * DH] for h in chunk], axis=0)
+
+
+def chunks_of(heads, size):
+    return [range(start, start + size) for start in range(0, heads, size)]
+
+
+def probs_kernel(seq_count, size, *refs):
+    spots_ref, query_ref, grad_ref = refs[:3]
+    part_refs = refs[3 : 3 + seq_count]
+    probs_ref, rows_ref, keep_ref, ship_ref, library, total, sems = refs[3 + seq_count :]
+    blocks_here = part_refs[0].shape[0]
+    all_blocks = seq_count * blocks_here
+    step = pl.program_id(0)
+    begin(step, part_refs, library, total, sems)
+    block = lax.axis_index("seq") * blocks_here + step
+    spots = listed_spots(spots_ref, step)
+    for number, spot in enumerate(spots):
+        rows_ref[0, pl.ds(number * BLOCK, BLOCK), :] = library[spot]
+    first_bias = jnp.where(block == 0, NEG_FILL, 0.0)
+    last_bias = jnp.where(block == all_blocks - 1, NEG_FILL, 0.0)
+    scale = DH ** (-0.5) * math.log2(math.e)
+    terms = 0.0
+    for chunk in chunks_of(query_ref.shape[1] // DH, size):
+        query = stacked_heads(query_ref, chunk)
+        grad = stacked_heads(grad_ref, chunk)
+        scores = dot(rows_ref[0], query, 1, 1)
+        scores = jnp.concatenate(
+            [
+                scores[:BLOCK] + first_bias,
+                scores[BLOCK : 2 * BLOCK],
+                scores[2 * BLOCK : 3 * BLOCK] + last_bias,
+                scores[3 * BLOCK :],
+            ],
+            axis=0,
+        )
+        peak = jnp.max(scores, axis=0, keepdims=True)
+        weights = jnp.exp2((scores - peak) * scale)
+        probs = weights * (1.0 / jnp.sum(weights, axis=0, keepdims=True))
+        probs16 = probs.astype(jnp.bfloat16)
+        probs_ref[0, :, chunk[0] * BLOCK : (chunk[-1] + 1) * BLOCK] = probs16
+        terms = terms + dot(probs16, grad, 1, 0)
+    add_terms(total, spots, terms)
+    finish(step, total, keep_ref, ship_ref)
+
+
+def dscores_kernel(size, *refs):
+    spots_ref, query_ref, grad_ref, probs_ref = refs[:4]
+    part_refs, refs = refs[4:-8], refs[-8:]
+    out_ref, dscores_ref, keep_ref, ship_ref, library, total, rows_ref, sems = refs
+    step = pl.program_id(0)
+    begin(step, part_refs, library, total, sems)
+    spots = listed_spots(spots_ref, step)
+    for number, spot in enumerate(spots):
+        rows_ref[pl.ds(number * BLOCK, BLOCK), :] = library[spot]
+    terms = 0.0
+    for chunk in chunks_of(query_ref.shape[1] // DH, size):
+        columns = slice(chunk[0] * BLOCK, (chunk[-1] + 1) * BLOCK)
+        query = stacked_heads(query_ref, chunk)
+        grad = stacked_heads(grad_ref, chunk)
+        probs16 = probs_ref[0, :, columns]
+        result = dot(rows_ref[...], probs16, 0, 0).astype(jnp.bfloat16).astype(jnp.float32)
+        grad_across = jnp.transpose(grad.astype(jnp.float32))
+        delta = jnp.sum(grad_across * result, axis=0, keepdims=True)
+        dprobs = dot(rows_ref[...], grad, 1, 1)
+        dscores = (probs16.astype(jnp.float32) * (dprobs - delta)).astype(jnp.bfloat16)
+        dscores_ref[0, :, columns] = dscores
+        terms = terms + dot(dscores, query, 1, 0)
+        down = jnp.transpose(result).astype(jnp.bfloat16)
+        for number, h in enumerate(chunk):
+            out_ref[:, h * DH : (h + 1) * DH] = down[number * BLOCK : (number + 1) * BLOCK]
+    add_terms(total, spots, terms * DH ** (-0.5))
+    finish(step, total, keep_ref, ship_ref)
+
+
+def dquery_kernel(size, dscores_ref, rows_ref, dquery_ref):
+    for chunk in chunks_of(dquery_ref.shape[1] // DH, size):
+        columns = slice(chunk[0] * BLOCK, (chunk[-1] + 1) * BLOCK)
+        across = dot(rows_ref[0], dscores_ref[0, :, columns], 0, 0) * DH ** (-0.5)
+        down = jnp.transpose(across).astype(jnp.bfloat16)
+        for number, h in enumerate(chunk):
+            dquery_ref[:, h * DH : (h + 1) * DH] = down[number * BLOCK : (number + 1) * BLOCK]
+
+
+def small_grant():
+    return pltpu.CompilerParams(vmem_limit_bytes=8 * 1024 * 1024)
+
+
+def kernel_options(products, pairs):
+    return {
+        "compiler_params": pltpu.CompilerParams(vmem_limit_bytes=40 * 1024 * 1024),
+        "cost_estimate": pl.CostEstimate(
+            flops=4 * products * pairs * DH, bytes_accessed=4 * pairs, transcendentals=pairs
+        ),
+    }
+
+
+def whole_body(queries, keys, values, d_out, rand_blocks, glob_blocks):
+    seq_count = lax.axis_size("seq")
+    head_count = lax.axis_size("head")
+    short = keys.shape[0]
+    tok_count, width = queries.shape
+    heads_here = width // DH
+    blocks_here = tok_count // BLOCK
+    pair_count = seq_count // 2
+    listed = (3 + GLOB + RAND) * BLOCK
+    columns = heads_here * BLOCK
+    pairs = blocks_here * listed * columns
+    size = math.gcd(heads_here, 4)
+
+    smem = pl.BlockSpec(memory_space=pltpu.SMEM)
+    anywhere = pl.BlockSpec(memory_space=pl.ANY)
+    tile_shape = jax.ShapeDtypeStruct(queries.shape, jnp.bfloat16)
+    piece = jax.ShapeDtypeStruct((2 * short, DH), jnp.bfloat16)
+    spots_shape = jax.ShapeDtypeStruct((blocks_here, 3 + GLOB + RAND), jnp.int32)
+    *pieces, spots, query_here, grad_here = pl.pallas_call(
+        lambda *refs: pack_kernel(seq_count, head_count, *refs),
+        in_specs=[anywhere] * 6,
+        out_specs=[anywhere] * head_count + [smem] + [anywhere] * 2,
+        out_shape=[piece] * head_count + [spots_shape, tile_shape, tile_shape],
+        scratch_shapes=[
+            pltpu.SMEM(rand_blocks.shape, jnp.int32),
+            pltpu.SMEM(glob_blocks.shape, jnp.int32),
+            pltpu.SemaphoreType.DMA((2 * head_count + 4,)),
+        ],
+        compiler_params=small_grant(),
+    )(
+        *[
+            pltpu.with_memory_space_constraint(x, pltpu.HBM)
+            for x in (rand_blocks, glob_blocks, keys, values, queries, d_out)
+        ]
+    )
+    pieces = [pieces[0]] + [
+        lax.ppermute(pieces[k], "head", flips(head_count, k)) for k in range(1, head_count)
+    ]
+
+    def along_far(own):
+        parts = [own]
+        for k in range(2, seq_count, 2):
+            parts.append(lax.ppermute(own, "seq", flips(seq_count, k)))
+        return parts
+
+    def to_near(part):
+        return lax.ppermute(part, "seq", flips(seq_count, 1))
+
+    key_parts = along_far(jnp.stack([p[:short] for p in pieces]))
+    key_parts += [to_near(p) for p in key_parts]
+    value_parts = along_far(jnp.stack([p[short:] for p in pieces]))
+    key_parts, value_parts = lax.optimization_barrier((key_parts, value_parts))
+    value_parts.append(to_near(jnp.concatenate(value_parts)))
+
+    tile = pl.BlockSpec((BLOCK, width), lambda i: (i, 0))
+    square = pl.BlockSpec((1, listed, columns), lambda i: (i, 0, 0))
+    listing = pl.BlockSpec((1, listed, DH), lambda i: (i, 0, 0))
+    half = (pair_count, blocks_here, BLOCK, DH)
+    whole = pl.BlockSpec(half, lambda i: (0, 0, 0, 0))
+    square_shape = jax.ShapeDtypeStruct((blocks_here, listed, columns), jnp.bfloat16)
+    listing_shape = jax.ShapeDtypeStruct((blocks_here, listed, DH), jnp.bfloat16)
+    keep_shape = jax.ShapeDtypeStruct(half, jnp.float32)
+    ship_shape = jax.ShapeDtypeStruct(half, jnp.bfloat16)
+    library = pltpu.VMEM((seq_count * blocks_here, BLOCK, DH), jnp.bfloat16)
+    total = pltpu.VMEM((seq_count * blocks_here, BLOCK, DH), jnp.float32)
+    sems = pltpu.SemaphoreType.DMA((seq_count,))
+
+    probs, key_lists, value_keep, value_ship = pl.pallas_call(
+        lambda *refs: probs_kernel(seq_count, size, *refs),
+        grid=(blocks_here,),
+        in_specs=[smem, tile, tile] + [anywhere] * len(key_parts),
+        out_specs=[square, listing, whole, whole],
+        out_shape=[square_shape, listing_shape, keep_shape, ship_shape],
+        scratch_shapes=[library, total, sems],
+        **kernel_options(2, pairs),
+    )(spots, query_here, grad_here, *key_parts)
+    value_near = lax.ppermute(value_ship, "seq", flips(seq_count, 1))
+    attn_out, dscores, key_keep, key_ship = pl.pallas_call(
+        lambda *refs: dscores_kernel(size, *refs),
+        grid=(blocks_here,),
+        in_specs=[smem, tile, tile, square] + [anywhere] * len(value_parts),
+        out_specs=[tile, square, whole, whole],
+        out_shape=[tile_shape, square_shape, keep_shape, ship_shape],
+        scratch_shapes=[library, total, pltpu.VMEM((listed, DH), jnp.bfloat16), sems],
+        **kernel_options(3, pairs),
+    )(spots, query_here, grad_here, probs, *value_parts)
+    key_near = lax.ppermute(key_ship, "seq", flips(seq_count, 1))
+    d_queries = pl.pallas_call(
+        lambda *refs: dquery_kernel(size, *refs),
+        grid=(blocks_here,),
+        in_specs=[square, listing],
+        out_specs=tile,
+        out_shape=tile_shape,
+        **kernel_options(1, pairs),
+    )(dscores, key_lists)
+
+    key_near, d_queries = lax.optimization_barrier((key_near, d_queries))
+
+    def returned(keep, near):
+        sums = keep + near.astype(jnp.float32)
+        result = sums[0]
+        for pair in range(pair_count - 1, 0, -1):
+            result = result + lax.ppermute(
+                sums[pair].astype(jnp.bfloat16), "seq", flips(seq_count, 2 * pair)
+            ).astype(jnp.float32)
+        return result
+
+    packed = jnp.concatenate(
+        [returned(key_keep, key_near), returned(value_keep, value_near)], axis=1
+    ).astype(jnp.bfloat16)
+    back = [packed[0]] + [
+        lax.ppermute(packed[k], "head", flips(head_count, k)) for k in range(1, head_count)
+    ]
+    flat = jax.ShapeDtypeStruct(keys.shape, jnp.bfloat16)
+    d_keys, d_values = pl.pallas_call(
+        unpack_kernel, out_shape=[flat, flat], compiler_params=small_grant()
+    )(*back)
+    return (attn_out, d_queries, d_keys, d_values)
+
+
+def body(queries, keys, values, d_out, rand_blocks, glob_blocks):
+    seq_count = lax.axis_size("seq")
+    head_count = lax.axis_size("head")
+    blocks_here = rand_blocks.shape[0]
+    capacity = -(-rand_blocks.size // seq_count)
+    powers = all(n & (n - 1) == 0 for n in (seq_count, head_count))
+    fits = keys.shape[0] == BLOCK and blocks_here == head_count
+    if capacity >= blocks_here and seq_count > 1 and powers and fits:
+        return whole_body(queries, keys, values, d_out, rand_blocks, glob_blocks)
+    return request_body(queries, keys, values, d_out, rand_blocks, glob_blocks)
+
+
 def solution(mesh):
     in_specs = (
         P("seq", "head"),

time: 271 us -> 67.7 us (0.25)
  waiting for transfers between devices: 147 us -> 17.9 us
  local copies, waits for them, and re-layouts: 37.5 us -> 0.04 us
  between operations: 19.6 us -> 0.76 us
  matrix products: 18.3 us -> 0 us
  Pallas kernels: 0 us -> 17.7 us
  other arithmetic: 14.3 us -> 0.32 us
    psum x2 -> x0, waiting for transfers between devices: 129 us -> none  [the longest x1 66 us: broadcast(): return lax.psum(block, axis)]
    all_to_all x5 -> x0, starting transfers between devices: 22.2 us -> none  [the longest x1 7.28 us: body(): lax.all_to_all(wanted, 'seq', split_axis=0, concat_axis=0, tiled=True)]
    ppermute x4 -> x25, starting transfers between devices: 10.2 us -> 30.8 us  [the longest x6 10 us: returned(): lax.ppermute(sums[pair].astype(jnp.bfloat16), 'seq', flips(seq_count, 2 *...]
    dot_general x30 -> x0, matrix products: 18.3 us -> none  [the longest x4 4.71 us: forward_step(): jnp.einsum('htk,kd->thd', probs16, values_here, preferred_element_type=jn...]
    pallas_call x0 -> x5, Pallas kernels: none -> 17.7 us  [the longest x1 6.42 us: whole_body(): pl.pallas_call(lambda *refs: dscores_kernel(size, *refs), grid=(blocks_he...]
    all_to_all x5 -> x0, waiting for transfers between devices: 10.6 us -> none  [the longest x1 4.84 us: body(): lax.all_to_all(wanted, 'seq', split_axis=0, concat_axis=0, tiled=True)]
    ppermute x4 -> x25, waiting for transfers between devices: 7.46 us -> 17.9 us  [the longest x6 4.48 us: returned(): lax.ppermute(sums[pair].astype(jnp.bfloat16), 'seq', flips(seq_count, 2 *...]
    reduce_sum x12 -> x0, other arithmetic: 7.98 us -> none  [the longest x4 4.2 us: backward_step(): jnp.sum(gradient_tile.astype(jnp.float32) * out_block.astype(jnp.float32)...]
  transfers between devices with their start and end apart: 11 -> 25, of which waited for: 7 -> 12; matrix products, arithmetic and copies ran while one was open for 6% -> 0% of each run, Pallas kernels for 0% -> 22%
where the time goes in v2:
time: 67.7 us; the launch traced here: 67.5 us
  starting transfers between devices  30.8 us (45%)
  waiting for transfers between devices  17.9 us (26%)
  Pallas kernels  17.7 us (26%)
  between operations  0.76 us (1%)
    ppermute x6, starting transfers between devices, returned(): lax.ppermute(sums[pair].astype(jnp.bfloat16), 'seq', flips(seq_count, 2 *...  10 us
    ppermute x6, starting transfers between devices, along_far(): parts.append(lax.ppermute(own, 'seq', flips(seq_count, k)))  8.84 us
    pallas_call x1, Pallas kernels, whole_body(): pl.pallas_call(lambda *refs: dscores_kernel(size, *refs), grid=(blocks_he...  6.42 us
    pallas_call x1, Pallas kernels, whole_body(): pl.pallas_call(lambda *refs: probs_kernel(seq_count, size, *refs), grid=(...  5.92 us
    ppermute x6, waiting for transfers between devices, returned(): lax.ppermute(sums[pair].astype(jnp.bfloat16), 'seq', flips(seq_count, 2 *...  4.48 us
    ppermute x5, starting transfers between devices, to_near(): return lax.ppermute(part, 'seq', flips(seq_count, 1))  4.38 us
    ppermute x5, waiting for transfers between devices, to_near(): return lax.ppermute(part, 'seq', flips(seq_count, 1))  3.89 us
    ppermute x6, waiting for transfers between devices, along_far(): parts.append(lax.ppermute(own, 'seq', flips(seq_count, k)))  3.48 us
  transfers between devices with their start and end apart: 25, of which 12 were waited for; matrix products, arithmetic and copies ran while one was open for 0% of the time, Pallas kernels for 22%

profile of v2, /device:TPU:0, one launch (start us, length us, event | category | flops | bytes accessed | tf_op | source)
XLA Modules:
  0.0 67.5 jit_solution(1125711246554864756)
XLA Ops:
  0.6 2.1 %shard_map.93 = (bf16[128,128]{1,0:T(8,128)(2,1)S(1)}, bf16[128,128]{1,0:T(8,128)(2,1)S(1)}, bf16[128,128]{1,0:T(8,128)(2,1)S(1)}, bf16[128,128]{1,0:T(8,128)(2,...) custom-call(s32[4,8]{1,0:T(4,128)} %refs_0_.1, s32[2]{0:T(128)} %refs_1_.1, ...), custom_call_target="tpu_custom_call" | custom-call | tf_op jit(solution)/shard_map/pallas_call | solution.py:450
  3.2 2.6 %collective-permute-start.1 = (bf16[128,128]{1,0:T(8,128)(2,1)S(1)}, bf16[128,128]{1,0:T(8,128)(2,1)S(1)}, u32[]{:S(2)}, u32[]{:S(2)}) collective-permute-start(bf16[128,128]{1,0:T(8,128)(2,1)S(1)} %get-tuple-element.40), channel_id=1, source_target_pairs={{0,2},{1,3},{2,0},{3,1},{4,6},{5,7},{6,4},{7,5},{8,10},{9,11},{10,... | collective-permute-start | bytes 98312 | tf_op jit(solution)/shard_map/ppermute | solution.py:468
  5.9 1.9 %collective-permute-done.1 = bf16[128,128]{1,0:T(8,128)(2,1)S(1)} collective-permute-done((bf16[128,128]{1,0:T(8,128)(2,1)S(1)}, bf16[128,128]{1,0:T(8,128)(2,1)S(1)}, u32[]{:S(2)}, u32[]{:S(2)}) %collective-permute-start.1) | collective-permute-done | bytes 32800 | tf_op jit(solution)/shard_map/ppermute | solution.py:468
  7.8 1.4 %collective-permute-done.2 = bf16[128,128]{1,0:T(8,128)(2,1)S(1)} collective-permute-done((bf16[128,128]{1,0:T(8,128)(2,1)S(1)}, bf16[128,128]{1,0:T(8,128)(2,1)S(1)}, u32[]{:S(2)}, u32[]{:S(2)}) %collective-permute-start.2) | collective-permute-done | bytes 32800 | tf_op jit(solution)/shard_map/ppermute | solution.py:468
  9.2 1.6 %collective-permute-start.6 = (bf16[4,64,128]{2,1,0:T(8,128)(2,1)S(1)}, bf16[4,64,128]{2,1,0:T(8,128)(2,1)S(1)}, u32[]{:S(2)}, u32[]{:S(2)}) collective-permute-start(bf16[4,64,128]{2,1,0:T(8,128)(2,1)S(1)} %pad_maximum_fusion.1.refs_3_), channel_id=1, source_target_pairs={{0,4},{4,0},{8,12},{12,8},{16,20},{20,16},{24,28},{28,24},{1,5},{5... | collective-permute-start | bytes 196616 | tf_op jit(solution)/shard_map/ppermute | solution.py:478
  10.7 3.6 %collective-permute-start.5 = (bf16[4,64,128]{2,1,0:T(8,128)(2,1)S(1)}, bf16[4,64,128]{2,1,0:T(8,128)(2,1)S(1)}, u32[]{:S(2)}, u32[]{:S(2)}) collective-permute-start(bf16[4,64,128]{2,1,0:T(8,128)(2,1)S(1)} %pad_maximum_fusion.1.refs_3_), channel_id=1, source_target_pairs={{0,24},{4,28},{8,16},{12,20},{16,8},{20,12},{24,0},{28,4},{1,25},{... | collective-permute-start | bytes 196616 | tf_op jit(solution)/shard_map/ppermute | solution.py:474
  15.1 3.7 %collective-permute-start.12 = (bf16[4,64,128]{2,1,0:T(8,128)(2,1)S(1)}, bf16[4,64,128]{2,1,0:T(8,128)(2,1)S(1)}, u32[]{:S(2)}, u32[]{:S(2)}) collective-permute-start(bf16[4,64,128]{2,1,0:T(8,128)(2,1)S(1)} %pad_maximum_fusion.2.refs_4_), channel_id=1, source_target_pairs={{0,24},{4,28},{8,16},{12,20},{16,8},{20,12},{24,0},{28,4},{1,25},{... | collective-permute-start | bytes 196616 | tf_op jit(solution)/shard_map/ppermute | solution.py:474
  19.6 3.1 %collective-permute-done.4.refs_5_ = bf16[4,64,128]{2,1,0:T(8,128)(2,1)S(1)} collective-permute-done((bf16[4,64,128]{2,1,0:T(8,128)(2,1)S(1)}, bf16[4,64,128]{2,1,0:T(8,128)(2,1)S(1)}, u32[]{:S(2)}, u32[]{:S(2)}) %collective-permute-start.4) | collective-permute-done | bytes 65568 | tf_op jit(solution)/shard_map/ppermute | solution.py:474
  23.2 1.5 %collective-permute-start.8 = (bf16[4,64,128]{2,1,0:T(8,128)(2,1)S(1)}, bf16[4,64,128]{2,1,0:T(8,128)(2,1)S(1)}, u32[]{:S(2)}, u32[]{:S(2)}) collective-permute-start(bf16[4,64,128]{2,1,0:T(8,128)(2,1)S(1)} %collective-permute-done.4.refs_5_), channel_id=1, source_target_pairs={{0,4},{4,0},{8,12},{12,8},{16,20},{20,16},{24,28},{28,24},{1,5},{5... | collective-permute-start | bytes 196616 | tf_op jit(solution)/shard_map/ppermute | solution.py:478
  25.6 1.3 %collective-permute-done.9.refs_10_ = bf16[4,64,128]{2,1,0:T(8,128)(2,1)S(1)} collective-permute-done((bf16[4,64,128]{2,1,0:T(8,128)(2,1)S(1)}, bf16[4,64,128]{2,1,0:T(8,128)(2,1)S(1)}, u32[]{:S(2)}, u32[]{:S(2)}) %collective-permute-start.9) | collective-permute-done | bytes 65568 | tf_op jit(solution)/shard_map/ppermute | solution.py:478
  27.7 1.8 %collective-permute-done.7.refs_8_ = bf16[4,64,128]{2,1,0:T(8,128)(2,1)S(1)} collective-permute-done((bf16[4,64,128]{2,1,0:T(8,128)(2,1)S(1)}, bf16[4,64,128]{2,1,0:T(8,128)(2,1)S(1)}, u32[]{:S(2)}, u32[]{:S(2)}) %collective-permute-start.7) | collective-permute-done | bytes 65568 | tf_op jit(solution)/shard_map/ppermute | solution.py:478
  29.8 5.9 %shard_map.94 = (bf16[4,832,512]{2,1,0:T(8,128)(2,1)S(1)}, bf16[4,832,128]{2,1,0:T(8,128)(2,1)S(1)}, f32[4,4,64,128]{3,2,1,0:T(8,128)S(1)}, bf16[4,4,64,128]{3,2,1,0:T(8,128)(2,1)S(1)}) custom-call(s32[4,13]{1,0:T(4,128)S(1)} %get-tuple-element.35.refs_0_, bf16[256,1024]{1,0:T(8,128)(2,1)S(1)} %get-tuple-element.36.refs_1_, ...), custom_call_target="tpu_custom_call" | custom-call | flops 1744830464 | bytes 6815744 | tf_op jit(solution)/shard_map/pallas_call | solution.py:499
  35.7 1.9 %collective-permute-start.18 = (bf16[4,4,64,128]{3,2,1,0:T(8,128)(2,1)S(1)}, bf16[4,4,64,128]{3,2,1,0:T(8,128)(2,1)S(1)}, u32[]{:S(2)}, u32[]{:S(2)}) collective-permute-start(bf16[4,4,64,128]{3,2,1,0:T(8,128)(2,1)S(1)} %get-tuple-element.63), channel_id=1, source_target_pairs={{0,4},{4,0},{8,12},{12,8},{16,20},{20,16},{24,28},{28,24},{1,5},{5... | collective-permute-start | bytes 786440 | tf_op jit(solution)/shard_map/ppermute | solution.py:508
  37.6 6.4 %shard_map.95 = (bf16[256,1024]{1,0:T(8,128)(2,1)}, bf16[4,832,512]{2,1,0:T(8,128)(2,1)S(1)}, f32[4,4,64,128]{3,2,1,0:T(8,128)S(1)}, bf16[4,4,64,128]{3,2,1,0:T(8,128)(2,1)S(1)}) custom-call(s32[4,13]{1,0:T(4,128)S(1)} %get-tuple-element.35.refs_0_, bf16[256,1024]{1,0:T(8,128)(2,1)S(1)} %get-tuple-element.36.refs_1_, ...), custom_call_target="tpu_custom_call" | custom-call | flops 2617245696 | bytes 6815744 | tf_op jit(solution)/shard_map/pallas_call | solution.py:509
  44.5 4.9 %collective-permute-start.19 = (bf16[4,64,128]{2,1,0:T(8,128)(2,1)S(1)}, bf16[4,64,128]{2,1,0:T(8,128)(2,1)S(1)}, u32[]{:S(2)}, u32[]{:S(2)}) collective-permute-start(bf16[4,64,128]{2,1,0:T(8,128)(2,1)S(1)} %get-tuple-element.70), channel_id=1, source_target_pairs={{0,24},{4,28},{8,16},{12,20},{16,8},{20,12},{24,0},{28,4},{1,25},{... | collective-permute-start | bytes 196616 | tf_op jit(solution)/shard_map/ppermute | solution.py:534
  50.0 2.6 %shard_map.96 = bf16[256,1024]{1,0:T(8,128)(2,1)} custom-call(bf16[4,832,512]{2,1,0:T(8,128)(2,1)S(1)} %get-tuple-element.57.refs_0_, bf16[4,832,128]{2,1,0:T(8,128)(2,1)S(1)} %get-tuple-element.58.refs_1_), custom_call_target="tpu_custom_call" | custom-call | flops 872415232 | bytes 6815744 | tf_op jit(solution)/shard_map/pallas_call | solution.py:519
  52.7 3.8 %collective-permute-start.15 = (bf16[4,64,128]{2,1,0:T(8,128)(2,1)S(1)}, bf16[4,64,128]{2,1,0:T(8,128)(2,1)S(1)}, u32[]{:S(2)}, u32[]{:S(2)}) collective-permute-start(bf16[4,64,128]{2,1,0:T(8,128)(2,1)S(1)} %get-tuple-element.73), channel_id=1, source_target_pairs={{0,24},{4,28},{8,16},{12,20},{16,8},{20,12},{24,0},{28,4},{1,25},{... | collective-permute-start | bytes 196616 | tf_op jit(solution)/shard_map/ppermute | solution.py:534
  57.3 1.6 %collective-permute-done.15 = bf16[4,64,128]{2,1,0:T(8,128)(2,1)S(1)} collective-permute-done((bf16[4,64,128]{2,1,0:T(8,128)(2,1)S(1)}, bf16[4,64,128]{2,1,0:T(8,128)(2,1)S(1)}, u32[]{:S(2)}, u32[]{:S(2)}) %collective-permute-start.15) | collective-permute-done | bytes 65568 | tf_op jit(solution)/shard_map/ppermute | solution.py:534
  58.9 1.9 %collective-permute-done.17 = bf16[4,64,128]{2,1,0:T(8,128)(2,1)S(1)} collective-permute-done((bf16[4,64,128]{2,1,0:T(8,128)(2,1)S(1)}, bf16[4,64,128]{2,1,0:T(8,128)(2,1)S(1)}, u32[]{:S(2)}, u32[]{:S(2)}) %collective-permute-start.17) | collective-permute-done | bytes 65568 | tf_op jit(solution)/shard_map/ppermute | solution.py:534
  60.8 0.9 %collective-permute-done.16 = bf16[4,64,128]{2,1,0:T(8,128)(2,1)S(1)} collective-permute-done((bf16[4,64,128]{2,1,0:T(8,128)(2,1)S(1)}, bf16[4,64,128]{2,1,0:T(8,128)(2,1)S(1)}, u32[]{:S(2)}, u32[]{:S(2)}) %collective-permute-start.16) | collective-permute-done | bytes 65568 | tf_op jit(solution)/shard_map/ppermute | solution.py:534
  61.9 1.0 %collective-permute-start.22 = (bf16[128,128]{1,0:T(8,128)(2,1)S(1)}, bf16[128,128]{1,0:T(8,128)(2,1)S(1)}, u32[]{:S(2)}, u32[]{:S(2)}) collective-permute-start(bf16[128,128]{1,0:T(8,128)(2,1)S(1)} %get-tuple-element.78), channel_id=1, source_target_pairs={{0,1},{1,0},{2,3},{3,2},{4,5},{5,4},{6,7},{7,6},{8,9},{9,8},{10,11... | collective-permute-start | bytes 98312 | tf_op jit(solution)/shard_map/ppermute | solution.py:543
  62.9 1.1 %collective-permute-start.23 = (bf16[128,128]{1,0:T(8,128)(2,1)S(1)}, bf16[128,128]{1,0:T(8,128)(2,1)S(1)}, u32[]{:S(2)}, u32[]{:S(2)}) collective-permute-start(bf16[128,128]{1,0:T(8,128)(2,1)S(1)} %get-tuple-element.79), channel_id=1, source_target_pairs={{0,2},{1,3},{2,0},{3,1},{4,6},{5,7},{6,4},{7,5},{8,10},{9,11},{10,... | collective-permute-start | bytes 98312 | tf_op jit(solution)/shard_map/ppermute | solution.py:543
  64.0 1.2 %collective-permute-done.24.refs_3_ = bf16[128,128]{1,0:T(8,128)(2,1)S(1)} collective-permute-done((bf16[128,128]{1,0:T(8,128)(2,1)S(1)}, bf16[128,128]{1,0:T(8,128)(2,1)S(1)}, u32[]{:S(2)}, u32[]{:S(2)}) %collective-permute-start.24) | collective-permute-done | bytes 32800 | tf_op jit(solution)/shard_map/ppermute | solution.py:543
  65.2 1.6 %collective-permute-done.23.refs_2_ = bf16[128,128]{1,0:T(8,128)(2,1)S(1)} collective-permute-done((bf16[128,128]{1,0:T(8,128)(2,1)S(1)}, bf16[128,128]{1,0:T(8,128)(2,1)S(1)}, u32[]{:S(2)}, u32[]{:S(2)}) %collective-permute-start.23) | collective-permute-done | bytes 32800 | tf_op jit(solution)/shard_map/ppermute | solution.py:543
  (45 shorter events, 7.2 us)
Async XLA Ops:
  3.2 4.5 %collective-permute-start.1 = (bf16[128,128]{1,0:T(8,128)(2,1)S(1)}, bf16[128,128]{1,0:T(8,128)(2,1)S(1)}, u32[]{:S(2)}, u32[]{:S(2)}) collective-permute-start(bf16[128,128]{1,0:T(8,128)(2,1)S(1)} %get-tuple-element.40), channel_id=1, source_target_pairs={{0,2},{1,3},{2,0},{3,1},{4,6},{5,7},{6,4},{7,5},{8,10},{9,11},{10,... | collective-permute-start | bytes 98312 | tf_op jit(solution)/shard_map/ppermute | solution.py:468
  5.8 3.3 %collective-permute-start.2 = (bf16[128,128]{1,0:T(8,128)(2,1)S(1)}, bf16[128,128]{1,0:T(8,128)(2,1)S(1)}, u32[]{:S(2)}, u32[]{:S(2)}) collective-permute-start(bf16[128,128]{1,0:T(8,128)(2,1)S(1)} %get-tuple-element.41), channel_id=1, source_target_pairs={{0,3},{1,2},{2,1},{3,0},{4,7},{5,6},{6,5},{7,4},{8,11},{9,10},{10,... | collective-permute-start | bytes 98312 | tf_op jit(solution)/shard_map/ppermute | solution.py:468
  9.2 9.7 %collective-permute-start.6 = (bf16[4,64,128]{2,1,0:T(8,128)(2,1)S(1)}, bf16[4,64,128]{2,1,0:T(8,128)(2,1)S(1)}, u32[]{:S(2)}, u32[]{:S(2)}) collective-permute-start(bf16[4,64,128]{2,1,0:T(8,128)(2,1)S(1)} %pad_maximum_fusion.1.refs_3_), channel_id=1, source_target_pairs={{0,4},{4,0},{8,12},{12,8},{16,20},{20,16},{24,28},{28,24},{1,5},{5... | collective-permute-start | bytes 196616 | tf_op jit(solution)/shard_map/ppermute | solution.py:478
  10.7 8.1 %collective-permute-start.5 = (bf16[4,64,128]{2,1,0:T(8,128)(2,1)S(1)}, bf16[4,64,128]{2,1,0:T(8,128)(2,1)S(1)}, u32[]{:S(2)}, u32[]{:S(2)}) collective-permute-start(bf16[4,64,128]{2,1,0:T(8,128)(2,1)S(1)} %pad_maximum_fusion.1.refs_3_), channel_id=1, source_target_pairs={{0,24},{4,28},{8,16},{12,20},{16,8},{20,12},{24,0},{28,4},{1,25},{... | collective-permute-start | bytes 196616 | tf_op jit(solution)/shard_map/ppermute | solution.py:474
  14.3 8.3 %collective-permute-start.4 = (bf16[4,64,128]{2,1,0:T(8,128)(2,1)S(1)}, bf16[4,64,128]{2,1,0:T(8,128)(2,1)S(1)}, u32[]{:S(2)}, u32[]{:S(2)}) collective-permute-start(bf16[4,64,128]{2,1,0:T(8,128)(2,1)S(1)} %pad_maximum_fusion.1.refs_3_), channel_id=1, source_target_pairs={{0,16},{4,20},{8,24},{12,28},{16,0},{20,4},{24,8},{28,12},{1,17},{... | collective-permute-start | bytes 196616 | tf_op jit(solution)/shard_map/ppermute | solution.py:474
  14.4 8.9 %collective-permute-start.3 = (bf16[4,64,128]{2,1,0:T(8,128)(2,1)S(1)}, bf16[4,64,128]{2,1,0:T(8,128)(2,1)S(1)}, u32[]{:S(2)}, u32[]{:S(2)}) collective-permute-start(bf16[4,64,128]{2,1,0:T(8,128)(2,1)S(1)} %pad_maximum_fusion.1.refs_3_), channel_id=1, source_target_pairs={{0,8},{4,12},{8,0},{12,4},{16,24},{20,28},{24,16},{28,20},{1,9},{5... | collective-permute-start | bytes 196616 | tf_op jit(solution)/shard_map/ppermute | solution.py:474
  15.1 9.6 %collective-permute-start.12 = (bf16[4,64,128]{2,1,0:T(8,128)(2,1)S(1)}, bf16[4,64,128]{2,1,0:T(8,128)(2,1)S(1)}, u32[]{:S(2)}, u32[]{:S(2)}) collective-permute-start(bf16[4,64,128]{2,1,0:T(8,128)(2,1)S(1)} %pad_maximum_fusion.2.refs_4_), channel_id=1, source_target_pairs={{0,24},{4,28},{8,16},{12,20},{16,8},{20,12},{24,0},{28,4},{1,25},{... | collective-permute-start | bytes 196616 | tf_op jit(solution)/shard_map/ppermute | solution.py:474
  18.8 6.8 %collective-permute-start.11 = (bf16[4,64,128]{2,1,0:T(8,128)(2,1)S(1)}, bf16[4,64,128]{2,1,0:T(8,128)(2,1)S(1)}, u32[]{:S(2)}, u32[]{:S(2)}) collective-permute-start(bf16[4,64,128]{2,1,0:T(8,128)(2,1)S(1)} %pad_maximum_fusion.2.refs_4_), channel_id=1, source_target_pairs={{0,16},{4,20},{8,24},{12,28},{16,0},{20,4},{24,8},{28,12},{1,17},{... | collective-permute-start | bytes 196616 | tf_op jit(solution)/shard_map/ppermute | solution.py:474
  18.8 6.8 %collective-permute-start.10 = (bf16[4,64,128]{2,1,0:T(8,128)(2,1)S(1)}, bf16[4,64,128]{2,1,0:T(8,128)(2,1)S(1)}, u32[]{:S(2)}, u32[]{:S(2)}) collective-permute-start(bf16[4,64,128]{2,1,0:T(8,128)(2,1)S(1)} %pad_maximum_fusion.2.refs_4_), channel_id=1, source_target_pairs={{0,8},{4,12},{8,0},{12,4},{16,24},{20,28},{24,16},{28,20},{1,9},{5... | collective-permute-start | bytes 196616 | tf_op jit(solution)/shard_map/ppermute | solution.py:474
  22.7 4.3 %collective-permute-start.9 = (bf16[4,64,128]{2,1,0:T(8,128)(2,1)S(1)}, bf16[4,64,128]{2,1,0:T(8,128)(2,1)S(1)}, u32[]{:S(2)}, u32[]{:S(2)}) collective-permute-start(bf16[4,64,128]{2,1,0:T(8,128)(2,1)S(1)} %collective-permute-done.5.refs_6_), channel_id=1, source_target_pairs={{0,4},{4,0},{8,12},{12,8},{16,20},{20,16},{24,28},{28,24},{1,5},{5... | collective-permute-start | bytes 196616 | tf_op jit(solution)/shard_map/ppermute | solution.py:478
  23.2 4.5 %collective-permute-start.8 = (bf16[4,64,128]{2,1,0:T(8,128)(2,1)S(1)}, bf16[4,64,128]{2,1,0:T(8,128)(2,1)S(1)}, u32[]{:S(2)}, u32[]{:S(2)}) collective-permute-start(bf16[4,64,128]{2,1,0:T(8,128)(2,1)S(1)} %collective-permute-done.4.refs_5_), channel_id=1, source_target_pairs={{0,4},{4,0},{8,12},{12,8},{16,20},{20,16},{24,28},{28,24},{1,5},{5... | collective-permute-start | bytes 196616 | tf_op jit(solution)/shard_map/ppermute | solution.py:478
  24.7 4.8 %collective-permute-start.7 = (bf16[4,64,128]{2,1,0:T(8,128)(2,1)S(1)}, bf16[4,64,128]{2,1,0:T(8,128)(2,1)S(1)}, u32[]{:S(2)}, u32[]{:S(2)}) collective-permute-start(bf16[4,64,128]{2,1,0:T(8,128)(2,1)S(1)} %collective-permute-done.3.refs_4_), channel_id=1, source_target_pairs={{0,4},{4,0},{8,12},{12,8},{16,20},{20,16},{24,28},{28,24},{1,5},{5... | collective-permute-start | bytes 196616 | tf_op jit(solution)/shard_map/ppermute | solution.py:478
  29.5 8.1 %collective-permute-start.13 = (bf16[16,64,128]{2,1,0:T(8,128)(2,1)S(1)}, bf16[16,64,128]{2,1,0:T(8,128)(2,1)S(1)}, u32[]{:S(2)}, u32[]{:S(2)}) collective-permute-start(bf16[16,64,128]{2,1,0:T(8,128)(2,1)S(1)} %pad_maximum_fusion), channel_id=1, source_target_pairs={{0,4},{4,0},{8,12},{12,8},{16,20},{20,16},{24,28},{28,24},{1,5},{5... | collective-permute-start | bytes 786440 | tf_op jit(solution)/shard_map/ppermute | solution.py:478
  35.7 8.6 %collective-permute-start.18 = (bf16[4,4,64,128]{3,2,1,0:T(8,128)(2,1)S(1)}, bf16[4,4,64,128]{3,2,1,0:T(8,128)(2,1)S(1)}, u32[]{:S(2)}, u32[]{:S(2)}) collective-permute-start(bf16[4,4,64,128]{3,2,1,0:T(8,128)(2,1)S(1)} %get-tuple-element.63), channel_id=1, source_target_pairs={{0,4},{4,0},{8,12},{12,8},{16,20},{20,16},{24,28},{28,24},{1,5},{5... | collective-permute-start | bytes 786440 | tf_op jit(solution)/shard_map/ppermute | solution.py:508
  44.1 8.6 %collective-permute-start.14 = (bf16[4,4,64,128]{3,2,1,0:T(8,128)(2,1)S(1)}, bf16[4,4,64,128]{3,2,1,0:T(8,128)(2,1)S(1)}, u32[]{:S(2)}, u32[]{:S(2)}) collective-permute-start(bf16[4,4,64,128]{3,2,1,0:T(8,128)(2,1)S(1)} %get-tuple-element.56), channel_id=1, source_target_pairs={{0,4},{4,0},{8,12},{12,8},{16,20},{20,16},{24,28},{28,24},{1,5},{5... | collective-permute-start | bytes 786440 | tf_op jit(solution)/shard_map/ppermute | solution.py:518
  44.5 12.1 %collective-permute-start.19 = (bf16[4,64,128]{2,1,0:T(8,128)(2,1)S(1)}, bf16[4,64,128]{2,1,0:T(8,128)(2,1)S(1)}, u32[]{:S(2)}, u32[]{:S(2)}) collective-permute-start(bf16[4,64,128]{2,1,0:T(8,128)(2,1)S(1)} %get-tuple-element.70), channel_id=1, source_target_pairs={{0,24},{4,28},{8,16},{12,20},{16,8},{20,12},{24,0},{28,4},{1,25},{... | collective-permute-start | bytes 196616 | tf_op jit(solution)/shard_map/ppermute | solution.py:534
  49.4 7.8 %collective-permute-start.21 = (bf16[4,64,128]{2,1,0:T(8,128)(2,1)S(1)}, bf16[4,64,128]{2,1,0:T(8,128)(2,1)S(1)}, u32[]{:S(2)}, u32[]{:S(2)}) collective-permute-start(bf16[4,64,128]{2,1,0:T(8,128)(2,1)S(1)} %get-tuple-element.71), channel_id=1, source_target_pairs={{0,8},{4,12},{8,0},{12,4},{16,24},{20,28},{24,16},{28,20},{1,9},{5... | collective-permute-start | bytes 196616 | tf_op jit(solution)/shard_map/ppermute | solution.py:534
  49.4 7.8 %collective-permute-start.20 = (bf16[4,64,128]{2,1,0:T(8,128)(2,1)S(1)}, bf16[4,64,128]{2,1,0:T(8,128)(2,1)S(1)}, u32[]{:S(2)}, u32[]{:S(2)}) collective-permute-start(bf16[4,64,128]{2,1,0:T(8,128)(2,1)S(1)} %get-tuple-element.72), channel_id=1, source_target_pairs={{0,16},{4,20},{8,24},{12,28},{16,0},{20,4},{24,8},{28,12},{1,17},{... | collective-permute-start | bytes 196616 | tf_op jit(solution)/shard_map/ppermute | solution.py:534
  52.7 6.1 %collective-permute-start.15 = (bf16[4,64,128]{2,1,0:T(8,128)(2,1)S(1)}, bf16[4,64,128]{2,1,0:T(8,128)(2,1)S(1)}, u32[]{:S(2)}, u32[]{:S(2)}) collective-permute-start(bf16[4,64,128]{2,1,0:T(8,128)(2,1)S(1)} %get-tuple-element.73), channel_id=1, source_target_pairs={{0,24},{4,28},{8,16},{12,20},{16,8},{20,12},{24,0},{28,4},{1,25},{... | collective-permute-start | bytes 196616 | tf_op jit(solution)/shard_map/ppermute | solution.py:534
  56.6 4.3 %collective-permute-start.17 = (bf16[4,64,128]{2,1,0:T(8,128)(2,1)S(1)}, bf16[4,64,128]{2,1,0:T(8,128)(2,1)S(1)}, u32[]{:S(2)}, u32[]{:S(2)}) collective-permute-start(bf16[4,64,128]{2,1,0:T(8,128)(2,1)S(1)} %get-tuple-element.74), channel_id=1, source_target_pairs={{0,8},{4,12},{8,0},{12,4},{16,24},{20,28},{24,16},{28,20},{1,9},{5... | collective-permute-start | bytes 196616 | tf_op jit(solution)/shard_map/ppermute | solution.py:534
  56.6 5.2 %collective-permute-start.16 = (bf16[4,64,128]{2,1,0:T(8,128)(2,1)S(1)}, bf16[4,64,128]{2,1,0:T(8,128)(2,1)S(1)}, u32[]{:S(2)}, u32[]{:S(2)}) collective-permute-start(bf16[4,64,128]{2,1,0:T(8,128)(2,1)S(1)} %get-tuple-element.75), channel_id=1, source_target_pairs={{0,16},{4,20},{8,24},{12,28},{16,0},{20,4},{24,8},{28,12},{1,17},{... | collective-permute-start | bytes 196616 | tf_op jit(solution)/shard_map/ppermute | solution.py:534
  61.8 3.4 %collective-permute-start.24 = (bf16[128,128]{1,0:T(8,128)(2,1)S(1)}, bf16[128,128]{1,0:T(8,128)(2,1)S(1)}, u32[]{:S(2)}, u32[]{:S(2)}) collective-permute-start(bf16[128,128]{1,0:T(8,128)(2,1)S(1)} %get-tuple-element.76), channel_id=1, source_target_pairs={{0,3},{1,2},{2,1},{3,0},{4,7},{5,6},{6,5},{7,4},{8,11},{9,10},{10,... | collective-permute-start | bytes 98312 | tf_op jit(solution)/shard_map/ppermute | solution.py:543
  61.9 3.3 %collective-permute-start.22 = (bf16[128,128]{1,0:T(8,128)(2,1)S(1)}, bf16[128,128]{1,0:T(8,128)(2,1)S(1)}, u32[]{:S(2)}, u32[]{:S(2)}) collective-permute-start(bf16[128,128]{1,0:T(8,128)(2,1)S(1)} %get-tuple-element.78), channel_id=1, source_target_pairs={{0,1},{1,0},{2,3},{3,2},{4,5},{5,4},{6,7},{7,6},{8,9},{9,8},{10,11... | collective-permute-start | bytes 98312 | tf_op jit(solution)/shard_map/ppermute | solution.py:543
  62.9 3.9 %collective-permute-start.23 = (bf16[128,128]{1,0:T(8,128)(2,1)S(1)}, bf16[128,128]{1,0:T(8,128)(2,1)S(1)}, u32[]{:S(2)}, u32[]{:S(2)}) collective-permute-start(bf16[128,128]{1,0:T(8,128)(2,1)S(1)} %get-tuple-element.79), channel_id=1, source_target_pairs={{0,2},{1,3},{2,0},{3,1},{4,6},{5,7},{6,4},{7,5},{8,10},{9,11},{10,... | collective-permute-start | bytes 98312 | tf_op jit(solution)/shard_map/ppermute | solution.py:543
  (1 other events, 3.2 us)

commit v3 on v2

--- a/solution.py
+++ b/solution.py
@@ -265,8 +265,7 @@
         names += [rand_ref[step, i] for i in range(RAND)]
         for number, name in enumerate(names):
             owner = lax.div(name, blocks_here) ^ here
-            slot = lax.rem(owner, 2) * (seq_count // 2) + lax.div(owner, 2)
-            spots_ref[step, number] = slot * blocks_here + (lax.rem(name, blocks_here) ^ head)
+            spots_ref[step, number] = owner * blocks_here + (lax.rem(name, blocks_here) ^ head)
     for copy in copies[2:]:
         copy.wait()
 
@@ -327,8 +326,8 @@
     @pl.when(step == pl.num_programs(0) - 1)
     def _():
         for pair in range(pairs):
-            keep_ref[pair] = total[pl.ds(pair * size, size)]
-            ship_ref[pair] = total[pl.ds((pairs + pair) * size, size)].astype(jnp.bfloat16)
+            keep_ref[pair] = total[pl.ds(2 * pair * size, size)]
+            ship_ref[pair] = total[pl.ds((2 * pair + 1) * size, size)].astype(jnp.bfloat16)
 
 
 def stacked_heads(ref, chunk):
@@ -440,7 +439,7 @@
     listed = (3 + GLOB + RAND) * BLOCK
     columns = heads_here * BLOCK
     pairs = blocks_here * listed * columns
-    size = math.gcd(heads_here, 4)
+    size = heads_here
 
     smem = pl.BlockSpec(memory_space=pltpu.SMEM)
     anywhere = pl.BlockSpec(memory_space=pl.ANY)
@@ -477,11 +476,12 @@
     def to_near(part):
         return lax.ppermute(part, "seq", flips(seq_count, 1))
 
-    key_parts = along_far(jnp.stack([p[:short] for p in pieces]))
-    key_parts += [to_near(p) for p in key_parts]
-    value_parts = along_far(jnp.stack([p[short:] for p in pieces]))
-    key_parts, value_parts = lax.optimization_barrier((key_parts, value_parts))
-    value_parts.append(to_near(jnp.concatenate(value_parts)))
+    key_far = along_far(jnp.stack([p[:short] for p in pieces]))
+    key_parts = [part for far in key_far for part in (far, to_near(far))]
+    value_own = jnp.stack([p[short:] for p in pieces])
+    value_pair = jnp.concatenate([value_own, to_near(value_own)])
+    value_pair, _ = lax.optimization_barrier((value_pair, key_far[1:]))
+    value_parts = along_far(value_pair)
 
     tile = pl.BlockSpec((BLOCK, width), lambda i: (i, 0))
     square = pl.BlockSpec((1, listed, columns), lambda i: (i, 0, 0))
@@ -523,9 +523,7 @@
         out_specs=tile,
         out_shape=tile_shape,
         **kernel_options(1, pairs),
-    )(dscores, key_lists)
-
-    key_near, d_queries = lax.optimization_barrier((key_near, d_queries))
+    )(*lax.optimization_barrier((dscores, key_lists, key_near))[:2])
 
     def returned(keep, near):
         sums = keep + near.astype(jnp.float32)

time: 67.7 us -> 61.1 us (0.903)
  waiting for transfers between devices: 17.9 us -> 10.7 us
  starting transfers between devices: 30.8 us -> 31.8 us
    ppermute x5, waiting for transfers between devices: 3.89 us -> 0.01 us  [to_near(): return lax.ppermute(part, 'seq', flips(seq_count, 1))]
    ppermute x3, waiting for transfers between devices: 2.81 us -> 0.25 us  [whole_body(): lax.ppermute(packed[k], 'head', flips(head_count, k))]
    ppermute x5, starting transfers between devices: 4.38 us -> 5.7 us  [to_near(): return lax.ppermute(part, 'seq', flips(seq_count, 1))]
    ppermute x6, waiting for transfers between devices: 4.48 us -> 3.24 us  [returned(): lax.ppermute(sums[pair].astype(jnp.bfloat16), 'seq', flips(seq_count, 2 *...]
    ppermute x6, starting transfers between devices: 10 us -> 8.91 us  [returned(): lax.ppermute(sums[pair].astype(jnp.bfloat16), 'seq', flips(seq_count, 2 *...]
    ppermute x1, waiting for transfers between devices: 0.01 us -> 1.12 us  [whole_body(): key_near = lax.ppermute(key_ship, 'seq', flips(seq_count, 1))]
    ppermute x1, starting transfers between devices: 0.26 us -> 1.32 us  [whole_body(): key_near = lax.ppermute(key_ship, 'seq', flips(seq_count, 1))]
  transfers between devices with their start and end apart: 25 -> 25, of which waited for: 12 -> 8; matrix products, arithmetic and copies ran while one was open for 0% -> 0% of each run, Pallas kernels for 22% -> 24%
where the time goes in v3:
time: 61.1 us; the launch traced here: 60.9 us
  starting transfers between devices  31.8 us (52%)
  Pallas kernels  17.3 us (28%)
  waiting for transfers between devices  10.7 us (18%)
  between operations  0.77 us (1%)
    ppermute x6, starting transfers between devices, returned(): lax.ppermute(sums[pair].astype(jnp.bfloat16), 'seq', flips(seq_count, 2 *...  8.91 us
    ppermute x6, starting transfers between devices, along_far(): parts.append(lax.ppermute(own, 'seq', flips(seq_count, k)))  8.9 us
    pallas_call x1, Pallas kernels, whole_body(): pl.pallas_call(lambda *refs: dscores_kernel(size, *refs), grid=(blocks_he...  6.1 us
    pallas_call x1, Pallas kernels, whole_body(): pl.pallas_call(lambda *refs: probs_kernel(seq_count, size, *refs), grid=(...  5.92 us
    ppermute x5, starting transfers between devices, to_near(): return lax.ppermute(part, 'seq', flips(seq_count, 1))  5.7 us
    ppermute x3, waiting for transfers between devices, whole_body(): lax.ppermute(pieces[k], 'head', flips(head_count, k))  3.25 us
    ppermute x6, waiting for transfers between devices, returned(): lax.ppermute(sums[pair].astype(jnp.bfloat16), 'seq', flips(seq_count, 2 *...  3.24 us
    ppermute x3, starting transfers between devices, whole_body(): lax.ppermute(pieces[k], 'head', flips(head_count, k))  3.15 us
  transfers between devices with their start and end apart: 25, of which 8 were waited for; matrix products, arithmetic and copies ran while one was open for 0% of the time, Pallas kernels for 24%

profile of v3, /device:TPU:0, one launch (start us, length us, event | category | flops | bytes accessed | tf_op | source)
XLA Modules:
  0.0 60.9 jit_solution(1305637179378410522)
XLA Ops:
  0.6 2.1 %shard_map.93 = (bf16[128,128]{1,0:T(8,128)(2,1)S(1)}, bf16[128,128]{1,0:T(8,128)(2,1)S(1)}, bf16[128,128]{1,0:T(8,128)(2,1)S(1)}, bf16[128,128]{1,0:T(8,128)(2,...) custom-call(s32[4,8]{1,0:T(4,128)} %refs_0_.1, s32[2]{0:T(128)} %refs_1_.1, ...), custom_call_target="tpu_custom_call" | custom-call | tf_op jit(solution)/shard_map/pallas_call | solution.py:449
  3.2 2.6 %collective-permute-start.1 = (bf16[128,128]{1,0:T(8,128)(2,1)S(1)}, bf16[128,128]{1,0:T(8,128)(2,1)S(1)}, u32[]{:S(2)}, u32[]{:S(2)}) collective-permute-start(bf16[128,128]{1,0:T(8,128)(2,1)S(1)} %get-tuple-element.29), channel_id=1, source_target_pairs={{0,2},{1,3},{2,0},{3,1},{4,6},{5,7},{6,4},{7,5},{8,10},{9,11},{10,... | collective-permute-start | bytes 98312 | tf_op jit(solution)/shard_map/ppermute | solution.py:467
  5.9 1.9 %collective-permute-done.1 = bf16[128,128]{1,0:T(8,128)(2,1)S(1)} collective-permute-done((bf16[128,128]{1,0:T(8,128)(2,1)S(1)}, bf16[128,128]{1,0:T(8,128)(2,1)S(1)}, u32[]{:S(2)}, u32[]{:S(2)}) %collective-permute-start.1) | collective-permute-done | bytes 32800 | tf_op jit(solution)/shard_map/ppermute | solution.py:467
  7.8 1.4 %collective-permute-done.2 = bf16[128,128]{1,0:T(8,128)(2,1)S(1)} collective-permute-done((bf16[128,128]{1,0:T(8,128)(2,1)S(1)}, bf16[128,128]{1,0:T(8,128)(2,1)S(1)}, u32[]{:S(2)}, u32[]{:S(2)}) %collective-permute-start.2) | collective-permute-done | bytes 32800 | tf_op jit(solution)/shard_map/ppermute | solution.py:467
  9.2 3.7 %collective-permute-start.8 = (bf16[4,64,128]{2,1,0:T(8,128)(2,1)S(1)}, bf16[4,64,128]{2,1,0:T(8,128)(2,1)S(1)}, u32[]{:S(2)}, u32[]{:S(2)}) collective-permute-start(bf16[4,64,128]{2,1,0:T(8,128)(2,1)S(1)} %pad_maximum_fusion.refs_3_), channel_id=1, source_target_pairs={{0,24},{4,28},{8,16},{12,20},{16,8},{20,12},{24,0},{28,4},{1,25},{... | collective-permute-start | bytes 196616 | tf_op jit(solution)/shard_map/ppermute | solution.py:473
  13.6 1.5 %collective-permute-start.3 = (bf16[4,64,128]{2,1,0:T(8,128)(2,1)S(1)}, bf16[4,64,128]{2,1,0:T(8,128)(2,1)S(1)}, u32[]{:S(2)}, u32[]{:S(2)}) collective-permute-start(bf16[4,64,128]{2,1,0:T(8,128)(2,1)S(1)} %pad_maximum_fusion.refs_3_), channel_id=1, source_target_pairs={{0,4},{4,0},{8,12},{12,8},{16,20},{20,16},{24,28},{28,24},{1,5},{5... | collective-permute-start | bytes 196616 | tf_op jit(solution)/shard_map/ppermute | solution.py:477
  15.8 1.6 %collective-permute-start.9 = (bf16[4,64,128]{2,1,0:T(8,128)(2,1)S(1)}, bf16[4,64,128]{2,1,0:T(8,128)(2,1)S(1)}, u32[]{:S(2)}, u32[]{:S(2)}) collective-permute-start(bf16[4,64,128]{2,1,0:T(8,128)(2,1)S(1)} %collective-permute-done.8.refs_9_), channel_id=1, source_target_pairs={{0,4},{4,0},{8,12},{12,8},{16,20},{20,16},{24,28},{28,24},{1,5},{5... | collective-permute-start | bytes 196616 | tf_op jit(solution)/shard_map/ppermute | solution.py:477
  17.3 1.4 %collective-permute-done.6.refs_7_ = bf16[4,64,128]{2,1,0:T(8,128)(2,1)S(1)} collective-permute-done((bf16[4,64,128]{2,1,0:T(8,128)(2,1)S(1)}, bf16[4,64,128]{2,1,0:T(8,128)(2,1)S(1)}, u32[]{:S(2)}, u32[]{:S(2)}) %collective-permute-start.6) | collective-permute-done | bytes 65568 | tf_op jit(solution)/shard_map/ppermute | solution.py:473
  18.7 1.5 %collective-permute-start.7 = (bf16[4,64,128]{2,1,0:T(8,128)(2,1)S(1)}, bf16[4,64,128]{2,1,0:T(8,128)(2,1)S(1)}, u32[]{:S(2)}, u32[]{:S(2)}) collective-permute-start(bf16[4,64,128]{2,1,0:T(8,128)(2,1)S(1)} %collective-permute-done.6.refs_7_), channel_id=1, source_target_pairs={{0,4},{4,0},{8,12},{12,8},{16,20},{20,16},{24,28},{28,24},{1,5},{5... | collective-permute-start | bytes 196616 | tf_op jit(solution)/shard_map/ppermute | solution.py:477
  20.8 2.8 %collective-permute-start.13 = (bf16[8,64,128]{2,1,0:T(8,128)(2,1)S(1)}, bf16[8,64,128]{2,1,0:T(8,128)(2,1)S(1)}, u32[]{:S(2)}, u32[]{:S(2)}) collective-permute-start(bf16[8,64,128]{2,1,0:T(8,128)(2,1)S(1)} %constant_dynamic-update-slice_fusion.refs_4_), channel_id=1, source_target_pairs={{0,24},{4,28},{8,16},{12,20},{16,8},{20,12},{24,0},{28,4},{1,25},{... | collective-permute-start | bytes 393224 | tf_op jit(solution)/shard_map/ppermute | solution.py:473
  23.6 1.7 %collective-permute-start.11 = (bf16[8,64,128]{2,1,0:T(8,128)(2,1)S(1)}, bf16[8,64,128]{2,1,0:T(8,128)(2,1)S(1)}, u32[]{:S(2)}, u32[]{:S(2)}) collective-permute-start(bf16[8,64,128]{2,1,0:T(8,128)(2,1)S(1)} %constant_dynamic-update-slice_fusion.refs_4_), channel_id=1, source_target_pairs={{0,8},{4,12},{8,0},{12,4},{16,24},{20,28},{24,16},{28,20},{1,9},{5... | collective-permute-start | bytes 393224 | tf_op jit(solution)/shard_map/ppermute | solution.py:473
  25.2 5.9 %shard_map.94 = (bf16[4,832,512]{2,1,0:T(8,128)(2,1)S(1)}, bf16[4,832,128]{2,1,0:T(8,128)(2,1)S(1)}, f32[4,4,64,128]{3,2,1,0:T(8,128)S(1)}, bf16[4,4,64,128]{3,2,1,0:T(8,128)(2,1)S(1)}) custom-call(s32[4,13]{1,0:T(4,128)S(1)} %get-tuple-element.24.refs_0_, bf16[256,1024]{1,0:T(8,128)(2,1)S(1)} %get-tuple-element.25.refs_1_, ...), custom_call_target="tpu_custom_call" | custom-call | flops 1744830464 | bytes 6815744 | tf_op jit(solution)/shard_map/pallas_call | solution.py:499
  31.2 1.6 %collective-permute-start.18 = (bf16[4,4,64,128]{3,2,1,0:T(8,128)(2,1)S(1)}, bf16[4,4,64,128]{3,2,1,0:T(8,128)(2,1)S(1)}, u32[]{:S(2)}, u32[]{:S(2)}) collective-permute-start(bf16[4,4,64,128]{3,2,1,0:T(8,128)(2,1)S(1)} %get-tuple-element.41), channel_id=1, source_target_pairs={{0,4},{4,0},{8,12},{12,8},{16,20},{20,16},{24,28},{28,24},{1,5},{5... | collective-permute-start | bytes 786440 | tf_op jit(solution)/shard_map/ppermute | solution.py:508
  32.8 1.4 %collective-permute-done.12.refs_6_ = bf16[8,64,128]{2,1,0:T(8,128)(2,1)S(1)} collective-permute-done((bf16[8,64,128]{2,1,0:T(8,128)(2,1)S(1)}, bf16[8,64,128]{2,1,0:T(8,128)(2,1)S(1)}, u32[]{:S(2)}, u32[]{:S(2)}) %collective-permute-start.12) | collective-permute-done | bytes 131104 | tf_op jit(solution)/shard_map/ppermute | solution.py:473
  34.2 6.1 %shard_map.95 = (bf16[256,1024]{1,0:T(8,128)(2,1)}, bf16[4,832,512]{2,1,0:T(8,128)(2,1)S(1)}, f32[4,4,64,128]{3,2,1,0:T(8,128)S(1)}, bf16[4,4,64,128]{3,2,1,0:T(8,128)(2,1)S(1)}) custom-call(s32[4,13]{1,0:T(4,128)S(1)} %get-tuple-element.24.refs_0_, bf16[256,1024]{1,0:T(8,128)(2,1)S(1)} %get-tuple-element.25.refs_1_, ...), custom_call_target="tpu_custom_call" | custom-call | flops 2617245696 | bytes 6815744 | tf_op jit(solution)/shard_map/pallas_call | solution.py:509
  40.3 1.3 %collective-permute-start.14 = (bf16[4,4,64,128]{3,2,1,0:T(8,128)(2,1)S(1)}, bf16[4,4,64,128]{3,2,1,0:T(8,128)(2,1)S(1)}, u32[]{:S(2)}, u32[]{:S(2)}) collective-permute-start(bf16[4,4,64,128]{3,2,1,0:T(8,128)(2,1)S(1)} %get-tuple-element.36), channel_id=1, source_target_pairs={{0,4},{4,0},{8,12},{12,8},{16,20},{20,16},{24,28},{28,24},{1,5},{5... | collective-permute-start | bytes 786440 | tf_op jit(solution)/shard_map/ppermute | solution.py:518
  41.8 2.4 %collective-permute-start.19 = (bf16[4,64,128]{2,1,0:T(8,128)(2,1)S(1)}, bf16[4,64,128]{2,1,0:T(8,128)(2,1)S(1)}, u32[]{:S(2)}, u32[]{:S(2)}) collective-permute-start(bf16[4,64,128]{2,1,0:T(8,128)(2,1)S(1)} %get-tuple-element.48), channel_id=1, source_target_pairs={{0,24},{4,28},{8,16},{12,20},{16,8},{20,12},{24,0},{28,4},{1,25},{... | collective-permute-start | bytes 196616 | tf_op jit(solution)/shard_map/ppermute | solution.py:532
  44.2 2.0 %collective-permute-start.20 = (bf16[4,64,128]{2,1,0:T(8,128)(2,1)S(1)}, bf16[4,64,128]{2,1,0:T(8,128)(2,1)S(1)}, u32[]{:S(2)}, u32[]{:S(2)}) collective-permute-start(bf16[4,64,128]{2,1,0:T(8,128)(2,1)S(1)} %get-tuple-element.50), channel_id=1, source_target_pairs={{0,16},{4,20},{8,24},{12,28},{16,0},{20,4},{24,8},{28,12},{1,17},{... | collective-permute-start | bytes 196616 | tf_op jit(solution)/shard_map/ppermute | solution.py:532
  47.4 1.9 %collective-permute-start.15 = (bf16[4,64,128]{2,1,0:T(8,128)(2,1)S(1)}, bf16[4,64,128]{2,1,0:T(8,128)(2,1)S(1)}, u32[]{:S(2)}, u32[]{:S(2)}) collective-permute-start(bf16[4,64,128]{2,1,0:T(8,128)(2,1)S(1)} %get-tuple-element.51), channel_id=1, source_target_pairs={{0,24},{4,28},{8,16},{12,20},{16,8},{20,12},{24,0},{28,4},{1,25},{... | collective-permute-start | bytes 196616 | tf_op jit(solution)/shard_map/ppermute | solution.py:532
  49.4 2.5 %collective-permute-start.16 = (bf16[4,64,128]{2,1,0:T(8,128)(2,1)S(1)}, bf16[4,64,128]{2,1,0:T(8,128)(2,1)S(1)}, u32[]{:S(2)}, u32[]{:S(2)}) collective-permute-start(bf16[4,64,128]{2,1,0:T(8,128)(2,1)S(1)} %get-tuple-element.53), channel_id=1, source_target_pairs={{0,16},{4,20},{8,24},{12,28},{16,0},{20,4},{24,8},{28,12},{1,17},{... | collective-permute-start | bytes 196616 | tf_op jit(solution)/shard_map/ppermute | solution.py:532
  52.0 1.7 %collective-permute-done.15 = bf16[4,64,128]{2,1,0:T(8,128)(2,1)S(1)} collective-permute-done((bf16[4,64,128]{2,1,0:T(8,128)(2,1)S(1)}, bf16[4,64,128]{2,1,0:T(8,128)(2,1)S(1)}, u32[]{:S(2)}, u32[]{:S(2)}) %collective-permute-start.15) | collective-permute-done | bytes 65568 | tf_op jit(solution)/shard_map/ppermute | solution.py:532
  53.6 1.5 %collective-permute-done.17 = bf16[4,64,128]{2,1,0:T(8,128)(2,1)S(1)} collective-permute-done((bf16[4,64,128]{2,1,0:T(8,128)(2,1)S(1)}, bf16[4,64,128]{2,1,0:T(8,128)(2,1)S(1)}, u32[]{:S(2)}, u32[]{:S(2)}) %collective-permute-start.17) | collective-permute-done | bytes 65568 | tf_op jit(solution)/shard_map/ppermute | solution.py:532
  56.3 1.1 %collective-permute-start.23 = (bf16[128,128]{1,0:T(8,128)(2,1)S(1)}, bf16[128,128]{1,0:T(8,128)(2,1)S(1)}, u32[]{:S(2)}, u32[]{:S(2)}) collective-permute-start(bf16[128,128]{1,0:T(8,128)(2,1)S(1)} %get-tuple-element.57), channel_id=1, source_target_pairs={{0,2},{1,3},{2,0},{3,1},{4,6},{5,7},{6,4},{7,5},{8,10},{9,11},{10,... | collective-permute-start | bytes 98312 | tf_op jit(solution)/shard_map/ppermute | solution.py:541
  57.5 2.5 %shard_map.96 = bf16[256,1024]{1,0:T(8,128)(2,1)} custom-call(bf16[4,832,512]{2,1,0:T(8,128)(2,1)S(1)} %get-tuple-element.37.refs_0_, bf16[4,832,128]{2,1,0:T(8,128)(2,1)S(1)} %get-tuple-element.38.refs_1_), custom_call_target="tpu_custom_call" | custom-call | flops 872415232 | bytes 6815744 | tf_op jit(solution)/shard_map/pallas_call | solution.py:519
  (49 shorter events, 6.0 us)
Async XLA Ops:
  3.2 4.5 %collective-permute-start.1 = (bf16[128,128]{1,0:T(8,128)(2,1)S(1)}, bf16[128,128]{1,0:T(8,128)(2,1)S(1)}, u32[]{:S(2)}, u32[]{:S(2)}) collective-permute-start(bf16[128,128]{1,0:T(8,128)(2,1)S(1)} %get-tuple-element.29), channel_id=1, source_target_pairs={{0,2},{1,3},{2,0},{3,1},{4,6},{5,7},{6,4},{7,5},{8,10},{9,11},{10,... | collective-permute-start | bytes 98312 | tf_op jit(solution)/shard_map/ppermute | solution.py:467
  5.8 3.3 %collective-permute-start.2 = (bf16[128,128]{1,0:T(8,128)(2,1)S(1)}, bf16[128,128]{1,0:T(8,128)(2,1)S(1)}, u32[]{:S(2)}, u32[]{:S(2)}) collective-permute-start(bf16[128,128]{1,0:T(8,128)(2,1)S(1)} %get-tuple-element.30), channel_id=1, source_target_pairs={{0,3},{1,2},{2,1},{3,0},{4,7},{5,6},{6,5},{7,4},{8,11},{9,10},{10,... | collective-permute-start | bytes 98312 | tf_op jit(solution)/shard_map/ppermute | solution.py:467
  9.2 6.6 %collective-permute-start.8 = (bf16[4,64,128]{2,1,0:T(8,128)(2,1)S(1)}, bf16[4,64,128]{2,1,0:T(8,128)(2,1)S(1)}, u32[]{:S(2)}, u32[]{:S(2)}) collective-permute-start(bf16[4,64,128]{2,1,0:T(8,128)(2,1)S(1)} %pad_maximum_fusion.refs_3_), channel_id=1, source_target_pairs={{0,24},{4,28},{8,16},{12,20},{16,8},{20,12},{24,0},{28,4},{1,25},{... | collective-permute-start | bytes 196616 | tf_op jit(solution)/shard_map/ppermute | solution.py:473
  12.8 5.9 %collective-permute-start.6 = (bf16[4,64,128]{2,1,0:T(8,128)(2,1)S(1)}, bf16[4,64,128]{2,1,0:T(8,128)(2,1)S(1)}, u32[]{:S(2)}, u32[]{:S(2)}) collective-permute-start(bf16[4,64,128]{2,1,0:T(8,128)(2,1)S(1)} %pad_maximum_fusion.refs_3_), channel_id=1, source_target_pairs={{0,16},{4,20},{8,24},{12,28},{16,0},{20,4},{24,8},{28,12},{1,17},{... | collective-permute-start | bytes 196616 | tf_op jit(solution)/shard_map/ppermute | solution.py:473
  12.8 7.4 %collective-permute-start.4 = (bf16[4,64,128]{2,1,0:T(8,128)(2,1)S(1)}, bf16[4,64,128]{2,1,0:T(8,128)(2,1)S(1)}, u32[]{:S(2)}, u32[]{:S(2)}) collective-permute-start(bf16[4,64,128]{2,1,0:T(8,128)(2,1)S(1)} %pad_maximum_fusion.refs_3_), channel_id=1, source_target_pairs={{0,8},{4,12},{8,0},{12,4},{16,24},{20,28},{24,16},{28,20},{1,9},{5... | collective-permute-start | bytes 196616 | tf_op jit(solution)/shard_map/ppermute | solution.py:473
  13.6 9.9 %collective-permute-start.3 = (bf16[4,64,128]{2,1,0:T(8,128)(2,1)S(1)}, bf16[4,64,128]{2,1,0:T(8,128)(2,1)S(1)}, u32[]{:S(2)}, u32[]{:S(2)}) collective-permute-start(bf16[4,64,128]{2,1,0:T(8,128)(2,1)S(1)} %pad_maximum_fusion.refs_3_), channel_id=1, source_target_pairs={{0,4},{4,0},{8,12},{12,8},{16,20},{20,16},{24,28},{28,24},{1,5},{5... | collective-permute-start | bytes 196616 | tf_op jit(solution)/shard_map/ppermute | solution.py:477
  15.1 5.6 %collective-permute-start.10 = (bf16[4,64,128]{2,1,0:T(8,128)(2,1)S(1)}, bf16[4,64,128]{2,1,0:T(8,128)(2,1)S(1)}, u32[]{:S(2)}, u32[]{:S(2)}) collective-permute-start(bf16[4,64,128]{2,1,0:T(8,128)(2,1)S(1)} %pad_maximum_fusion.1), channel_id=1, source_target_pairs={{0,4},{4,0},{8,12},{12,8},{16,20},{20,16},{24,28},{28,24},{1,5},{5... | collective-permute-start | bytes 196616 | tf_op jit(solution)/shard_map/ppermute | solution.py:477
  15.8 7.8 %collective-permute-start.9 = (bf16[4,64,128]{2,1,0:T(8,128)(2,1)S(1)}, bf16[4,64,128]{2,1,0:T(8,128)(2,1)S(1)}, u32[]{:S(2)}, u32[]{:S(2)}) collective-permute-start(bf16[4,64,128]{2,1,0:T(8,128)(2,1)S(1)} %collective-permute-done.8.refs_9_), channel_id=1, source_target_pairs={{0,4},{4,0},{8,12},{12,8},{16,20},{20,16},{24,28},{28,24},{1,5},{5... | collective-permute-start | bytes 196616 | tf_op jit(solution)/shard_map/ppermute | solution.py:477
  18.7 6.5 %collective-permute-start.7 = (bf16[4,64,128]{2,1,0:T(8,128)(2,1)S(1)}, bf16[4,64,128]{2,1,0:T(8,128)(2,1)S(1)}, u32[]{:S(2)}, u32[]{:S(2)}) collective-permute-start(bf16[4,64,128]{2,1,0:T(8,128)(2,1)S(1)} %collective-permute-done.6.refs_7_), channel_id=1, source_target_pairs={{0,4},{4,0},{8,12},{12,8},{16,20},{20,16},{24,28},{28,24},{1,5},{5... | collective-permute-start | bytes 196616 | tf_op jit(solution)/shard_map/ppermute | solution.py:477
  20.2 5.0 %collective-permute-start.5 = (bf16[4,64,128]{2,1,0:T(8,128)(2,1)S(1)}, bf16[4,64,128]{2,1,0:T(8,128)(2,1)S(1)}, u32[]{:S(2)}, u32[]{:S(2)}) collective-permute-start(bf16[4,64,128]{2,1,0:T(8,128)(2,1)S(1)} %collective-permute-done.4.refs_5_), channel_id=1, source_target_pairs={{0,4},{4,0},{8,12},{12,8},{16,20},{20,16},{24,28},{28,24},{1,5},{5... | collective-permute-start | bytes 196616 | tf_op jit(solution)/shard_map/ppermute | solution.py:477
  20.8 12.0 %collective-permute-start.13 = (bf16[8,64,128]{2,1,0:T(8,128)(2,1)S(1)}, bf16[8,64,128]{2,1,0:T(8,128)(2,1)S(1)}, u32[]{:S(2)}, u32[]{:S(2)}) collective-permute-start(bf16[8,64,128]{2,1,0:T(8,128)(2,1)S(1)} %constant_dynamic-update-slice_fusion.refs_4_), channel_id=1, source_target_pairs={{0,24},{4,28},{8,16},{12,20},{16,8},{20,12},{24,0},{28,4},{1,25},{... | collective-permute-start | bytes 393224 | tf_op jit(solution)/shard_map/ppermute | solution.py:473
  23.6 10.6 %collective-permute-start.12 = (bf16[8,64,128]{2,1,0:T(8,128)(2,1)S(1)}, bf16[8,64,128]{2,1,0:T(8,128)(2,1)S(1)}, u32[]{:S(2)}, u32[]{:S(2)}) collective-permute-start(bf16[8,64,128]{2,1,0:T(8,128)(2,1)S(1)} %constant_dynamic-update-slice_fusion.refs_4_), channel_id=1, source_target_pairs={{0,16},{4,20},{8,24},{12,28},{16,0},{20,4},{24,8},{28,12},{1,17},{... | collective-permute-start | bytes 393224 | tf_op jit(solution)/shard_map/ppermute | solution.py:473
  23.6 10.6 %collective-permute-start.11 = (bf16[8,64,128]{2,1,0:T(8,128)(2,1)S(1)}, bf16[8,64,128]{2,1,0:T(8,128)(2,1)S(1)}, u32[]{:S(2)}, u32[]{:S(2)}) collective-permute-start(bf16[8,64,128]{2,1,0:T(8,128)(2,1)S(1)} %constant_dynamic-update-slice_fusion.refs_4_), channel_id=1, source_target_pairs={{0,8},{4,12},{8,0},{12,4},{16,24},{20,28},{24,16},{28,20},{1,9},{5... | collective-permute-start | bytes 393224 | tf_op jit(solution)/shard_map/ppermute | solution.py:473
  31.2 10.5 %collective-permute-start.18 = (bf16[4,4,64,128]{3,2,1,0:T(8,128)(2,1)S(1)}, bf16[4,4,64,128]{3,2,1,0:T(8,128)(2,1)S(1)}, u32[]{:S(2)}, u32[]{:S(2)}) collective-permute-start(bf16[4,4,64,128]{3,2,1,0:T(8,128)(2,1)S(1)} %get-tuple-element.41), channel_id=1, source_target_pairs={{0,4},{4,0},{8,12},{12,8},{16,20},{20,16},{24,28},{28,24},{1,5},{5... | collective-permute-start | bytes 786440 | tf_op jit(solution)/shard_map/ppermute | solution.py:508
  40.3 7.0 %collective-permute-start.14 = (bf16[4,4,64,128]{3,2,1,0:T(8,128)(2,1)S(1)}, bf16[4,4,64,128]{3,2,1,0:T(8,128)(2,1)S(1)}, u32[]{:S(2)}, u32[]{:S(2)}) collective-permute-start(bf16[4,4,64,128]{3,2,1,0:T(8,128)(2,1)S(1)} %get-tuple-element.36), channel_id=1, source_target_pairs={{0,4},{4,0},{8,12},{12,8},{16,20},{20,16},{24,28},{28,24},{1,5},{5... | collective-permute-start | bytes 786440 | tf_op jit(solution)/shard_map/ppermute | solution.py:518
  41.8 7.6 %collective-permute-start.19 = (bf16[4,64,128]{2,1,0:T(8,128)(2,1)S(1)}, bf16[4,64,128]{2,1,0:T(8,128)(2,1)S(1)}, u32[]{:S(2)}, u32[]{:S(2)}) collective-permute-start(bf16[4,64,128]{2,1,0:T(8,128)(2,1)S(1)} %get-tuple-element.48), channel_id=1, source_target_pairs={{0,24},{4,28},{8,16},{12,20},{16,8},{20,12},{24,0},{28,4},{1,25},{... | collective-permute-start | bytes 196616 | tf_op jit(solution)/shard_map/ppermute | solution.py:532
  44.2 7.7 %collective-permute-start.21 = (bf16[4,64,128]{2,1,0:T(8,128)(2,1)S(1)}, bf16[4,64,128]{2,1,0:T(8,128)(2,1)S(1)}, u32[]{:S(2)}, u32[]{:S(2)}) collective-permute-start(bf16[4,64,128]{2,1,0:T(8,128)(2,1)S(1)} %get-tuple-element.49), channel_id=1, source_target_pairs={{0,8},{4,12},{8,0},{12,4},{16,24},{20,28},{24,16},{28,20},{1,9},{5... | collective-permute-start | bytes 196616 | tf_op jit(solution)/shard_map/ppermute | solution.py:532
  44.2 7.7 %collective-permute-start.20 = (bf16[4,64,128]{2,1,0:T(8,128)(2,1)S(1)}, bf16[4,64,128]{2,1,0:T(8,128)(2,1)S(1)}, u32[]{:S(2)}, u32[]{:S(2)}) collective-permute-start(bf16[4,64,128]{2,1,0:T(8,128)(2,1)S(1)} %get-tuple-element.50), channel_id=1, source_target_pairs={{0,16},{4,20},{8,24},{12,28},{16,0},{20,4},{24,8},{28,12},{1,17},{... | collective-permute-start | bytes 196616 | tf_op jit(solution)/shard_map/ppermute | solution.py:532
  47.4 6.2 %collective-permute-start.15 = (bf16[4,64,128]{2,1,0:T(8,128)(2,1)S(1)}, bf16[4,64,128]{2,1,0:T(8,128)(2,1)S(1)}, u32[]{:S(2)}, u32[]{:S(2)}) collective-permute-start(bf16[4,64,128]{2,1,0:T(8,128)(2,1)S(1)} %get-tuple-element.51), channel_id=1, source_target_pairs={{0,24},{4,28},{8,16},{12,20},{16,8},{20,12},{24,0},{28,4},{1,25},{... | collective-permute-start | bytes 196616 | tf_op jit(solution)/shard_map/ppermute | solution.py:532
  49.4 5.8 %collective-permute-start.17 = (bf16[4,64,128]{2,1,0:T(8,128)(2,1)S(1)}, bf16[4,64,128]{2,1,0:T(8,128)(2,1)S(1)}, u32[]{:S(2)}, u32[]{:S(2)}) collective-permute-start(bf16[4,64,128]{2,1,0:T(8,128)(2,1)S(1)} %get-tuple-element.52), channel_id=1, source_target_pairs={{0,8},{4,12},{8,0},{12,4},{16,24},{20,28},{24,16},{28,20},{1,9},{5... | collective-permute-start | bytes 196616 | tf_op jit(solution)/shard_map/ppermute | solution.py:532
  49.4 5.8 %collective-permute-start.16 = (bf16[4,64,128]{2,1,0:T(8,128)(2,1)S(1)}, bf16[4,64,128]{2,1,0:T(8,128)(2,1)S(1)}, u32[]{:S(2)}, u32[]{:S(2)}) collective-permute-start(bf16[4,64,128]{2,1,0:T(8,128)(2,1)S(1)} %get-tuple-element.53), channel_id=1, source_target_pairs={{0,16},{4,20},{8,24},{12,28},{16,0},{20,4},{24,8},{28,12},{1,17},{... | collective-permute-start | bytes 196616 | tf_op jit(solution)/shard_map/ppermute | solution.py:532
  55.2 4.7 %collective-permute-start.24 = (bf16[128,128]{1,0:T(8,128)(2,1)S(1)}, bf16[128,128]{1,0:T(8,128)(2,1)S(1)}, u32[]{:S(2)}, u32[]{:S(2)}) collective-permute-start(bf16[128,128]{1,0:T(8,128)(2,1)S(1)} %get-tuple-element.54), channel_id=1, source_target_pairs={{0,3},{1,2},{2,1},{3,0},{4,7},{5,6},{6,5},{7,4},{8,11},{9,10},{10,... | collective-permute-start | bytes 98312 | tf_op jit(solution)/shard_map/ppermute | solution.py:541
  55.3 4.7 %collective-permute-start.22 = (bf16[128,128]{1,0:T(8,128)(2,1)S(1)}, bf16[128,128]{1,0:T(8,128)(2,1)S(1)}, u32[]{:S(2)}, u32[]{:S(2)}) collective-permute-start(bf16[128,128]{1,0:T(8,128)(2,1)S(1)} %get-tuple-element.56), channel_id=1, source_target_pairs={{0,1},{1,0},{2,3},{3,2},{4,5},{5,4},{6,7},{7,6},{8,9},{9,8},{10,11... | collective-permute-start | bytes 98312 | tf_op jit(solution)/shard_map/ppermute | solution.py:541
  56.3 3.9 %collective-permute-start.23 = (bf16[128,128]{1,0:T(8,128)(2,1)S(1)}, bf16[128,128]{1,0:T(8,128)(2,1)S(1)}, u32[]{:S(2)}, u32[]{:S(2)}) collective-permute-start(bf16[128,128]{1,0:T(8,128)(2,1)S(1)} %get-tuple-element.57), channel_id=1, source_target_pairs={{0,2},{1,3},{2,0},{3,1},{4,6},{5,7},{6,4},{7,5},{8,10},{9,11},{10,... | collective-permute-start | bytes 98312 | tf_op jit(solution)/shard_map/ppermute | solution.py:541
  (1 other events, 3.2 us)

commit v4 on v3

--- a/solution.py
+++ b/solution.py
@@ -238,20 +238,33 @@
     return pl.ds(pl.multiple_of((head ^ offset) * DH, DH), DH)
 
 
-def pack_kernel(seq_count, head_count, *refs):
-    rand_from, glob_from, keys_ref, values_ref, query_ref, grad_ref = refs[:6]
-    piece_refs = refs[6 : 6 + head_count]
-    spots_ref, query_out, grad_out, rand_ref, glob_ref, sems = refs[6 + head_count :]
+def run_copies(copies):
+    for copy in copies:
+        copy.start()
+    for copy in copies:
+        copy.wait()
+
+
+def pack_kernel(*refs):
+    keys_ref, values_ref, *piece_refs, sems = refs
+    head = lax.axis_index("head")
+    short = keys_ref.shape[0]
+    moves = []
+    for offset, piece in enumerate(piece_refs):
+        columns = head_columns(head, offset)
+        moves.append((keys_ref.at[:, columns], piece.at[pl.ds(0, short)]))
+        moves.append((values_ref.at[:, columns], piece.at[pl.ds(short, short)]))
+    run_copies([pltpu.make_async_copy(a, b, sems.at[n]) for n, (a, b) in enumerate(moves)])
+
+
+def list_kernel(seq_count, *refs):
+    rand_from, glob_from, query_from, grad_from = refs[:4]
+    spots_ref, query_ref, grad_ref, rand_ref, glob_ref, sems = refs[4:]
     here = lax.axis_index("seq")
     head = lax.axis_index("head")
-    short = keys_ref.shape[0]
-    copies = [(rand_from, rand_ref), (glob_from, glob_ref)]
-    for offset, piece in enumerate(piece_refs):
-        columns = head_columns(head, offset)
-        copies.append((keys_ref.at[:, columns], piece.at[pl.ds(0, short)]))
-        copies.append((values_ref.at[:, columns], piece.at[pl.ds(short, short)]))
-    copies += [(query_ref, query_out), (grad_ref, grad_out)]
-    copies = [pltpu.make_async_copy(a, b, sems.at[n]) for n, (a, b) in enumerate(copies)]
+    moves = [(rand_from, rand_ref), (glob_from, glob_ref)]
+    moves += [(query_from, query_ref), (grad_from, grad_ref)]
+    copies = [pltpu.make_async_copy(a, b, sems.at[n]) for n, (a, b) in enumerate(moves)]
     for copy in copies:
         copy.start()
     copies[0].wait()
@@ -266,8 +279,8 @@
         for number, name in enumerate(names):
             owner = lax.div(name, blocks_here) ^ here
             spots_ref[step, number] = owner * blocks_here + (lax.rem(name, blocks_here) ^ head)
-    for copy in copies[2:]:
-        copy.wait()
+    copies[2].wait()
+    copies[3].wait()
 
 
 def unpack_kernel(*refs):
@@ -446,23 +459,33 @@
     tile_shape = jax.ShapeDtypeStruct(queries.shape, jnp.bfloat16)
     piece = jax.ShapeDtypeStruct((2 * short, DH), jnp.bfloat16)
     spots_shape = jax.ShapeDtypeStruct((blocks_here, 3 + GLOB + RAND), jnp.int32)
-    *pieces, spots, query_here, grad_here = pl.pallas_call(
-        lambda *refs: pack_kernel(seq_count, head_count, *refs),
-        in_specs=[anywhere] * 6,
-        out_specs=[anywhere] * head_count + [smem] + [anywhere] * 2,
-        out_shape=[piece] * head_count + [spots_shape, tile_shape, tile_shape],
+    rand_blocks, glob_blocks, keys, values, queries, d_out = [
+        pltpu.with_memory_space_constraint(x, pltpu.HBM)
+        for x in (rand_blocks, glob_blocks, keys, values, queries, d_out)
+    ]
+    pieces = pl.pallas_call(
+        pack_kernel,
+        in_specs=[anywhere] * 2,
+        out_specs=[anywhere] * head_count,
+        out_shape=[piece] * head_count,
+        scratch_shapes=[pltpu.SemaphoreType.DMA((2 * head_count,))],
+        compiler_params=small_grant(),
+    )(keys, values)
+    spots, query_here, grad_here = pl.pallas_call(
+        lambda *refs: list_kernel(seq_count, *refs),
+        in_specs=[anywhere] * 4,
+        out_specs=[smem] + [anywhere] * 2,
+        out_shape=[spots_shape, tile_shape, tile_shape],
         scratch_shapes=[
             pltpu.SMEM(rand_blocks.shape, jnp.int32),
             pltpu.SMEM(glob_blocks.shape, jnp.int32),
-            pltpu.SemaphoreType.DMA((2 * head_count + 4,)),
+            pltpu.SemaphoreType.DMA((4,)),
         ],
         compiler_params=small_grant(),
-    )(
-        *[
-            pltpu.with_memory_space_constraint(x, pltpu.HBM)
-            for x in (rand_blocks, glob_blocks, keys, values, queries, d_out)
-        ]
-    )
+        cost_estimate=pl.CostEstimate(
+            flops=0, bytes_accessed=8 * tok_count * width, transcendentals=0
+        ),
+    )(rand_blocks, glob_blocks, queries, d_out)
     pieces = [pieces[0]] + [
         lax.ppermute(pieces[k], "head", flips(head_count, k)) for k in range(1, head_count)
     ]
@@ -516,6 +539,26 @@
         **kernel_options(3, pairs),
     )(spots, query_here, grad_here, probs, *value_parts)
     key_near = lax.ppermute(key_ship, "seq", flips(seq_count, 1))
+
+    def sums_of(keep, near):
+        sums = keep + near.astype(jnp.float32)
+        return sums[0], [sums[pair].astype(jnp.bfloat16) for pair in range(1, pair_count)]
+
+    def from_far(sums):
+        return [
+            lax.ppermute(sums[pair - 1], "seq", flips(seq_count, 2 * pair))
+            for pair in range(1, pair_count)
+        ]
+
+    def added(own, far):
+        for part in far:
+            own = own + part.astype(jnp.float32)
+        return own
+
+    key_own, key_sums = sums_of(key_keep, key_near)
+    key_far = from_far(key_sums)
+    value_own, value_sums = sums_of(value_keep, value_near)
+    value_far = from_far(value_sums)
     d_queries = pl.pallas_call(
         lambda *refs: dquery_kernel(size, *refs),
         grid=(blocks_here,),
@@ -523,19 +566,11 @@
         out_specs=tile,
         out_shape=tile_shape,
         **kernel_options(1, pairs),
-    )(*lax.optimization_barrier((dscores, key_lists, key_near))[:2])
-
-    def returned(keep, near):
-        sums = keep + near.astype(jnp.float32)
-        result = sums[0]
-        for pair in range(pair_count - 1, 0, -1):
-            result = result + lax.ppermute(
-                sums[pair].astype(jnp.bfloat16), "seq", flips(seq_count, 2 * pair)
-            ).astype(jnp.float32)
-        return result
-
+    )(*lax.optimization_barrier((dscores, key_lists, key_sums))[:2])
+
+    key_far, value_far, d_queries = lax.optimization_barrier((key_far, value_far, d_queries))
     packed = jnp.concatenate(
-        [returned(key_keep, key_near), returned(value_keep, value_near)], axis=1
+        [added(key_own, key_far), added(value_own, value_far)], axis=1
     ).astype(jnp.bfloat16)
     back = [packed[0]] + [
         lax.ppermute(packed[k], "head", flips(head_count, k)) for k in range(1, head_count)

time: 61.1 us -> 59.8 us (0.979)
  waiting for transfers between devices: 10.7 us -> 8.69 us
  Pallas kernels: 17.3 us -> 18 us
    ppermute x6, waiting for transfers between devices: 3.24 us -> 0.55 us  [from_far(): lax.ppermute(sums[pair - 1], 'seq', flips(seq_count, 2 * pair))]
    ppermute x3, waiting for transfers between devices: 0.25 us -> 2.78 us  [whole_body(): lax.ppermute(packed[k], 'head', flips(head_count, k))]
    ppermute x3, waiting for transfers between devices: 3.25 us -> 1.38 us  [whole_body(): lax.ppermute(pieces[k], 'head', flips(head_count, k))]
    pallas_call x1 -> x2, Pallas kernels: 2.07 us -> 2.77 us  [the longest x1 1.85 us: whole_body(): pl.pallas_call(lambda *refs: list_kernel(seq_count, *refs), in_specs=[any...]
  transfers between devices with their start and end apart: 25 -> 25, of which waited for: 8 -> 7; matrix products, arithmetic and copies ran while one was open for 0% -> 0% of each run, Pallas kernels for 24% -> 28%
where the time goes in v4:
time: 59.8 us; the launch traced here: 59.6 us
  starting transfers between devices  31.8 us (53%)
  Pallas kernels  18 us (30%)
  waiting for transfers between devices  8.69 us (15%)
  between operations  0.78 us (1%)
    ppermute x6, starting transfers between devices, from_far(): lax.ppermute(sums[pair - 1], 'seq', flips(seq_count, 2 * pair))  8.91 us
    ppermute x6, starting transfers between devices, along_far(): parts.append(lax.ppermute(own, 'seq', flips(seq_count, k)))  8.9 us
    pallas_call x1, Pallas kernels, whole_body(): pl.pallas_call(lambda *refs: dscores_kernel(size, *refs), grid=(blocks_he...  6.1 us
    pallas_call x1, Pallas kernels, whole_body(): pl.pallas_call(lambda *refs: probs_kernel(seq_count, size, *refs), grid=(...  5.92 us
    ppermute x5, starting transfers between devices, to_near(): return lax.ppermute(part, 'seq', flips(seq_count, 1))  5.7 us
    ppermute x3, starting transfers between devices, whole_body(): lax.ppermute(pieces[k], 'head', flips(head_count, k))  3.15 us
    ppermute x6, waiting for transfers between devices, along_far(): parts.append(lax.ppermute(own, 'seq', flips(seq_count, k)))  2.83 us
    ppermute x3, waiting for transfers between devices, whole_body(): lax.ppermute(packed[k], 'head', flips(head_count, k))  2.78 us
  transfers between devices with their start and end apart: 25, of which 7 were waited for; matrix products, arithmetic and copies ran while one was open for 0% of the time, Pallas kernels for 28%

profile of v4, /device:TPU:0, one launch (start us, length us, event | category | flops | bytes accessed | tf_op | source)
XLA Modules:
  0.0 59.6 jit_solution(18319386997277987627)
XLA Ops:
  2.1 2.6 %collective-permute-start.1 = (bf16[128,128]{1,0:T(8,128)(2,1)S(1)}, bf16[128,128]{1,0:T(8,128)(2,1)S(1)}, u32[]{:S(2)}, u32[]{:S(2)}) collective-permute-start(bf16[128,128]{1,0:T(8,128)(2,1)S(1)} %get-tuple-element.36), channel_id=1, source_target_pairs={{0,2},{1,3},{2,0},{3,1},{4,6},{5,7},{6,4},{7,5},{8,10},{9,11},{10,... | collective-permute-start | bytes 98312 | tf_op jit(solution)/shard_map/ppermute | solution.py:490
  4.7 1.9 %shard_map.93 = (s32[4,13]{1,0:T(4,128)S(1)}, bf16[256,1024]{1,0:T(8,128)(2,1)S(1)}, bf16[256,1024]{1,0:T(8,128)(2,1)S(1)}) custom-call(s32[4,8]{1,0:T(4,128)} %refs_0_.2, s32[2]{0:T(128)} %refs_1_.2, bf16[256,1024]{1,0:T(8,128)(2,1)} %refs_2_.1, bf16[256,1024]{1,0:T(8,128)(2,1)} %refs_3_.1), custom_call_target="tpu_custom_call" | custom-call | bytes 2097152 | tf_op jit(solution)/shard_map/pallas_call | solution.py:474
  6.6 1.4 %collective-permute-done.2 = bf16[128,128]{1,0:T(8,128)(2,1)S(1)} collective-permute-done((bf16[128,128]{1,0:T(8,128)(2,1)S(1)}, bf16[128,128]{1,0:T(8,128)(2,1)S(1)}, u32[]{:S(2)}, u32[]{:S(2)}) %collective-permute-start.2) | collective-permute-done | bytes 32800 | tf_op jit(solution)/shard_map/ppermute | solution.py:490
  8.0 3.7 %collective-permute-start.8 = (bf16[4,64,128]{2,1,0:T(8,128)(2,1)S(1)}, bf16[4,64,128]{2,1,0:T(8,128)(2,1)S(1)}, u32[]{:S(2)}, u32[]{:S(2)}) collective-permute-start(bf16[4,64,128]{2,1,0:T(8,128)(2,1)S(1)} %pad_maximum_fusion.refs_3_), channel_id=1, source_target_pairs={{0,24},{4,28},{8,16},{12,20},{16,8},{20,12},{24,0},{28,4},{1,25},{... | collective-permute-start | bytes 196616 | tf_op jit(solution)/shard_map/ppermute | solution.py:496
  12.5 1.5 %collective-permute-start.3 = (bf16[4,64,128]{2,1,0:T(8,128)(2,1)S(1)}, bf16[4,64,128]{2,1,0:T(8,128)(2,1)S(1)}, u32[]{:S(2)}, u32[]{:S(2)}) collective-permute-start(bf16[4,64,128]{2,1,0:T(8,128)(2,1)S(1)} %pad_maximum_fusion.refs_3_), channel_id=1, source_target_pairs={{0,4},{4,0},{8,12},{12,8},{16,20},{20,16},{24,28},{28,24},{1,5},{5... | collective-permute-start | bytes 196616 | tf_op jit(solution)/shard_map/ppermute | solution.py:500
  14.6 1.6 %collective-permute-start.9 = (bf16[4,64,128]{2,1,0:T(8,128)(2,1)S(1)}, bf16[4,64,128]{2,1,0:T(8,128)(2,1)S(1)}, u32[]{:S(2)}, u32[]{:S(2)}) collective-permute-start(bf16[4,64,128]{2,1,0:T(8,128)(2,1)S(1)} %collective-permute-done.8.refs_9_), channel_id=1, source_target_pairs={{0,4},{4,0},{8,12},{12,8},{16,20},{20,16},{24,28},{28,24},{1,5},{5... | collective-permute-start | bytes 196616 | tf_op jit(solution)/shard_map/ppermute | solution.py:500
  16.2 1.4 %collective-permute-done.6.refs_7_ = bf16[4,64,128]{2,1,0:T(8,128)(2,1)S(1)} collective-permute-done((bf16[4,64,128]{2,1,0:T(8,128)(2,1)S(1)}, bf16[4,64,128]{2,1,0:T(8,128)(2,1)S(1)}, u32[]{:S(2)}, u32[]{:S(2)}) %collective-permute-start.6) | collective-permute-done | bytes 65568 | tf_op jit(solution)/shard_map/ppermute | solution.py:496
  17.6 1.5 %collective-permute-start.7 = (bf16[4,64,128]{2,1,0:T(8,128)(2,1)S(1)}, bf16[4,64,128]{2,1,0:T(8,128)(2,1)S(1)}, u32[]{:S(2)}, u32[]{:S(2)}) collective-permute-start(bf16[4,64,128]{2,1,0:T(8,128)(2,1)S(1)} %collective-permute-done.6.refs_7_), channel_id=1, source_target_pairs={{0,4},{4,0},{8,12},{12,8},{16,20},{20,16},{24,28},{28,24},{1,5},{5... | collective-permute-start | bytes 196616 | tf_op jit(solution)/shard_map/ppermute | solution.py:500
  19.6 2.8 %collective-permute-start.13 = (bf16[8,64,128]{2,1,0:T(8,128)(2,1)S(1)}, bf16[8,64,128]{2,1,0:T(8,128)(2,1)S(1)}, u32[]{:S(2)}, u32[]{:S(2)}) collective-permute-start(bf16[8,64,128]{2,1,0:T(8,128)(2,1)S(1)} %constant_dynamic-update-slice_fusion.refs_4_), channel_id=1, source_target_pairs={{0,24},{4,28},{8,16},{12,20},{16,8},{20,12},{24,0},{28,4},{1,25},{... | collective-permute-start | bytes 393224 | tf_op jit(solution)/shard_map/ppermute | solution.py:496
  22.4 1.7 %collective-permute-start.11 = (bf16[8,64,128]{2,1,0:T(8,128)(2,1)S(1)}, bf16[8,64,128]{2,1,0:T(8,128)(2,1)S(1)}, u32[]{:S(2)}, u32[]{:S(2)}) collective-permute-start(bf16[8,64,128]{2,1,0:T(8,128)(2,1)S(1)} %constant_dynamic-update-slice_fusion.refs_4_), channel_id=1, source_target_pairs={{0,8},{4,12},{8,0},{12,4},{16,24},{20,28},{24,16},{28,20},{1,9},{5... | collective-permute-start | bytes 393224 | tf_op jit(solution)/shard_map/ppermute | solution.py:496
  24.1 5.9 %shard_map.95 = (bf16[4,832,512]{2,1,0:T(8,128)(2,1)S(1)}, bf16[4,832,128]{2,1,0:T(8,128)(2,1)S(1)}, f32[4,4,64,128]{3,2,1,0:T(8,128)S(1)}, bf16[4,4,64,128]{3,2,1,0:T(8,128)(2,1)S(1)}) custom-call(s32[4,13]{1,0:T(4,128)S(1)} %get-tuple-element.31.refs_0_, bf16[256,1024]{1,0:T(8,128)(2,1)S(1)} %get-tuple-element.32.refs_1_, ...), custom_call_target="tpu_custom_call" | custom-call | flops 1744830464 | bytes 6815744 | tf_op jit(solution)/shard_map/pallas_call | solution.py:522
  30.0 1.6 %collective-permute-start.18 = (bf16[4,4,64,128]{3,2,1,0:T(8,128)(2,1)S(1)}, bf16[4,4,64,128]{3,2,1,0:T(8,128)(2,1)S(1)}, u32[]{:S(2)}, u32[]{:S(2)}) collective-permute-start(bf16[4,4,64,128]{3,2,1,0:T(8,128)(2,1)S(1)} %get-tuple-element.44), channel_id=1, source_target_pairs={{0,4},{4,0},{8,12},{12,8},{16,20},{20,16},{24,28},{28,24},{1,5},{5... | collective-permute-start | bytes 786440 | tf_op jit(solution)/shard_map/ppermute | solution.py:531
  31.6 1.4 %collective-permute-done.12.refs_6_ = bf16[8,64,128]{2,1,0:T(8,128)(2,1)S(1)} collective-permute-done((bf16[8,64,128]{2,1,0:T(8,128)(2,1)S(1)}, bf16[8,64,128]{2,1,0:T(8,128)(2,1)S(1)}, u32[]{:S(2)}, u32[]{:S(2)}) %collective-permute-start.12) | collective-permute-done | bytes 131104 | tf_op jit(solution)/shard_map/ppermute | solution.py:496
  33.0 6.1 %shard_map.96 = (bf16[256,1024]{1,0:T(8,128)(2,1)}, bf16[4,832,512]{2,1,0:T(8,128)(2,1)S(1)}, f32[4,4,64,128]{3,2,1,0:T(8,128)S(1)}, bf16[4,4,64,128]{3,2,1,0:T(8,128)(2,1)S(1)}) custom-call(s32[4,13]{1,0:T(4,128)S(1)} %get-tuple-element.31.refs_0_, bf16[256,1024]{1,0:T(8,128)(2,1)S(1)} %get-tuple-element.32.refs_1_, ...), custom_call_target="tpu_custom_call" | custom-call | flops 2617245696 | bytes 6815744 | tf_op jit(solution)/shard_map/pallas_call | solution.py:532
  39.2 1.3 %collective-permute-start.14 = (bf16[4,4,64,128]{3,2,1,0:T(8,128)(2,1)S(1)}, bf16[4,4,64,128]{3,2,1,0:T(8,128)(2,1)S(1)}, u32[]{:S(2)}, u32[]{:S(2)}) collective-permute-start(bf16[4,4,64,128]{3,2,1,0:T(8,128)(2,1)S(1)} %get-tuple-element.42), channel_id=1, source_target_pairs={{0,4},{4,0},{8,12},{12,8},{16,20},{20,16},{24,28},{28,24},{1,5},{5... | collective-permute-start | bytes 786440 | tf_op jit(solution)/shard_map/ppermute | solution.py:541
  40.6 2.4 %collective-permute-start.21 = (bf16[4,64,128]{2,1,0:T(8,128)(2,1)S(1)}, bf16[4,64,128]{2,1,0:T(8,128)(2,1)S(1)}, u32[]{:S(2)}, u32[]{:S(2)}) collective-permute-start(bf16[4,64,128]{2,1,0:T(8,128)(2,1)S(1)} %get-tuple-element.62), channel_id=1, source_target_pairs={{0,24},{4,28},{8,16},{12,20},{16,8},{20,12},{24,0},{28,4},{1,25},{... | collective-permute-start | bytes 196616 | tf_op jit(solution)/shard_map/ppermute | solution.py:549
  43.0 2.0 %collective-permute-start.19 = (bf16[4,64,128]{2,1,0:T(8,128)(2,1)S(1)}, bf16[4,64,128]{2,1,0:T(8,128)(2,1)S(1)}, u32[]{:S(2)}, u32[]{:S(2)}) collective-permute-start(bf16[4,64,128]{2,1,0:T(8,128)(2,1)S(1)} %get-tuple-element.64), channel_id=1, source_target_pairs={{0,8},{4,12},{8,0},{12,4},{16,24},{20,28},{24,16},{28,20},{1,9},{5... | collective-permute-start | bytes 196616 | tf_op jit(solution)/shard_map/ppermute | solution.py:549
  45.0 1.1 %collective-permute-done.14 = bf16[4,4,64,128]{3,2,1,0:T(8,128)(2,1)S(1)} collective-permute-done((bf16[4,4,64,128]{3,2,1,0:T(8,128)(2,1)S(1)}, bf16[4,4,64,128]{3,2,1,0:T(8,128)(2,1)S(1)}, u32[]{:S(2)}, u32[]{:S(2)}) %collective-permute-start.14) | collective-permute-done | bytes 262176 | tf_op jit(solution)/shard_map/ppermute | solution.py:541
  46.3 1.9 %collective-permute-start.17 = (bf16[4,64,128]{2,1,0:T(8,128)(2,1)S(1)}, bf16[4,64,128]{2,1,0:T(8,128)(2,1)S(1)}, u32[]{:S(2)}, u32[]{:S(2)}) collective-permute-start(bf16[4,64,128]{2,1,0:T(8,128)(2,1)S(1)} %get-tuple-element.65), channel_id=1, source_target_pairs={{0,24},{4,28},{8,16},{12,20},{16,8},{20,12},{24,0},{28,4},{1,25},{... | collective-permute-start | bytes 196616 | tf_op jit(solution)/shard_map/ppermute | solution.py:549
  48.2 2.5 %collective-permute-start.15 = (bf16[4,64,128]{2,1,0:T(8,128)(2,1)S(1)}, bf16[4,64,128]{2,1,0:T(8,128)(2,1)S(1)}, u32[]{:S(2)}, u32[]{:S(2)}) collective-permute-start(bf16[4,64,128]{2,1,0:T(8,128)(2,1)S(1)} %get-tuple-element.67), channel_id=1, source_target_pairs={{0,8},{4,12},{8,0},{12,4},{16,24},{20,28},{24,16},{28,20},{1,9},{5... | collective-permute-start | bytes 196616 | tf_op jit(solution)/shard_map/ppermute | solution.py:549
  50.8 2.5 %shard_map.97 = bf16[256,1024]{1,0:T(8,128)(2,1)} custom-call(bf16[4,832,512]{2,1,0:T(8,128)(2,1)S(1)} %get-tuple-element.47.refs_0_, bf16[4,832,128]{2,1,0:T(8,128)(2,1)S(1)} %get-tuple-element.48.refs_1_), custom_call_target="tpu_custom_call" | custom-call | flops 872415232 | bytes 6815744 | tf_op jit(solution)/shard_map/pallas_call | solution.py:562
  55.0 1.1 %collective-permute-start.23 = (bf16[128,128]{1,0:T(8,128)(2,1)S(1)}, bf16[128,128]{1,0:T(8,128)(2,1)S(1)}, u32[]{:S(2)}, u32[]{:S(2)}) collective-permute-start(bf16[128,128]{1,0:T(8,128)(2,1)S(1)} %get-tuple-element.71), channel_id=1, source_target_pairs={{0,2},{1,3},{2,0},{3,1},{4,6},{5,7},{6,4},{7,5},{8,10},{9,11},{10,... | collective-permute-start | bytes 98312 | tf_op jit(solution)/shard_map/ppermute | solution.py:576
  56.1 1.2 %collective-permute-done.24.refs_3_ = bf16[128,128]{1,0:T(8,128)(2,1)S(1)} collective-permute-done((bf16[128,128]{1,0:T(8,128)(2,1)S(1)}, bf16[128,128]{1,0:T(8,128)(2,1)S(1)}, u32[]{:S(2)}, u32[]{:S(2)}) %collective-permute-start.24) | collective-permute-done | bytes 32800 | tf_op jit(solution)/shard_map/ppermute | solution.py:576
  57.3 1.6 %collective-permute-done.23.refs_2_ = bf16[128,128]{1,0:T(8,128)(2,1)S(1)} collective-permute-done((bf16[128,128]{1,0:T(8,128)(2,1)S(1)}, bf16[128,128]{1,0:T(8,128)(2,1)S(1)}, u32[]{:S(2)}, u32[]{:S(2)}) %collective-permute-start.23) | collective-permute-done | bytes 32800 | tf_op jit(solution)/shard_map/ppermute | solution.py:576
  (49 shorter events, 6.1 us)
Async XLA Ops:
  1.6 5.0 %collective-permute-start = (bf16[128,128]{1,0:T(8,128)(2,1)S(1)}, bf16[128,128]{1,0:T(8,128)(2,1)S(1)}, u32[]{:S(2)}, u32[]{:S(2)}) collective-permute-start(bf16[128,128]{1,0:T(8,128)(2,1)S(1)} %get-tuple-element.35), channel_id=1, source_target_pairs={{0,1},{1,0},{2,3},{3,2},{4,5},{5,4},{6,7},{7,6},{8,9},{9,8},{10,11... | collective-permute-start | bytes 98312 | tf_op jit(solution)/shard_map/ppermute | solution.py:490
  2.1 4.5 %collective-permute-start.1 = (bf16[128,128]{1,0:T(8,128)(2,1)S(1)}, bf16[128,128]{1,0:T(8,128)(2,1)S(1)}, u32[]{:S(2)}, u32[]{:S(2)}) collective-permute-start(bf16[128,128]{1,0:T(8,128)(2,1)S(1)} %get-tuple-element.36), channel_id=1, source_target_pairs={{0,2},{1,3},{2,0},{3,1},{4,6},{5,7},{6,4},{7,5},{8,10},{9,11},{10,... | collective-permute-start | bytes 98312 | tf_op jit(solution)/shard_map/ppermute | solution.py:490
  4.6 3.3 %collective-permute-start.2 = (bf16[128,128]{1,0:T(8,128)(2,1)S(1)}, bf16[128,128]{1,0:T(8,128)(2,1)S(1)}, u32[]{:S(2)}, u32[]{:S(2)}) collective-permute-start(bf16[128,128]{1,0:T(8,128)(2,1)S(1)} %get-tuple-element.37), channel_id=1, source_target_pairs={{0,3},{1,2},{2,1},{3,0},{4,7},{5,6},{6,5},{7,4},{8,11},{9,10},{10,... | collective-permute-start | bytes 98312 | tf_op jit(solution)/shard_map/ppermute | solution.py:490
  8.0 6.6 %collective-permute-start.8 = (bf16[4,64,128]{2,1,0:T(8,128)(2,1)S(1)}, bf16[4,64,128]{2,1,0:T(8,128)(2,1)S(1)}, u32[]{:S(2)}, u32[]{:S(2)}) collective-permute-start(bf16[4,64,128]{2,1,0:T(8,128)(2,1)S(1)} %pad_maximum_fusion.refs_3_), channel_id=1, source_target_pairs={{0,24},{4,28},{8,16},{12,20},{16,8},{20,12},{24,0},{28,4},{1,25},{... | collective-permute-start | bytes 196616 | tf_op jit(solution)/shard_map/ppermute | solution.py:496
  11.7 5.9 %collective-permute-start.6 = (bf16[4,64,128]{2,1,0:T(8,128)(2,1)S(1)}, bf16[4,64,128]{2,1,0:T(8,128)(2,1)S(1)}, u32[]{:S(2)}, u32[]{:S(2)}) collective-permute-start(bf16[4,64,128]{2,1,0:T(8,128)(2,1)S(1)} %pad_maximum_fusion.refs_3_), channel_id=1, source_target_pairs={{0,16},{4,20},{8,24},{12,28},{16,0},{20,4},{24,8},{28,12},{1,17},{... | collective-permute-start | bytes 196616 | tf_op jit(solution)/shard_map/ppermute | solution.py:496
  11.7 7.4 %collective-permute-start.4 = (bf16[4,64,128]{2,1,0:T(8,128)(2,1)S(1)}, bf16[4,64,128]{2,1,0:T(8,128)(2,1)S(1)}, u32[]{:S(2)}, u32[]{:S(2)}) collective-permute-start(bf16[4,64,128]{2,1,0:T(8,128)(2,1)S(1)} %pad_maximum_fusion.refs_3_), channel_id=1, source_target_pairs={{0,8},{4,12},{8,0},{12,4},{16,24},{20,28},{24,16},{28,20},{1,9},{5... | collective-permute-start | bytes 196616 | tf_op jit(solution)/shard_map/ppermute | solution.py:496
  12.5 9.9 %collective-permute-start.3 = (bf16[4,64,128]{2,1,0:T(8,128)(2,1)S(1)}, bf16[4,64,128]{2,1,0:T(8,128)(2,1)S(1)}, u32[]{:S(2)}, u32[]{:S(2)}) collective-permute-start(bf16[4,64,128]{2,1,0:T(8,128)(2,1)S(1)} %pad_maximum_fusion.refs_3_), channel_id=1, source_target_pairs={{0,4},{4,0},{8,12},{12,8},{16,20},{20,16},{24,28},{28,24},{1,5},{5... | collective-permute-start | bytes 196616 | tf_op jit(solution)/shard_map/ppermute | solution.py:500
  14.0 5.6 %collective-permute-start.10 = (bf16[4,64,128]{2,1,0:T(8,128)(2,1)S(1)}, bf16[4,64,128]{2,1,0:T(8,128)(2,1)S(1)}, u32[]{:S(2)}, u32[]{:S(2)}) collective-permute-start(bf16[4,64,128]{2,1,0:T(8,128)(2,1)S(1)} %pad_maximum_fusion.1), channel_id=1, source_target_pairs={{0,4},{4,0},{8,12},{12,8},{16,20},{20,16},{24,28},{28,24},{1,5},{5... | collective-permute-start | bytes 196616 | tf_op jit(solution)/shard_map/ppermute | solution.py:500
  14.6 7.8 %collective-permute-start.9 = (bf16[4,64,128]{2,1,0:T(8,128)(2,1)S(1)}, bf16[4,64,128]{2,1,0:T(8,128)(2,1)S(1)}, u32[]{:S(2)}, u32[]{:S(2)}) collective-permute-start(bf16[4,64,128]{2,1,0:T(8,128)(2,1)S(1)} %collective-permute-done.8.refs_9_), channel_id=1, source_target_pairs={{0,4},{4,0},{8,12},{12,8},{16,20},{20,16},{24,28},{28,24},{1,5},{5... | collective-permute-start | bytes 196616 | tf_op jit(solution)/shard_map/ppermute | solution.py:500
  17.6 6.5 %collective-permute-start.7 = (bf16[4,64,128]{2,1,0:T(8,128)(2,1)S(1)}, bf16[4,64,128]{2,1,0:T(8,128)(2,1)S(1)}, u32[]{:S(2)}, u32[]{:S(2)}) collective-permute-start(bf16[4,64,128]{2,1,0:T(8,128)(2,1)S(1)} %collective-permute-done.6.refs_7_), channel_id=1, source_target_pairs={{0,4},{4,0},{8,12},{12,8},{16,20},{20,16},{24,28},{28,24},{1,5},{5... | collective-permute-start | bytes 196616 | tf_op jit(solution)/shard_map/ppermute | solution.py:500
  19.1 5.0 %collective-permute-start.5 = (bf16[4,64,128]{2,1,0:T(8,128)(2,1)S(1)}, bf16[4,64,128]{2,1,0:T(8,128)(2,1)S(1)}, u32[]{:S(2)}, u32[]{:S(2)}) collective-permute-start(bf16[4,64,128]{2,1,0:T(8,128)(2,1)S(1)} %collective-permute-done.4.refs_5_), channel_id=1, source_target_pairs={{0,4},{4,0},{8,12},{12,8},{16,20},{20,16},{24,28},{28,24},{1,5},{5... | collective-permute-start | bytes 196616 | tf_op jit(solution)/shard_map/ppermute | solution.py:500
  19.6 12.0 %collective-permute-start.13 = (bf16[8,64,128]{2,1,0:T(8,128)(2,1)S(1)}, bf16[8,64,128]{2,1,0:T(8,128)(2,1)S(1)}, u32[]{:S(2)}, u32[]{:S(2)}) collective-permute-start(bf16[8,64,128]{2,1,0:T(8,128)(2,1)S(1)} %constant_dynamic-update-slice_fusion.refs_4_), channel_id=1, source_target_pairs={{0,24},{4,28},{8,16},{12,20},{16,8},{20,12},{24,0},{28,4},{1,25},{... | collective-permute-start | bytes 393224 | tf_op jit(solution)/shard_map/ppermute | solution.py:496
  22.4 10.6 %collective-permute-start.12 = (bf16[8,64,128]{2,1,0:T(8,128)(2,1)S(1)}, bf16[8,64,128]{2,1,0:T(8,128)(2,1)S(1)}, u32[]{:S(2)}, u32[]{:S(2)}) collective-permute-start(bf16[8,64,128]{2,1,0:T(8,128)(2,1)S(1)} %constant_dynamic-update-slice_fusion.refs_4_), channel_id=1, source_target_pairs={{0,16},{4,20},{8,24},{12,28},{16,0},{20,4},{24,8},{28,12},{1,17},{... | collective-permute-start | bytes 393224 | tf_op jit(solution)/shard_map/ppermute | solution.py:496
  22.4 10.6 %collective-permute-start.11 = (bf16[8,64,128]{2,1,0:T(8,128)(2,1)S(1)}, bf16[8,64,128]{2,1,0:T(8,128)(2,1)S(1)}, u32[]{:S(2)}, u32[]{:S(2)}) collective-permute-start(bf16[8,64,128]{2,1,0:T(8,128)(2,1)S(1)} %constant_dynamic-update-slice_fusion.refs_4_), channel_id=1, source_target_pairs={{0,8},{4,12},{8,0},{12,4},{16,24},{20,28},{24,16},{28,20},{1,9},{5... | collective-permute-start | bytes 393224 | tf_op jit(solution)/shard_map/ppermute | solution.py:496
  30.0 10.5 %collective-permute-start.18 = (bf16[4,4,64,128]{3,2,1,0:T(8,128)(2,1)S(1)}, bf16[4,4,64,128]{3,2,1,0:T(8,128)(2,1)S(1)}, u32[]{:S(2)}, u32[]{:S(2)}) collective-permute-start(bf16[4,4,64,128]{3,2,1,0:T(8,128)(2,1)S(1)} %get-tuple-element.44), channel_id=1, source_target_pairs={{0,4},{4,0},{8,12},{12,8},{16,20},{20,16},{24,28},{28,24},{1,5},{5... | collective-permute-start | bytes 786440 | tf_op jit(solution)/shard_map/ppermute | solution.py:531
  39.2 7.0 %collective-permute-start.14 = (bf16[4,4,64,128]{3,2,1,0:T(8,128)(2,1)S(1)}, bf16[4,4,64,128]{3,2,1,0:T(8,128)(2,1)S(1)}, u32[]{:S(2)}, u32[]{:S(2)}) collective-permute-start(bf16[4,4,64,128]{3,2,1,0:T(8,128)(2,1)S(1)} %get-tuple-element.42), channel_id=1, source_target_pairs={{0,4},{4,0},{8,12},{12,8},{16,20},{20,16},{24,28},{28,24},{1,5},{5... | collective-permute-start | bytes 786440 | tf_op jit(solution)/shard_map/ppermute | solution.py:541
  40.6 7.6 %collective-permute-start.21 = (bf16[4,64,128]{2,1,0:T(8,128)(2,1)S(1)}, bf16[4,64,128]{2,1,0:T(8,128)(2,1)S(1)}, u32[]{:S(2)}, u32[]{:S(2)}) collective-permute-start(bf16[4,64,128]{2,1,0:T(8,128)(2,1)S(1)} %get-tuple-element.62), channel_id=1, source_target_pairs={{0,24},{4,28},{8,16},{12,20},{16,8},{20,12},{24,0},{28,4},{1,25},{... | collective-permute-start | bytes 196616 | tf_op jit(solution)/shard_map/ppermute | solution.py:549
  43.0 10.3 %collective-permute-start.20 = (bf16[4,64,128]{2,1,0:T(8,128)(2,1)S(1)}, bf16[4,64,128]{2,1,0:T(8,128)(2,1)S(1)}, u32[]{:S(2)}, u32[]{:S(2)}) collective-permute-start(bf16[4,64,128]{2,1,0:T(8,128)(2,1)S(1)} %get-tuple-element.63), channel_id=1, source_target_pairs={{0,16},{4,20},{8,24},{12,28},{16,0},{20,4},{24,8},{28,12},{1,17},{... | collective-permute-start | bytes 196616 | tf_op jit(solution)/shard_map/ppermute | solution.py:549
  43.0 10.3 %collective-permute-start.19 = (bf16[4,64,128]{2,1,0:T(8,128)(2,1)S(1)}, bf16[4,64,128]{2,1,0:T(8,128)(2,1)S(1)}, u32[]{:S(2)}, u32[]{:S(2)}) collective-permute-start(bf16[4,64,128]{2,1,0:T(8,128)(2,1)S(1)} %get-tuple-element.64), channel_id=1, source_target_pairs={{0,8},{4,12},{8,0},{12,4},{16,24},{20,28},{24,16},{28,20},{1,9},{5... | collective-permute-start | bytes 196616 | tf_op jit(solution)/shard_map/ppermute | solution.py:549
  46.3 7.0 %collective-permute-start.17 = (bf16[4,64,128]{2,1,0:T(8,128)(2,1)S(1)}, bf16[4,64,128]{2,1,0:T(8,128)(2,1)S(1)}, u32[]{:S(2)}, u32[]{:S(2)}) collective-permute-start(bf16[4,64,128]{2,1,0:T(8,128)(2,1)S(1)} %get-tuple-element.65), channel_id=1, source_target_pairs={{0,24},{4,28},{8,16},{12,20},{16,8},{20,12},{24,0},{28,4},{1,25},{... | collective-permute-start | bytes 196616 | tf_op jit(solution)/shard_map/ppermute | solution.py:549
  48.2 5.6 %collective-permute-start.16 = (bf16[4,64,128]{2,1,0:T(8,128)(2,1)S(1)}, bf16[4,64,128]{2,1,0:T(8,128)(2,1)S(1)}, u32[]{:S(2)}, u32[]{:S(2)}) collective-permute-start(bf16[4,64,128]{2,1,0:T(8,128)(2,1)S(1)} %get-tuple-element.66), channel_id=1, source_target_pairs={{0,16},{4,20},{8,24},{12,28},{16,0},{20,4},{24,8},{28,12},{1,17},{... | collective-permute-start | bytes 196616 | tf_op jit(solution)/shard_map/ppermute | solution.py:549
  48.2 5.6 %collective-permute-start.15 = (bf16[4,64,128]{2,1,0:T(8,128)(2,1)S(1)}, bf16[4,64,128]{2,1,0:T(8,128)(2,1)S(1)}, u32[]{:S(2)}, u32[]{:S(2)}) collective-permute-start(bf16[4,64,128]{2,1,0:T(8,128)(2,1)S(1)} %get-tuple-element.67), channel_id=1, source_target_pairs={{0,8},{4,12},{8,0},{12,4},{16,24},{20,28},{24,16},{28,20},{1,9},{5... | collective-permute-start | bytes 196616 | tf_op jit(solution)/shard_map/ppermute | solution.py:549
  53.9 3.4 %collective-permute-start.24 = (bf16[128,128]{1,0:T(8,128)(2,1)S(1)}, bf16[128,128]{1,0:T(8,128)(2,1)S(1)}, u32[]{:S(2)}, u32[]{:S(2)}) collective-permute-start(bf16[128,128]{1,0:T(8,128)(2,1)S(1)} %get-tuple-element.68), channel_id=1, source_target_pairs={{0,3},{1,2},{2,1},{3,0},{4,7},{5,6},{6,5},{7,4},{8,11},{9,10},{10,... | collective-permute-start | bytes 98312 | tf_op jit(solution)/shard_map/ppermute | solution.py:576
  55.0 3.9 %collective-permute-start.23 = (bf16[128,128]{1,0:T(8,128)(2,1)S(1)}, bf16[128,128]{1,0:T(8,128)(2,1)S(1)}, u32[]{:S(2)}, u32[]{:S(2)}) collective-permute-start(bf16[128,128]{1,0:T(8,128)(2,1)S(1)} %get-tuple-element.71), channel_id=1, source_target_pairs={{0,2},{1,3},{2,0},{3,1},{4,6},{5,7},{6,4},{7,5},{8,10},{9,11},{10,... | collective-permute-start | bytes 98312 | tf_op jit(solution)/shard_map/ppermute | solution.py:576
  (1 other events, 3.3 us)

commit v5 on v4

--- a/solution.py
+++ b/solution.py
@@ -302,30 +302,16 @@
     )
 
 
-def load_parts(part_refs, library, sems):
-    copies, at = [], 0
-    for part in part_refs:
-        size = part.shape[0]
-        copies.append(
-            pltpu.make_async_copy(part, library.at[pl.ds(at, size)], sems.at[len(copies)])
-        )
-        at += size
-    return copies
-
-
 def listed_spots(spots_ref, step):
     return [spots_ref[step, number] for number in range(spots_ref.shape[1])]
 
 
-def begin(step, part_refs, library, total, sems):
-    @pl.when(step == 0)
-    def _():
-        copies = load_parts(part_refs, library, sems)
-        for copy in copies:
-            copy.start()
-        total[...] = jnp.zeros_like(total)
-        for copy in copies:
-            copy.wait()
+def begin(part_refs, library, total):
+    at = 0
+    for part in part_refs:
+        library[at : at + part.shape[0]] = part[...]
+        at += part.shape[0]
+    total[...] = jnp.zeros_like(total)
 
 
 def add_terms(total, spots, terms):
@@ -333,18 +319,16 @@
         total[spot] += terms[number * BLOCK : (number + 1) * BLOCK]
 
 
-def finish(step, total, keep_ref, ship_ref):
+def finish(total, keep_ref, ship_ref):
     pairs, size = keep_ref.shape[:2]
-
-    @pl.when(step == pl.num_programs(0) - 1)
-    def _():
-        for pair in range(pairs):
-            keep_ref[pair] = total[pl.ds(2 * pair * size, size)]
-            ship_ref[pair] = total[pl.ds((2 * pair + 1) * size, size)].astype(jnp.bfloat16)
-
-
-def stacked_heads(ref, chunk):
-    return jnp.concatenate([ref[:, h * DH : (h + 1) * DH] for h in chunk], axis=0)
+    for pair in range(pairs):
+        keep_ref[pair] = total[pl.ds(2 * pair * size, size)]
+        ship_ref[pair] = total[pl.ds((2 * pair + 1) * size, size)].astype(jnp.bfloat16)
+
+
+def stacked_heads(ref, step, chunk):
+    rows = slice(step * BLOCK, (step + 1) * BLOCK)
+    return jnp.concatenate([ref[rows, h * DH : (h + 1) * DH] for h in chunk], axis=0)
 
 
 def chunks_of(heads, size):
@@ -354,78 +338,95 @@
 def probs_kernel(seq_count, size, *refs):
     spots_ref, query_ref, grad_ref = refs[:3]
     part_refs = refs[3 : 3 + seq_count]
-    probs_ref, rows_ref, keep_ref, ship_ref, library, total, sems = refs[3 + seq_count :]
-    blocks_here = part_refs[0].shape[0]
-    all_blocks = seq_count * blocks_here
-    step = pl.program_id(0)
-    begin(step, part_refs, library, total, sems)
-    block = lax.axis_index("seq") * blocks_here + step
-    spots = listed_spots(spots_ref, step)
-    for number, spot in enumerate(spots):
-        rows_ref[0, pl.ds(number * BLOCK, BLOCK), :] = library[spot]
-    first_bias = jnp.where(block == 0, NEG_FILL, 0.0)
-    last_bias = jnp.where(block == all_blocks - 1, NEG_FILL, 0.0)
-    scale = DH ** (-0.5) * math.log2(math.e)
-    terms = 0.0
-    for chunk in chunks_of(query_ref.shape[1] // DH, size):
-        query = stacked_heads(query_ref, chunk)
-        grad = stacked_heads(grad_ref, chunk)
-        scores = dot(rows_ref[0], query, 1, 1)
-        scores = jnp.concatenate(
-            [
-                scores[:BLOCK] + first_bias,
-                scores[BLOCK : 2 * BLOCK],
-                scores[2 * BLOCK : 3 * BLOCK] + last_bias,
-                scores[3 * BLOCK :],
-            ],
-            axis=0,
-        )
-        peak = jnp.max(scores, axis=0, keepdims=True)
-        weights = jnp.exp2((scores - peak) * scale)
-        probs = weights * (1.0 / jnp.sum(weights, axis=0, keepdims=True))
-        probs16 = probs.astype(jnp.bfloat16)
-        probs_ref[0, :, chunk[0] * BLOCK : (chunk[-1] + 1) * BLOCK] = probs16
-        terms = terms + dot(probs16, grad, 1, 0)
-    add_terms(total, spots, terms)
-    finish(step, total, keep_ref, ship_ref)
+    probs_ref, rows_ref, keep_ref, ship_ref, library, total = refs[3 + seq_count :]
+    blocks_here = probs_ref.shape[0]
+    all_blocks = library.shape[0]
+    begin(part_refs, library, total)
+    for step in range(blocks_here):
+        block = lax.axis_index("seq") * blocks_here + step
+        spots = listed_spots(spots_ref, step)
+        for number, spot in enumerate(spots):
+            rows_ref[step, pl.ds(number * BLOCK, BLOCK), :] = library[spot]
+        first_bias = jnp.where(block == 0, NEG_FILL, 0.0)
+        last_bias = jnp.where(block == all_blocks - 1, NEG_FILL, 0.0)
+        scale = DH ** (-0.5) * math.log2(math.e)
+        terms = 0.0
+        for chunk in chunks_of(query_ref.shape[1] // DH, size):
+            query = stacked_heads(query_ref, step, chunk)
+            grad = stacked_heads(grad_ref, step, chunk)
+            scores = dot(rows_ref[step], query, 1, 1)
+            scores = jnp.concatenate(
+                [
+                    scores[:BLOCK] + first_bias,
+                    scores[BLOCK : 2 * BLOCK],
+                    scores[2 * BLOCK : 3 * BLOCK] + last_bias,
+                    scores[3 * BLOCK :],
+                ],
+                axis=0,
+            )
+            peak = jnp.max(scores, axis=0, keepdims=True)
+            weights = jnp.exp2((scores - peak) * scale)
+            probs = weights * (1.0 / jnp.sum(weights, axis=0, keepdims=True))
+            probs16 = probs.astype(jnp.bfloat16)
+            probs_ref[step, :, chunk[0] * BLOCK : (chunk[-1] + 1) * BLOCK] = probs16
+            terms = terms + dot(probs16, grad, 1, 0)
+        add_terms(total, spots, terms)
+    finish(total, keep_ref, ship_ref)
+
+
+def send_tile(stage, out_ref, step, sems):
+    rows = pl.ds(step * BLOCK, BLOCK)
+    copy = pltpu.make_async_copy(stage.at[step], out_ref.at[rows], sems.at[step])
+    copy.start()
+    return copy
 
 
 def dscores_kernel(size, *refs):
     spots_ref, query_ref, grad_ref, probs_ref = refs[:4]
-    part_refs, refs = refs[4:-8], refs[-8:]
-    out_ref, dscores_ref, keep_ref, ship_ref, library, total, rows_ref, sems = refs
-    step = pl.program_id(0)
-    begin(step, part_refs, library, total, sems)
-    spots = listed_spots(spots_ref, step)
-    for number, spot in enumerate(spots):
-        rows_ref[pl.ds(number * BLOCK, BLOCK), :] = library[spot]
-    terms = 0.0
-    for chunk in chunks_of(query_ref.shape[1] // DH, size):
-        columns = slice(chunk[0] * BLOCK, (chunk[-1] + 1) * BLOCK)
-        query = stacked_heads(query_ref, chunk)
-        grad = stacked_heads(grad_ref, chunk)
-        probs16 = probs_ref[0, :, columns]
-        result = dot(rows_ref[...], probs16, 0, 0).astype(jnp.bfloat16).astype(jnp.float32)
-        grad_across = jnp.transpose(grad.astype(jnp.float32))
-        delta = jnp.sum(grad_across * result, axis=0, keepdims=True)
-        dprobs = dot(rows_ref[...], grad, 1, 1)
-        dscores = (probs16.astype(jnp.float32) * (dprobs - delta)).astype(jnp.bfloat16)
-        dscores_ref[0, :, columns] = dscores
-        terms = terms + dot(dscores, query, 1, 0)
-        down = jnp.transpose(result).astype(jnp.bfloat16)
-        for number, h in enumerate(chunk):
-            out_ref[:, h * DH : (h + 1) * DH] = down[number * BLOCK : (number + 1) * BLOCK]
-    add_terms(total, spots, terms * DH ** (-0.5))
-    finish(step, total, keep_ref, ship_ref)
-
-
-def dquery_kernel(size, dscores_ref, rows_ref, dquery_ref):
-    for chunk in chunks_of(dquery_ref.shape[1] // DH, size):
-        columns = slice(chunk[0] * BLOCK, (chunk[-1] + 1) * BLOCK)
-        across = dot(rows_ref[0], dscores_ref[0, :, columns], 0, 0) * DH ** (-0.5)
-        down = jnp.transpose(across).astype(jnp.bfloat16)
-        for number, h in enumerate(chunk):
-            dquery_ref[:, h * DH : (h + 1) * DH] = down[number * BLOCK : (number + 1) * BLOCK]
+    part_refs, refs = refs[4:-9], refs[-9:]
+    out_ref, dscores_ref, keep_ref, ship_ref, library, total, rows_ref, stage, sems = refs
+    begin(part_refs, library, total)
+    copies = []
+    for step in range(stage.shape[0]):
+        spots = listed_spots(spots_ref, step)
+        for number, spot in enumerate(spots):
+            rows_ref[step, pl.ds(number * BLOCK, BLOCK), :] = library[spot]
+        terms = 0.0
+        for chunk in chunks_of(query_ref.shape[1] // DH, size):
+            columns = slice(chunk[0] * BLOCK, (chunk[-1] + 1) * BLOCK)
+            query = stacked_heads(query_ref, step, chunk)
+            grad = stacked_heads(grad_ref, step, chunk)
+            probs16 = probs_ref[step, :, columns]
+            result = dot(rows_ref[step], probs16, 0, 0).astype(jnp.bfloat16).astype(jnp.float32)
+            grad_across = jnp.transpose(grad.astype(jnp.float32))
+            delta = jnp.sum(grad_across * result, axis=0, keepdims=True)
+            dprobs = dot(rows_ref[step], grad, 1, 1)
+            dscores = (probs16.astype(jnp.float32) * (dprobs - delta)).astype(jnp.bfloat16)
+            dscores_ref[step, :, columns] = dscores
+            terms = terms + dot(dscores, query, 1, 0)
+            down = jnp.transpose(result).astype(jnp.bfloat16)
+            for number, h in enumerate(chunk):
+                stage[step, :, h * DH : (h + 1) * DH] = down[number * BLOCK : (number + 1) * BLOCK]
+        add_terms(total, spots, terms * DH ** (-0.5))
+        copies.append(send_tile(stage, out_ref, step, sems))
+    finish(total, keep_ref, ship_ref)
+    for copy in copies:
+        copy.wait()
+
+
+def dquery_kernel(size, dscores_ref, rows_ref, dquery_ref, stage, sems):
+    copies = []
+    for step in range(stage.shape[0]):
+        for chunk in chunks_of(dquery_ref.shape[1] // DH, size):
+            columns = slice(chunk[0] * BLOCK, (chunk[-1] + 1) * BLOCK)
+            across = dot(rows_ref[step], dscores_ref[step, :, columns], 0, 0) * DH ** (-0.5)
+            down = jnp.transpose(across).astype(jnp.bfloat16)
+            for number, h in enumerate(chunk):
+                rows = slice(number * BLOCK, (number + 1) * BLOCK)
+                stage[step, :, h * DH : (h + 1) * DH] = down[rows]
+        copies.append(send_tile(stage, dquery_ref, step, sems))
+    for copy in copies:
+        copy.wait()
 
 
 def small_grant():
@@ -434,7 +435,7 @@
 
 def kernel_options(products, pairs):
     return {
-        "compiler_params": pltpu.CompilerParams(vmem_limit_bytes=40 * 1024 * 1024),
+        "compiler_params": pltpu.CompilerParams(vmem_limit_bytes=36 * 1024 * 1024),
         "cost_estimate": pl.CostEstimate(
             flops=4 * products * pairs * DH, bytes_accessed=4 * pairs, transcendentals=pairs
         ),
@@ -506,36 +507,33 @@
     value_pair, _ = lax.optimization_barrier((value_pair, key_far[1:]))
     value_parts = along_far(value_pair)
 
-    tile = pl.BlockSpec((BLOCK, width), lambda i: (i, 0))
-    square = pl.BlockSpec((1, listed, columns), lambda i: (i, 0, 0))
-    listing = pl.BlockSpec((1, listed, DH), lambda i: (i, 0, 0))
+    lists = pltpu.VMEM((blocks_here, listed, DH), jnp.bfloat16)
+    stage = pltpu.VMEM((blocks_here, BLOCK, width), jnp.bfloat16)
+    tile_sems = pltpu.SemaphoreType.DMA((blocks_here,))
+    vmem = pl.BlockSpec(memory_space=pltpu.VMEM)
     half = (pair_count, blocks_here, BLOCK, DH)
-    whole = pl.BlockSpec(half, lambda i: (0, 0, 0, 0))
     square_shape = jax.ShapeDtypeStruct((blocks_here, listed, columns), jnp.bfloat16)
     listing_shape = jax.ShapeDtypeStruct((blocks_here, listed, DH), jnp.bfloat16)
     keep_shape = jax.ShapeDtypeStruct(half, jnp.float32)
     ship_shape = jax.ShapeDtypeStruct(half, jnp.bfloat16)
     library = pltpu.VMEM((seq_count * blocks_here, BLOCK, DH), jnp.bfloat16)
     total = pltpu.VMEM((seq_count * blocks_here, BLOCK, DH), jnp.float32)
-    sems = pltpu.SemaphoreType.DMA((seq_count,))
 
     probs, key_lists, value_keep, value_ship = pl.pallas_call(
         lambda *refs: probs_kernel(seq_count, size, *refs),
-        grid=(blocks_here,),
-        in_specs=[smem, tile, tile] + [anywhere] * len(key_parts),
-        out_specs=[square, listing, whole, whole],
+        in_specs=[smem, vmem, vmem] + [vmem] * len(key_parts),
+        out_specs=[vmem] * 4,
         out_shape=[square_shape, listing_shape, keep_shape, ship_shape],
-        scratch_shapes=[library, total, sems],
+        scratch_shapes=[library, total],
         **kernel_options(2, pairs),
     )(spots, query_here, grad_here, *key_parts)
     value_near = lax.ppermute(value_ship, "seq", flips(seq_count, 1))
     attn_out, dscores, key_keep, key_ship = pl.pallas_call(
         lambda *refs: dscores_kernel(size, *refs),
-        grid=(blocks_here,),
-        in_specs=[smem, tile, tile, square] + [anywhere] * len(value_parts),
-        out_specs=[tile, square, whole, whole],
+        in_specs=[smem, vmem, vmem, vmem] + [vmem] * len(value_parts),
+        out_specs=[anywhere, vmem, vmem, vmem],
         out_shape=[tile_shape, square_shape, keep_shape, ship_shape],
-        scratch_shapes=[library, total, pltpu.VMEM((listed, DH), jnp.bfloat16), sems],
+        scratch_shapes=[library, total, lists, stage, tile_sems],
         **kernel_options(3, pairs),
     )(spots, query_here, grad_here, probs, *value_parts)
     key_near = lax.ppermute(key_ship, "seq", flips(seq_count, 1))
@@ -561,10 +559,10 @@
     value_far = from_far(value_sums)
     d_queries = pl.pallas_call(
         lambda *refs: dquery_kernel(size, *refs),
-        grid=(blocks_here,),
-        in_specs=[square, listing],
-        out_specs=tile,
+        in_specs=[vmem, vmem],
+        out_specs=anywhere,
         out_shape=tile_shape,
+        scratch_shapes=[stage, tile_sems],
         **kernel_options(1, pairs),
     )(*lax.optimization_barrier((dscores, key_lists, key_sums))[:2])
 

time: 59.8 us -> 58.1 us (0.972)
  Pallas kernels: 18 us -> 13.9 us
  waiting for transfers between devices: 8.69 us -> 11.1 us
    pallas_call x3, Pallas kernels: 14.6 us -> 10.4 us  [the longest x1 4.55 us: whole_body(): pl.pallas_call(lambda *refs: probs_kernel(seq_count, size, *refs), in_spe...]
    ppermute x6, waiting for transfers between devices: 2.83 us -> 4.21 us  [along_far(): parts.append(lax.ppermute(own, 'seq', flips(seq_count, k)))]
    ppermute x6, waiting for transfers between devices: 0.55 us -> 1.55 us  [from_far(): lax.ppermute(sums[pair - 1], 'seq', flips(seq_count, 2 * pair))]
  transfers between devices with their start and end apart: 25 -> 25, of which waited for: 7 -> 8; matrix products, arithmetic and copies ran while one was open for 0% -> 0% of each run, Pallas kernels for 28% -> 21%
where the time goes in v5:
time: 58.1 us; the launch traced here: 57.9 us
  starting transfers between devices  31.8 us (55%)
  Pallas kernels  13.9 us (24%)
  waiting for transfers between devices  11.1 us (19%)
  between operations  0.8 us (1%)
    ppermute x6, starting transfers between devices, from_far(): lax.ppermute(sums[pair - 1], 'seq', flips(seq_count, 2 * pair))  8.91 us
    ppermute x6, starting transfers between devices, along_far(): parts.append(lax.ppermute(own, 'seq', flips(seq_count, k)))  8.9 us
    ppermute x5, starting transfers between devices, to_near(): return lax.ppermute(part, 'seq', flips(seq_count, 1))  5.7 us
    pallas_call x1, Pallas kernels, whole_body(): pl.pallas_call(lambda *refs: probs_kernel(seq_count, size, *refs), in_spe...  4.55 us
    pallas_call x1, Pallas kernels, whole_body(): pl.pallas_call(lambda *refs: dscores_kernel(size, *refs), in_specs=[smem,...  4.37 us
    ppermute x6, waiting for transfers between devices, along_far(): parts.append(lax.ppermute(own, 'seq', flips(seq_count, k)))  4.21 us
    ppermute x3, starting transfers between devices, whole_body(): lax.ppermute(pieces[k], 'head', flips(head_count, k))  3.15 us
    ppermute x3, waiting for transfers between devices, whole_body(): lax.ppermute(packed[k], 'head', flips(head_count, k))  2.79 us
  transfers between devices with their start and end apart: 25, of which 8 were waited for; matrix products, arithmetic and copies ran while one was open for 0% of the time, Pallas kernels for 21%

profile of v5, /device:TPU:0, one launch (start us, length us, event | category | flops | bytes accessed | tf_op | source)
XLA Modules:
  0.0 57.9 jit_solution(17865840839937718198)
XLA Ops:
  2.1 2.6 %collective-permute-start.1 = (bf16[128,128]{1,0:T(8,128)(2,1)S(1)}, bf16[128,128]{1,0:T(8,128)(2,1)S(1)}, u32[]{:S(2)}, u32[]{:S(2)}) collective-permute-start(bf16[128,128]{1,0:T(8,128)(2,1)S(1)} %get-tuple-element.36), channel_id=1, source_target_pairs={{0,2},{1,3},{2,0},{3,1},{4,6},{5,7},{6,4},{7,5},{8,10},{9,11},{10,... | collective-permute-start | bytes 98312 | tf_op jit(solution)/shard_map/ppermute | solution.py:491
  4.7 1.9 %shard_map.93 = (s32[4,13]{1,0:T(4,128)S(1)}, bf16[256,1024]{1,0:T(8,128)(2,1)S(1)}, bf16[256,1024]{1,0:T(8,128)(2,1)S(1)}) custom-call(s32[4,8]{1,0:T(4,128)} %refs_0_.2, s32[2]{0:T(128)} %refs_1_.2, bf16[256,1024]{1,0:T(8,128)(2,1)} %refs_2_.1, bf16[256,1024]{1,0:T(8,128)(2,1)} %refs_3_.1), custom_call_target="tpu_custom_call" | custom-call | bytes 2097152 | tf_op jit(solution)/shard_map/pallas_call | solution.py:475
  6.6 1.4 %collective-permute-done.2 = bf16[128,128]{1,0:T(8,128)(2,1)S(1)} collective-permute-done((bf16[128,128]{1,0:T(8,128)(2,1)S(1)}, bf16[128,128]{1,0:T(8,128)(2,1)S(1)}, u32[]{:S(2)}, u32[]{:S(2)}) %collective-permute-start.2) | collective-permute-done | bytes 32800 | tf_op jit(solution)/shard_map/ppermute | solution.py:491
  8.0 3.7 %collective-permute-start.8 = (bf16[4,64,128]{2,1,0:T(8,128)(2,1)S(1)}, bf16[4,64,128]{2,1,0:T(8,128)(2,1)S(1)}, u32[]{:S(2)}, u32[]{:S(2)}) collective-permute-start(bf16[4,64,128]{2,1,0:T(8,128)(2,1)S(1)} %pad_maximum_fusion.refs_3_), channel_id=1, source_target_pairs={{0,24},{4,28},{8,16},{12,20},{16,8},{20,12},{24,0},{28,4},{1,25},{... | collective-permute-start | bytes 196616 | tf_op jit(solution)/shard_map/ppermute | solution.py:497
  12.5 1.5 %collective-permute-start.3 = (bf16[4,64,128]{2,1,0:T(8,128)(2,1)S(1)}, bf16[4,64,128]{2,1,0:T(8,128)(2,1)S(1)}, u32[]{:S(2)}, u32[]{:S(2)}) collective-permute-start(bf16[4,64,128]{2,1,0:T(8,128)(2,1)S(1)} %pad_maximum_fusion.refs_3_), channel_id=1, source_target_pairs={{0,4},{4,0},{8,12},{12,8},{16,20},{20,16},{24,28},{28,24},{1,5},{5... | collective-permute-start | bytes 196616 | tf_op jit(solution)/shard_map/ppermute | solution.py:501
  14.6 1.6 %collective-permute-start.9 = (bf16[4,64,128]{2,1,0:T(8,128)(2,1)S(1)}, bf16[4,64,128]{2,1,0:T(8,128)(2,1)S(1)}, u32[]{:S(2)}, u32[]{:S(2)}) collective-permute-start(bf16[4,64,128]{2,1,0:T(8,128)(2,1)S(1)} %collective-permute-done.8.refs_9_), channel_id=1, source_target_pairs={{0,4},{4,0},{8,12},{12,8},{16,20},{20,16},{24,28},{28,24},{1,5},{5... | collective-permute-start | bytes 196616 | tf_op jit(solution)/shard_map/ppermute | solution.py:501
  16.2 1.4 %collective-permute-done.6.refs_7_ = bf16[4,64,128]{2,1,0:T(8,128)(2,1)S(1)} collective-permute-done((bf16[4,64,128]{2,1,0:T(8,128)(2,1)S(1)}, bf16[4,64,128]{2,1,0:T(8,128)(2,1)S(1)}, u32[]{:S(2)}, u32[]{:S(2)}) %collective-permute-start.6) | collective-permute-done | bytes 65568 | tf_op jit(solution)/shard_map/ppermute | solution.py:497
  17.6 1.5 %collective-permute-start.7 = (bf16[4,64,128]{2,1,0:T(8,128)(2,1)S(1)}, bf16[4,64,128]{2,1,0:T(8,128)(2,1)S(1)}, u32[]{:S(2)}, u32[]{:S(2)}) collective-permute-start(bf16[4,64,128]{2,1,0:T(8,128)(2,1)S(1)} %collective-permute-done.6.refs_7_), channel_id=1, source_target_pairs={{0,4},{4,0},{8,12},{12,8},{16,20},{20,16},{24,28},{28,24},{1,5},{5... | collective-permute-start | bytes 196616 | tf_op jit(solution)/shard_map/ppermute | solution.py:501
  19.6 2.8 %collective-permute-start.13 = (bf16[8,64,128]{2,1,0:T(8,128)(2,1)S(1)}, bf16[8,64,128]{2,1,0:T(8,128)(2,1)S(1)}, u32[]{:S(2)}, u32[]{:S(2)}) collective-permute-start(bf16[8,64,128]{2,1,0:T(8,128)(2,1)S(1)} %constant_dynamic-update-slice_fusion.refs_4_), channel_id=1, source_target_pairs={{0,24},{4,28},{8,16},{12,20},{16,8},{20,12},{24,0},{28,4},{1,25},{... | collective-permute-start | bytes 393224 | tf_op jit(solution)/shard_map/ppermute | solution.py:497
  22.4 1.7 %collective-permute-start.11 = (bf16[8,64,128]{2,1,0:T(8,128)(2,1)S(1)}, bf16[8,64,128]{2,1,0:T(8,128)(2,1)S(1)}, u32[]{:S(2)}, u32[]{:S(2)}) collective-permute-start(bf16[8,64,128]{2,1,0:T(8,128)(2,1)S(1)} %constant_dynamic-update-slice_fusion.refs_4_), channel_id=1, source_target_pairs={{0,8},{4,12},{8,0},{12,4},{16,24},{20,28},{24,16},{28,20},{1,9},{5... | collective-permute-start | bytes 393224 | tf_op jit(solution)/shard_map/ppermute | solution.py:497
  24.1 4.5 %shard_map.95 = (bf16[4,832,512]{2,1,0:T(8,128)(2,1)S(1)}, bf16[4,832,128]{2,1,0:T(8,128)(2,1)S(1)}, f32[4,4,64,128]{3,2,1,0:T(8,128)S(1)}, bf16[4,4,64,128]{3,2,1,0:T(8,128)(2,1)S(1)}) custom-call(s32[4,13]{1,0:T(4,128)S(1)} %get-tuple-element.31.refs_0_, bf16[256,1024]{1,0:T(8,128)(2,1)S(1)} %get-tuple-element.32.refs_1_, ...), custom_call_target="tpu_custom_call" | custom-call | flops 1744830464 | bytes 6815744 | tf_op jit(solution)/shard_map/pallas_call | solution.py:522
  28.6 1.6 %collective-permute-start.18 = (bf16[4,4,64,128]{3,2,1,0:T(8,128)(2,1)S(1)}, bf16[4,4,64,128]{3,2,1,0:T(8,128)(2,1)S(1)}, u32[]{:S(2)}, u32[]{:S(2)}) collective-permute-start(bf16[4,4,64,128]{3,2,1,0:T(8,128)(2,1)S(1)} %get-tuple-element.44), channel_id=1, source_target_pairs={{0,4},{4,0},{8,12},{12,8},{16,20},{20,16},{24,28},{28,24},{1,5},{5... | collective-permute-start | bytes 786440 | tf_op jit(solution)/shard_map/ppermute | solution.py:530
  30.2 2.8 %collective-permute-done.12.refs_6_ = bf16[8,64,128]{2,1,0:T(8,128)(2,1)S(1)} collective-permute-done((bf16[8,64,128]{2,1,0:T(8,128)(2,1)S(1)}, bf16[8,64,128]{2,1,0:T(8,128)(2,1)S(1)}, u32[]{:S(2)}, u32[]{:S(2)}) %collective-permute-start.12) | collective-permute-done | bytes 131104 | tf_op jit(solution)/shard_map/ppermute | solution.py:497
  33.0 4.4 %shard_map.96 = (bf16[256,1024]{1,0:T(8,128)(2,1)}, bf16[4,832,512]{2,1,0:T(8,128)(2,1)S(1)}, f32[4,4,64,128]{3,2,1,0:T(8,128)S(1)}, bf16[4,4,64,128]{3,2,1,0:T(8,128)(2,1)S(1)}) custom-call(s32[4,13]{1,0:T(4,128)S(1)} %get-tuple-element.31.refs_0_, bf16[256,1024]{1,0:T(8,128)(2,1)S(1)} %get-tuple-element.32.refs_1_, ...), custom_call_target="tpu_custom_call" | custom-call | flops 2617245696 | bytes 6815744 | tf_op jit(solution)/shard_map/pallas_call | solution.py:531
  37.4 1.3 %collective-permute-start.14 = (bf16[4,4,64,128]{3,2,1,0:T(8,128)(2,1)S(1)}, bf16[4,4,64,128]{3,2,1,0:T(8,128)(2,1)S(1)}, u32[]{:S(2)}, u32[]{:S(2)}) collective-permute-start(bf16[4,4,64,128]{3,2,1,0:T(8,128)(2,1)S(1)} %get-tuple-element.42), channel_id=1, source_target_pairs={{0,4},{4,0},{8,12},{12,8},{16,20},{20,16},{24,28},{28,24},{1,5},{5... | collective-permute-start | bytes 786440 | tf_op jit(solution)/shard_map/ppermute | solution.py:539
  38.9 2.4 %collective-permute-start.21 = (bf16[4,64,128]{2,1,0:T(8,128)(2,1)S(1)}, bf16[4,64,128]{2,1,0:T(8,128)(2,1)S(1)}, u32[]{:S(2)}, u32[]{:S(2)}) collective-permute-start(bf16[4,64,128]{2,1,0:T(8,128)(2,1)S(1)} %get-tuple-element.62), channel_id=1, source_target_pairs={{0,24},{4,28},{8,16},{12,20},{16,8},{20,12},{24,0},{28,4},{1,25},{... | collective-permute-start | bytes 196616 | tf_op jit(solution)/shard_map/ppermute | solution.py:547
  41.3 2.0 %collective-permute-start.19 = (bf16[4,64,128]{2,1,0:T(8,128)(2,1)S(1)}, bf16[4,64,128]{2,1,0:T(8,128)(2,1)S(1)}, u32[]{:S(2)}, u32[]{:S(2)}) collective-permute-start(bf16[4,64,128]{2,1,0:T(8,128)(2,1)S(1)} %get-tuple-element.64), channel_id=1, source_target_pairs={{0,8},{4,12},{8,0},{12,4},{16,24},{20,28},{24,16},{28,20},{1,9},{5... | collective-permute-start | bytes 196616 | tf_op jit(solution)/shard_map/ppermute | solution.py:547
  44.6 1.9 %collective-permute-start.17 = (bf16[4,64,128]{2,1,0:T(8,128)(2,1)S(1)}, bf16[4,64,128]{2,1,0:T(8,128)(2,1)S(1)}, u32[]{:S(2)}, u32[]{:S(2)}) collective-permute-start(bf16[4,64,128]{2,1,0:T(8,128)(2,1)S(1)} %get-tuple-element.65), channel_id=1, source_target_pairs={{0,24},{4,28},{8,16},{12,20},{16,8},{20,12},{24,0},{28,4},{1,25},{... | collective-permute-start | bytes 196616 | tf_op jit(solution)/shard_map/ppermute | solution.py:547
  46.5 2.5 %collective-permute-start.15 = (bf16[4,64,128]{2,1,0:T(8,128)(2,1)S(1)}, bf16[4,64,128]{2,1,0:T(8,128)(2,1)S(1)}, u32[]{:S(2)}, u32[]{:S(2)}) collective-permute-start(bf16[4,64,128]{2,1,0:T(8,128)(2,1)S(1)} %get-tuple-element.67), channel_id=1, source_target_pairs={{0,8},{4,12},{8,0},{12,4},{16,24},{20,28},{24,16},{28,20},{1,9},{5... | collective-permute-start | bytes 196616 | tf_op jit(solution)/shard_map/ppermute | solution.py:547
  49.0 1.5 %shard_map.97 = bf16[256,1024]{1,0:T(8,128)(2,1)} custom-call(bf16[4,832,512]{2,1,0:T(8,128)(2,1)S(1)} %get-tuple-element.47.refs_0_, bf16[4,832,128]{2,1,0:T(8,128)(2,1)S(1)} %get-tuple-element.48.refs_1_), custom_call_target="tpu_custom_call" | custom-call | flops 872415232 | bytes 6815744 | tf_op jit(solution)/shard_map/pallas_call | solution.py:560
  50.7 1.4 %collective-permute-done.16 = bf16[4,64,128]{2,1,0:T(8,128)(2,1)S(1)} collective-permute-done((bf16[4,64,128]{2,1,0:T(8,128)(2,1)S(1)}, bf16[4,64,128]{2,1,0:T(8,128)(2,1)S(1)}, u32[]{:S(2)}, u32[]{:S(2)}) %collective-permute-start.16) | collective-permute-done | bytes 65568 | tf_op jit(solution)/shard_map/ppermute | solution.py:547
  53.3 1.1 %collective-permute-start.23 = (bf16[128,128]{1,0:T(8,128)(2,1)S(1)}, bf16[128,128]{1,0:T(8,128)(2,1)S(1)}, u32[]{:S(2)}, u32[]{:S(2)}) collective-permute-start(bf16[128,128]{1,0:T(8,128)(2,1)S(1)} %get-tuple-element.71), channel_id=1, source_target_pairs={{0,2},{1,3},{2,0},{3,1},{4,6},{5,7},{6,4},{7,5},{8,10},{9,11},{10,... | collective-permute-start | bytes 98312 | tf_op jit(solution)/shard_map/ppermute | solution.py:574
  54.4 1.2 %collective-permute-done.24.refs_3_ = bf16[128,128]{1,0:T(8,128)(2,1)S(1)} collective-permute-done((bf16[128,128]{1,0:T(8,128)(2,1)S(1)}, bf16[128,128]{1,0:T(8,128)(2,1)S(1)}, u32[]{:S(2)}, u32[]{:S(2)}) %collective-permute-start.24) | collective-permute-done | bytes 32800 | tf_op jit(solution)/shard_map/ppermute | solution.py:574
  55.6 1.6 %collective-permute-done.23.refs_2_ = bf16[128,128]{1,0:T(8,128)(2,1)S(1)} collective-permute-done((bf16[128,128]{1,0:T(8,128)(2,1)S(1)}, bf16[128,128]{1,0:T(8,128)(2,1)S(1)}, u32[]{:S(2)}, u32[]{:S(2)}) %collective-permute-start.23) | collective-permute-done | bytes 32800 | tf_op jit(solution)/shard_map/ppermute | solution.py:574
  (49 shorter events, 6.8 us)
Async XLA Ops:
  1.6 5.0 %collective-permute-start = (bf16[128,128]{1,0:T(8,128)(2,1)S(1)}, bf16[128,128]{1,0:T(8,128)(2,1)S(1)}, u32[]{:S(2)}, u32[]{:S(2)}) collective-permute-start(bf16[128,128]{1,0:T(8,128)(2,1)S(1)} %get-tuple-element.35), channel_id=1, source_target_pairs={{0,1},{1,0},{2,3},{3,2},{4,5},{5,4},{6,7},{7,6},{8,9},{9,8},{10,11... | collective-permute-start | bytes 98312 | tf_op jit(solution)/shard_map/ppermute | solution.py:491
  2.1 4.5 %collective-permute-start.1 = (bf16[128,128]{1,0:T(8,128)(2,1)S(1)}, bf16[128,128]{1,0:T(8,128)(2,1)S(1)}, u32[]{:S(2)}, u32[]{:S(2)}) collective-permute-start(bf16[128,128]{1,0:T(8,128)(2,1)S(1)} %get-tuple-element.36), channel_id=1, source_target_pairs={{0,2},{1,3},{2,0},{3,1},{4,6},{5,7},{6,4},{7,5},{8,10},{9,11},{10,... | collective-permute-start | bytes 98312 | tf_op jit(solution)/shard_map/ppermute | solution.py:491
  4.6 3.3 %collective-permute-start.2 = (bf16[128,128]{1,0:T(8,128)(2,1)S(1)}, bf16[128,128]{1,0:T(8,128)(2,1)S(1)}, u32[]{:S(2)}, u32[]{:S(2)}) collective-permute-start(bf16[128,128]{1,0:T(8,128)(2,1)S(1)} %get-tuple-element.37), channel_id=1, source_target_pairs={{0,3},{1,2},{2,1},{3,0},{4,7},{5,6},{6,5},{7,4},{8,11},{9,10},{10,... | collective-permute-start | bytes 98312 | tf_op jit(solution)/shard_map/ppermute | solution.py:491
  8.0 6.6 %collective-permute-start.8 = (bf16[4,64,128]{2,1,0:T(8,128)(2,1)S(1)}, bf16[4,64,128]{2,1,0:T(8,128)(2,1)S(1)}, u32[]{:S(2)}, u32[]{:S(2)}) collective-permute-start(bf16[4,64,128]{2,1,0:T(8,128)(2,1)S(1)} %pad_maximum_fusion.refs_3_), channel_id=1, source_target_pairs={{0,24},{4,28},{8,16},{12,20},{16,8},{20,12},{24,0},{28,4},{1,25},{... | collective-permute-start | bytes 196616 | tf_op jit(solution)/shard_map/ppermute | solution.py:497
  11.7 5.9 %collective-permute-start.6 = (bf16[4,64,128]{2,1,0:T(8,128)(2,1)S(1)}, bf16[4,64,128]{2,1,0:T(8,128)(2,1)S(1)}, u32[]{:S(2)}, u32[]{:S(2)}) collective-permute-start(bf16[4,64,128]{2,1,0:T(8,128)(2,1)S(1)} %pad_maximum_fusion.refs_3_), channel_id=1, source_target_pairs={{0,16},{4,20},{8,24},{12,28},{16,0},{20,4},{24,8},{28,12},{1,17},{... | collective-permute-start | bytes 196616 | tf_op jit(solution)/shard_map/ppermute | solution.py:497
  11.7 7.4 %collective-permute-start.4 = (bf16[4,64,128]{2,1,0:T(8,128)(2,1)S(1)}, bf16[4,64,128]{2,1,0:T(8,128)(2,1)S(1)}, u32[]{:S(2)}, u32[]{:S(2)}) collective-permute-start(bf16[4,64,128]{2,1,0:T(8,128)(2,1)S(1)} %pad_maximum_fusion.refs_3_), channel_id=1, source_target_pairs={{0,8},{4,12},{8,0},{12,4},{16,24},{20,28},{24,16},{28,20},{1,9},{5... | collective-permute-start | bytes 196616 | tf_op jit(solution)/shard_map/ppermute | solution.py:497
  12.5 9.9 %collective-permute-start.3 = (bf16[4,64,128]{2,1,0:T(8,128)(2,1)S(1)}, bf16[4,64,128]{2,1,0:T(8,128)(2,1)S(1)}, u32[]{:S(2)}, u32[]{:S(2)}) collective-permute-start(bf16[4,64,128]{2,1,0:T(8,128)(2,1)S(1)} %pad_maximum_fusion.refs_3_), channel_id=1, source_target_pairs={{0,4},{4,0},{8,12},{12,8},{16,20},{20,16},{24,28},{28,24},{1,5},{5... | collective-permute-start | bytes 196616 | tf_op jit(solution)/shard_map/ppermute | solution.py:501
  14.0 5.6 %collective-permute-start.10 = (bf16[4,64,128]{2,1,0:T(8,128)(2,1)S(1)}, bf16[4,64,128]{2,1,0:T(8,128)(2,1)S(1)}, u32[]{:S(2)}, u32[]{:S(2)}) collective-permute-start(bf16[4,64,128]{2,1,0:T(8,128)(2,1)S(1)} %pad_maximum_fusion.1), channel_id=1, source_target_pairs={{0,4},{4,0},{8,12},{12,8},{16,20},{20,16},{24,28},{28,24},{1,5},{5... | collective-permute-start | bytes 196616 | tf_op jit(solution)/shard_map/ppermute | solution.py:501
  14.6 7.8 %collective-permute-start.9 = (bf16[4,64,128]{2,1,0:T(8,128)(2,1)S(1)}, bf16[4,64,128]{2,1,0:T(8,128)(2,1)S(1)}, u32[]{:S(2)}, u32[]{:S(2)}) collective-permute-start(bf16[4,64,128]{2,1,0:T(8,128)(2,1)S(1)} %collective-permute-done.8.refs_9_), channel_id=1, source_target_pairs={{0,4},{4,0},{8,12},{12,8},{16,20},{20,16},{24,28},{28,24},{1,5},{5... | collective-permute-start | bytes 196616 | tf_op jit(solution)/shard_map/ppermute | solution.py:501
  17.6 6.5 %collective-permute-start.7 = (bf16[4,64,128]{2,1,0:T(8,128)(2,1)S(1)}, bf16[4,64,128]{2,1,0:T(8,128)(2,1)S(1)}, u32[]{:S(2)}, u32[]{:S(2)}) collective-permute-start(bf16[4,64,128]{2,1,0:T(8,128)(2,1)S(1)} %collective-permute-done.6.refs_7_), channel_id=1, source_target_pairs={{0,4},{4,0},{8,12},{12,8},{16,20},{20,16},{24,28},{28,24},{1,5},{5... | collective-permute-start | bytes 196616 | tf_op jit(solution)/shard_map/ppermute | solution.py:501
  19.1 5.0 %collective-permute-start.5 = (bf16[4,64,128]{2,1,0:T(8,128)(2,1)S(1)}, bf16[4,64,128]{2,1,0:T(8,128)(2,1)S(1)}, u32[]{:S(2)}, u32[]{:S(2)}) collective-permute-start(bf16[4,64,128]{2,1,0:T(8,128)(2,1)S(1)} %collective-permute-done.4.refs_5_), channel_id=1, source_target_pairs={{0,4},{4,0},{8,12},{12,8},{16,20},{20,16},{24,28},{28,24},{1,5},{5... | collective-permute-start | bytes 196616 | tf_op jit(solution)/shard_map/ppermute | solution.py:501
  19.6 10.6 %collective-permute-start.13 = (bf16[8,64,128]{2,1,0:T(8,128)(2,1)S(1)}, bf16[8,64,128]{2,1,0:T(8,128)(2,1)S(1)}, u32[]{:S(2)}, u32[]{:S(2)}) collective-permute-start(bf16[8,64,128]{2,1,0:T(8,128)(2,1)S(1)} %constant_dynamic-update-slice_fusion.refs_4_), channel_id=1, source_target_pairs={{0,24},{4,28},{8,16},{12,20},{16,8},{20,12},{24,0},{28,4},{1,25},{... | collective-permute-start | bytes 393224 | tf_op jit(solution)/shard_map/ppermute | solution.py:497
  22.4 10.6 %collective-permute-start.12 = (bf16[8,64,128]{2,1,0:T(8,128)(2,1)S(1)}, bf16[8,64,128]{2,1,0:T(8,128)(2,1)S(1)}, u32[]{:S(2)}, u32[]{:S(2)}) collective-permute-start(bf16[8,64,128]{2,1,0:T(8,128)(2,1)S(1)} %constant_dynamic-update-slice_fusion.refs_4_), channel_id=1, source_target_pairs={{0,16},{4,20},{8,24},{12,28},{16,0},{20,4},{24,8},{28,12},{1,17},{... | collective-permute-start | bytes 393224 | tf_op jit(solution)/shard_map/ppermute | solution.py:497
  22.4 10.6 %collective-permute-start.11 = (bf16[8,64,128]{2,1,0:T(8,128)(2,1)S(1)}, bf16[8,64,128]{2,1,0:T(8,128)(2,1)S(1)}, u32[]{:S(2)}, u32[]{:S(2)}) collective-permute-start(bf16[8,64,128]{2,1,0:T(8,128)(2,1)S(1)} %constant_dynamic-update-slice_fusion.refs_4_), channel_id=1, source_target_pairs={{0,8},{4,12},{8,0},{12,4},{16,24},{20,28},{24,16},{28,20},{1,9},{5... | collective-permute-start | bytes 393224 | tf_op jit(solution)/shard_map/ppermute | solution.py:497
  28.6 10.1 %collective-permute-start.18 = (bf16[4,4,64,128]{3,2,1,0:T(8,128)(2,1)S(1)}, bf16[4,4,64,128]{3,2,1,0:T(8,128)(2,1)S(1)}, u32[]{:S(2)}, u32[]{:S(2)}) collective-permute-start(bf16[4,4,64,128]{3,2,1,0:T(8,128)(2,1)S(1)} %get-tuple-element.44), channel_id=1, source_target_pairs={{0,4},{4,0},{8,12},{12,8},{16,20},{20,16},{24,28},{28,24},{1,5},{5... | collective-permute-start | bytes 786440 | tf_op jit(solution)/shard_map/ppermute | solution.py:530
  37.4 7.0 %collective-permute-start.14 = (bf16[4,4,64,128]{3,2,1,0:T(8,128)(2,1)S(1)}, bf16[4,4,64,128]{3,2,1,0:T(8,128)(2,1)S(1)}, u32[]{:S(2)}, u32[]{:S(2)}) collective-permute-start(bf16[4,4,64,128]{3,2,1,0:T(8,128)(2,1)S(1)} %get-tuple-element.42), channel_id=1, source_target_pairs={{0,4},{4,0},{8,12},{12,8},{16,20},{20,16},{24,28},{28,24},{1,5},{5... | collective-permute-start | bytes 786440 | tf_op jit(solution)/shard_map/ppermute | solution.py:539
  38.9 7.6 %collective-permute-start.21 = (bf16[4,64,128]{2,1,0:T(8,128)(2,1)S(1)}, bf16[4,64,128]{2,1,0:T(8,128)(2,1)S(1)}, u32[]{:S(2)}, u32[]{:S(2)}) collective-permute-start(bf16[4,64,128]{2,1,0:T(8,128)(2,1)S(1)} %get-tuple-element.62), channel_id=1, source_target_pairs={{0,24},{4,28},{8,16},{12,20},{16,8},{20,12},{24,0},{28,4},{1,25},{... | collective-permute-start | bytes 196616 | tf_op jit(solution)/shard_map/ppermute | solution.py:547
  41.3 9.3 %collective-permute-start.20 = (bf16[4,64,128]{2,1,0:T(8,128)(2,1)S(1)}, bf16[4,64,128]{2,1,0:T(8,128)(2,1)S(1)}, u32[]{:S(2)}, u32[]{:S(2)}) collective-permute-start(bf16[4,64,128]{2,1,0:T(8,128)(2,1)S(1)} %get-tuple-element.63), channel_id=1, source_target_pairs={{0,16},{4,20},{8,24},{12,28},{16,0},{20,4},{24,8},{28,12},{1,17},{... | collective-permute-start | bytes 196616 | tf_op jit(solution)/shard_map/ppermute | solution.py:547
  41.3 9.3 %collective-permute-start.19 = (bf16[4,64,128]{2,1,0:T(8,128)(2,1)S(1)}, bf16[4,64,128]{2,1,0:T(8,128)(2,1)S(1)}, u32[]{:S(2)}, u32[]{:S(2)}) collective-permute-start(bf16[4,64,128]{2,1,0:T(8,128)(2,1)S(1)} %get-tuple-element.64), channel_id=1, source_target_pairs={{0,8},{4,12},{8,0},{12,4},{16,24},{20,28},{24,16},{28,20},{1,9},{5... | collective-permute-start | bytes 196616 | tf_op jit(solution)/shard_map/ppermute | solution.py:547
  44.6 6.1 %collective-permute-start.17 = (bf16[4,64,128]{2,1,0:T(8,128)(2,1)S(1)}, bf16[4,64,128]{2,1,0:T(8,128)(2,1)S(1)}, u32[]{:S(2)}, u32[]{:S(2)}) collective-permute-start(bf16[4,64,128]{2,1,0:T(8,128)(2,1)S(1)} %get-tuple-element.65), channel_id=1, source_target_pairs={{0,24},{4,28},{8,16},{12,20},{16,8},{20,12},{24,0},{28,4},{1,25},{... | collective-permute-start | bytes 196616 | tf_op jit(solution)/shard_map/ppermute | solution.py:547
  46.5 5.6 %collective-permute-start.16 = (bf16[4,64,128]{2,1,0:T(8,128)(2,1)S(1)}, bf16[4,64,128]{2,1,0:T(8,128)(2,1)S(1)}, u32[]{:S(2)}, u32[]{:S(2)}) collective-permute-start(bf16[4,64,128]{2,1,0:T(8,128)(2,1)S(1)} %get-tuple-element.66), channel_id=1, source_target_pairs={{0,16},{4,20},{8,24},{12,28},{16,0},{20,4},{24,8},{28,12},{1,17},{... | collective-permute-start | bytes 196616 | tf_op jit(solution)/shard_map/ppermute | solution.py:547
  46.5 5.6 %collective-permute-start.15 = (bf16[4,64,128]{2,1,0:T(8,128)(2,1)S(1)}, bf16[4,64,128]{2,1,0:T(8,128)(2,1)S(1)}, u32[]{:S(2)}, u32[]{:S(2)}) collective-permute-start(bf16[4,64,128]{2,1,0:T(8,128)(2,1)S(1)} %get-tuple-element.67), channel_id=1, source_target_pairs={{0,8},{4,12},{8,0},{12,4},{16,24},{20,28},{24,16},{28,20},{1,9},{5... | collective-permute-start | bytes 196616 | tf_op jit(solution)/shard_map/ppermute | solution.py:547
  52.2 3.4 %collective-permute-start.24 = (bf16[128,128]{1,0:T(8,128)(2,1)S(1)}, bf16[128,128]{1,0:T(8,128)(2,1)S(1)}, u32[]{:S(2)}, u32[]{:S(2)}) collective-permute-start(bf16[128,128]{1,0:T(8,128)(2,1)S(1)} %get-tuple-element.68), channel_id=1, source_target_pairs={{0,3},{1,2},{2,1},{3,0},{4,7},{5,6},{6,5},{7,4},{8,11},{9,10},{10,... | collective-permute-start | bytes 98312 | tf_op jit(solution)/shard_map/ppermute | solution.py:574
  53.3 3.9 %collective-permute-start.23 = (bf16[128,128]{1,0:T(8,128)(2,1)S(1)}, bf16[128,128]{1,0:T(8,128)(2,1)S(1)}, u32[]{:S(2)}, u32[]{:S(2)}) collective-permute-start(bf16[128,128]{1,0:T(8,128)(2,1)S(1)} %get-tuple-element.71), channel_id=1, source_target_pairs={{0,2},{1,3},{2,0},{3,1},{4,6},{5,7},{6,4},{7,5},{8,10},{9,11},{10,... | collective-permute-start | bytes 98312 | tf_op jit(solution)/shard_map/ppermute | solution.py:574
  (1 other events, 3.3 us)

commit v6 on v5

--- a/solution.py
+++ b/solution.py
@@ -257,18 +257,59 @@
     run_copies([pltpu.make_async_copy(a, b, sems.at[n]) for n, (a, b) in enumerate(moves)])
 
 
-def list_kernel(seq_count, *refs):
-    rand_from, glob_from, query_from, grad_from = refs[:4]
-    spots_ref, query_ref, grad_ref, rand_ref, glob_ref, sems = refs[4:]
+def unpack_kernel(*refs):
+    piece_refs, (keys_ref, values_ref) = refs[:-2], refs[-2:]
+    head = lax.axis_index("head")
+    short = keys_ref.shape[0]
+    for offset, piece in enumerate(piece_refs):
+        columns = head_columns(head, offset)
+        keys_ref[:, columns] = piece[:short, :]
+        values_ref[:, columns] = piece[short:, :]
+
+
+def dot(left, right, left_dim, right_dim):
+    return lax.dot_general(
+        left,
+        right,
+        (((left_dim,), (right_dim,)), ((), ())),
+        preferred_element_type=jnp.float32,
+    )
+
+
+def listed_spots(spots_ref, step):
+    return [spots_ref[step, number] for number in range(spots_ref.shape[1])]
+
+
+def begin(part_refs, starts, library, total):
+    for part, at in zip(part_refs, starts):
+        library[at : at + part.shape[0]] = part[...]
+    total[...] = jnp.zeros_like(total)
+
+
+def add_terms(total, spots, terms):
+    for number, spot in enumerate(spots):
+        total[spot] += terms[number * BLOCK : (number + 1) * BLOCK]
+
+
+def finish(total, keep_ref, ship_ref):
+    pairs, size = keep_ref.shape[:2]
+    for pair in range(pairs):
+        keep_ref[pair] = total[pl.ds(2 * pair * size, size)]
+        ship_ref[pair] = total[pl.ds((2 * pair + 1) * size, size)].astype(jnp.bfloat16)
+
+
+def stacked_heads(ref, step, chunk):
+    rows = slice(step * BLOCK, (step + 1) * BLOCK)
+    return jnp.concatenate([ref[rows, h * DH : (h + 1) * DH] for h in chunk], axis=0)
+
+
+def chunks_of(heads, size):
+    return [range(start, start + size) for start in range(0, heads, size)]
+
+
+def list_entries(spots_ref, rand_ref, glob_ref, seq_count):
     here = lax.axis_index("seq")
     head = lax.axis_index("head")
-    moves = [(rand_from, rand_ref), (glob_from, glob_ref)]
-    moves += [(query_from, query_ref), (grad_from, grad_ref)]
-    copies = [pltpu.make_async_copy(a, b, sems.at[n]) for n, (a, b) in enumerate(moves)]
-    for copy in copies:
-        copy.start()
-    copies[0].wait()
-    copies[1].wait()
     blocks_here = rand_ref.shape[0]
     last = seq_count * blocks_here - 1
     for step in range(blocks_here):
@@ -279,69 +320,25 @@
         for number, name in enumerate(names):
             owner = lax.div(name, blocks_here) ^ here
             spots_ref[step, number] = owner * blocks_here + (lax.rem(name, blocks_here) ^ head)
+
+
+def probs_kernel(seq_count, starts, size, *refs):
+    sources, part_refs, refs = refs[:4], refs[4 : 4 + seq_count], refs[4 + seq_count :]
+    probs_ref, rows_ref, keep_ref, ship_ref, spots_ref, query_ref, grad_ref = refs[:7]
+    library, total, rand_ref, glob_ref, sems = refs[7:]
+    targets = (rand_ref, glob_ref, query_ref, grad_ref)
+    moves = enumerate(zip(sources, targets))
+    copies = [pltpu.make_async_copy(a, b, sems.at[n]) for n, (a, b) in moves]
+    for copy in copies:
+        copy.start()
+    blocks_here = probs_ref.shape[0]
+    all_blocks = library.shape[0]
+    begin(part_refs, starts, library, total)
+    copies[0].wait()
+    copies[1].wait()
+    list_entries(spots_ref, rand_ref, glob_ref, seq_count)
     copies[2].wait()
     copies[3].wait()
-
-
-def unpack_kernel(*refs):
-    piece_refs, (keys_ref, values_ref) = refs[:-2], refs[-2:]
-    head = lax.axis_index("head")
-    short = keys_ref.shape[0]
-    for offset, piece in enumerate(piece_refs):
-        columns = head_columns(head, offset)
-        keys_ref[:, columns] = piece[:short, :]
-        values_ref[:, columns] = piece[short:, :]
-
-
-def dot(left, right, left_dim, right_dim):
-    return lax.dot_general(
-        left,
-        right,
-        (((left_dim,), (right_dim,)), ((), ())),
-        preferred_element_type=jnp.float32,
-    )
-
-
-def listed_spots(spots_ref, step):
-    return [spots_ref[step, number] for number in range(spots_ref.shape[1])]
-
-
-def begin(part_refs, library, total):
-    at = 0
-    for part in part_refs:
-        library[at : at + part.shape[0]] = part[...]
-        at += part.shape[0]
-    total[...] = jnp.zeros_like(total)
-
-
-def add_terms(total, spots, terms):
-    for number, spot in enumerate(spots):
-        total[spot] += terms[number * BLOCK : (number + 1) * BLOCK]
-
-
-def finish(total, keep_ref, ship_ref):
-    pairs, size = keep_ref.shape[:2]
-    for pair in range(pairs):
-        keep_ref[pair] = total[pl.ds(2 * pair * size, size)]
-        ship_ref[pair] = total[pl.ds((2 * pair + 1) * size, size)].astype(jnp.bfloat16)
-
-
-def stacked_heads(ref, step, chunk):
-    rows = slice(step * BLOCK, (step + 1) * BLOCK)
-    return jnp.concatenate([ref[rows, h * DH : (h + 1) * DH] for h in chunk], axis=0)
-
-
-def chunks_of(heads, size):
-    return [range(start, start + size) for start in range(0, heads, size)]
-
-
-def probs_kernel(seq_count, size, *refs):
-    spots_ref, query_ref, grad_ref = refs[:3]
-    part_refs = refs[3 : 3 + seq_count]
-    probs_ref, rows_ref, keep_ref, ship_ref, library, total = refs[3 + seq_count :]
-    blocks_here = probs_ref.shape[0]
-    all_blocks = library.shape[0]
-    begin(part_refs, library, total)
     for step in range(blocks_here):
         block = lax.axis_index("seq") * blocks_here + step
         spots = listed_spots(spots_ref, step)
@@ -381,11 +378,11 @@
     return copy
 
 
-def dscores_kernel(size, *refs):
+def dscores_kernel(starts, size, *refs):
     spots_ref, query_ref, grad_ref, probs_ref = refs[:4]
     part_refs, refs = refs[4:-9], refs[-9:]
     out_ref, dscores_ref, keep_ref, ship_ref, library, total, rows_ref, stage, sems = refs
-    begin(part_refs, library, total)
+    begin(part_refs, starts, library, total)
     copies = []
     for step in range(stage.shape[0]):
         spots = listed_spots(spots_ref, step)
@@ -472,21 +469,6 @@
         scratch_shapes=[pltpu.SemaphoreType.DMA((2 * head_count,))],
         compiler_params=small_grant(),
     )(keys, values)
-    spots, query_here, grad_here = pl.pallas_call(
-        lambda *refs: list_kernel(seq_count, *refs),
-        in_specs=[anywhere] * 4,
-        out_specs=[smem] + [anywhere] * 2,
-        out_shape=[spots_shape, tile_shape, tile_shape],
-        scratch_shapes=[
-            pltpu.SMEM(rand_blocks.shape, jnp.int32),
-            pltpu.SMEM(glob_blocks.shape, jnp.int32),
-            pltpu.SemaphoreType.DMA((4,)),
-        ],
-        compiler_params=small_grant(),
-        cost_estimate=pl.CostEstimate(
-            flops=0, bytes_accessed=8 * tok_count * width, transcendentals=0
-        ),
-    )(rand_blocks, glob_blocks, queries, d_out)
     pieces = [pieces[0]] + [
         lax.ppermute(pieces[k], "head", flips(head_count, k)) for k in range(1, head_count)
     ]
@@ -501,11 +483,15 @@
         return lax.ppermute(part, "seq", flips(seq_count, 1))
 
     key_far = along_far(jnp.stack([p[:short] for p in pieces]))
-    key_parts = [part for far in key_far for part in (far, to_near(far))]
+    order = sorted(range(pair_count), key=lambda n: (bin(n).count("1"), -n))
+    key_parts = [part for n in order for part in (key_far[n], to_near(key_far[n]))]
+    key_starts = [slot * blocks_here for n in order for slot in (2 * n, 2 * n + 1)]
+    value_starts = [2 * n * blocks_here for n in order]
     value_own = jnp.stack([p[short:] for p in pieces])
     value_pair = jnp.concatenate([value_own, to_near(value_own)])
     value_pair, _ = lax.optimization_barrier((value_pair, key_far[1:]))
-    value_parts = along_far(value_pair)
+    value_far = along_far(value_pair)
+    value_parts = [value_far[n] for n in order]
 
     lists = pltpu.VMEM((blocks_here, listed, DH), jnp.bfloat16)
     stage = pltpu.VMEM((blocks_here, BLOCK, width), jnp.bfloat16)
@@ -519,17 +505,31 @@
     library = pltpu.VMEM((seq_count * blocks_here, BLOCK, DH), jnp.bfloat16)
     total = pltpu.VMEM((seq_count * blocks_here, BLOCK, DH), jnp.float32)
 
-    probs, key_lists, value_keep, value_ship = pl.pallas_call(
-        lambda *refs: probs_kernel(seq_count, size, *refs),
-        in_specs=[smem, vmem, vmem] + [vmem] * len(key_parts),
-        out_specs=[vmem] * 4,
-        out_shape=[square_shape, listing_shape, keep_shape, ship_shape],
-        scratch_shapes=[library, total],
+    probs, key_lists, value_keep, value_ship, spots, query_here, grad_here = pl.pallas_call(
+        lambda *refs: probs_kernel(seq_count, key_starts, size, *refs),
+        in_specs=[anywhere] * 4 + [vmem] * len(key_parts),
+        out_specs=[vmem] * 4 + [smem] + [vmem] * 2,
+        out_shape=[
+            square_shape,
+            listing_shape,
+            keep_shape,
+            ship_shape,
+            spots_shape,
+            tile_shape,
+            tile_shape,
+        ],
+        scratch_shapes=[
+            library,
+            total,
+            pltpu.SMEM(rand_blocks.shape, jnp.int32),
+            pltpu.SMEM(glob_blocks.shape, jnp.int32),
+            pltpu.SemaphoreType.DMA((4,)),
+        ],
         **kernel_options(2, pairs),
-    )(spots, query_here, grad_here, *key_parts)
+    )(rand_blocks, glob_blocks, queries, d_out, *key_parts)
     value_near = lax.ppermute(value_ship, "seq", flips(seq_count, 1))
     attn_out, dscores, key_keep, key_ship = pl.pallas_call(
-        lambda *refs: dscores_kernel(size, *refs),
+        lambda *refs: dscores_kernel(value_starts, size, *refs),
         in_specs=[smem, vmem, vmem, vmem] + [vmem] * len(value_parts),
         out_specs=[anywhere, vmem, vmem, vmem],
         out_shape=[tile_shape, square_shape, keep_shape, ship_shape],
@@ -545,7 +545,7 @@
     def from_far(sums):
         return [
             lax.ppermute(sums[pair - 1], "seq", flips(seq_count, 2 * pair))
-            for pair in range(1, pair_count)
+            for pair in order[1:]
         ]
 
     def added(own, far):
@@ -556,7 +556,7 @@
     key_own, key_sums = sums_of(key_keep, key_near)
     key_far = from_far(key_sums)
     value_own, value_sums = sums_of(value_keep, value_near)
-    value_far = from_far(value_sums)
+    value_terms = from_far(value_sums)
     d_queries = pl.pallas_call(
         lambda *refs: dquery_kernel(size, *refs),
         in_specs=[vmem, vmem],
@@ -566,9 +566,9 @@
         **kernel_options(1, pairs),
     )(*lax.optimization_barrier((dscores, key_lists, key_sums))[:2])
 
-    key_far, value_far, d_queries = lax.optimization_barrier((key_far, value_far, d_queries))
+    key_far, value_terms, d_queries = lax.optimization_barrier((key_far, value_terms, d_queries))
     packed = jnp.concatenate(
-        [added(key_own, key_far), added(value_own, value_far)], axis=1
+        [added(key_own, key_far), added(value_own, value_terms)], axis=1
     ).astype(jnp.bfloat16)
     back = [packed[0]] + [
         lax.ppermute(packed[k], "head", flips(head_count, k)) for k in range(1, head_count)

time: 58.1 us -> 57.4 us (0.988)
  Pallas kernels: 13.9 us -> 12.5 us
  waiting for transfers between devices: 11.1 us -> 11.7 us
    ppermute x3, waiting for transfers between devices: 1.38 us -> 3.25 us  [whole_body(): lax.ppermute(pieces[k], 'head', flips(head_count, k))]
    ppermute x6, waiting for transfers between devices: 4.21 us -> 2.73 us  [along_far(): parts.append(lax.ppermute(own, 'seq', flips(seq_count, k)))]
    pallas_call x3 -> x2, Pallas kernels: 10.8 us -> 9.42 us  [the longest x1 5.09 us: whole_body(): pl.pallas_call(lambda *refs: probs_kernel(seq_count, key_starts, size, *r...]
  transfers between devices with their start and end apart: 25 -> 25, of which waited for: 8 -> 10; matrix products, arithmetic and copies ran while one was open for 0% -> 0% of each run, Pallas kernels for 21% -> 19%
where the time goes in v6:
time: 57.4 us; the launch traced here: 57.2 us
  starting transfers between devices  31.8 us (55%)
  Pallas kernels  12.5 us (22%)
  waiting for transfers between devices  11.7 us (20%)
  between operations  0.78 us (1%)
    ppermute x6, starting transfers between devices, from_far(): lax.ppermute(sums[pair - 1], 'seq', flips(seq_count, 2 * pair))  8.91 us
    ppermute x6, starting transfers between devices, along_far(): parts.append(lax.ppermute(own, 'seq', flips(seq_count, k)))  8.9 us
    ppermute x5, starting transfers between devices, to_near(): return lax.ppermute(part, 'seq', flips(seq_count, 1))  5.89 us
    pallas_call x1, Pallas kernels, whole_body(): pl.pallas_call(lambda *refs: probs_kernel(seq_count, key_starts, size, *r...  5.09 us
    pallas_call x1, Pallas kernels, whole_body(): pl.pallas_call(lambda *refs: dscores_kernel(value_starts, size, *refs), i...  4.33 us
    ppermute x3, waiting for transfers between devices, whole_body(): lax.ppermute(pieces[k], 'head', flips(head_count, k))  3.25 us
    ppermute x3, starting transfers between devices, whole_body(): lax.ppermute(pieces[k], 'head', flips(head_count, k))  3.15 us
    ppermute x3, waiting for transfers between devices, whole_body(): lax.ppermute(packed[k], 'head', flips(head_count, k))  2.77 us
  transfers between devices with their start and end apart: 25, of which 10 were waited for; matrix products, arithmetic and copies ran while one was open for 0% of the time, Pallas kernels for 19%

profile of v6, /device:TPU:0, one launch (start us, length us, event | category | flops | bytes accessed | tf_op | source)
XLA Modules:
  0.0 57.2 jit_solution(13736080526518839899)
XLA Ops:
  2.1 2.6 %collective-permute-start.1 = (bf16[128,128]{1,0:T(8,128)(2,1)S(1)}, bf16[128,128]{1,0:T(8,128)(2,1)S(1)}, u32[]{:S(2)}, u32[]{:S(2)}) collective-permute-start(bf16[128,128]{1,0:T(8,128)(2,1)S(1)} %get-tuple-element.33), channel_id=1, source_target_pairs={{0,2},{1,3},{2,0},{3,1},{4,6},{5,7},{6,4},{7,5},{8,10},{9,11},{10,... | collective-permute-start | bytes 98312 | tf_op jit(solution)/shard_map/ppermute | solution.py:473
  4.7 1.9 %collective-permute-done.1 = bf16[128,128]{1,0:T(8,128)(2,1)S(1)} collective-permute-done((bf16[128,128]{1,0:T(8,128)(2,1)S(1)}, bf16[128,128]{1,0:T(8,128)(2,1)S(1)}, u32[]{:S(2)}, u32[]{:S(2)}) %collective-permute-start.1) | collective-permute-done | bytes 32800 | tf_op jit(solution)/shard_map/ppermute | solution.py:473
  6.6 1.4 %collective-permute-done.2 = bf16[128,128]{1,0:T(8,128)(2,1)S(1)} collective-permute-done((bf16[128,128]{1,0:T(8,128)(2,1)S(1)}, bf16[128,128]{1,0:T(8,128)(2,1)S(1)}, u32[]{:S(2)}, u32[]{:S(2)}) %collective-permute-start.2) | collective-permute-done | bytes 32800 | tf_op jit(solution)/shard_map/ppermute | solution.py:473
  8.0 3.7 %collective-permute-start.8 = (bf16[4,64,128]{2,1,0:T(8,128)(2,1)S(1)}, bf16[4,64,128]{2,1,0:T(8,128)(2,1)S(1)}, u32[]{:S(2)}, u32[]{:S(2)}) collective-permute-start(bf16[4,64,128]{2,1,0:T(8,128)(2,1)S(1)} %pad_maximum_fusion.refs_4_), channel_id=1, source_target_pairs={{0,24},{4,28},{8,16},{12,20},{16,8},{20,12},{24,0},{28,4},{1,25},{... | collective-permute-start | bytes 196616 | tf_op jit(solution)/shard_map/ppermute | solution.py:479
  12.5 1.5 %collective-permute-start.3 = (bf16[4,64,128]{2,1,0:T(8,128)(2,1)S(1)}, bf16[4,64,128]{2,1,0:T(8,128)(2,1)S(1)}, u32[]{:S(2)}, u32[]{:S(2)}) collective-permute-start(bf16[4,64,128]{2,1,0:T(8,128)(2,1)S(1)} %pad_maximum_fusion.refs_4_), channel_id=1, source_target_pairs={{0,4},{4,0},{8,12},{12,8},{16,20},{20,16},{24,28},{28,24},{1,5},{5... | collective-permute-start | bytes 196616 | tf_op jit(solution)/shard_map/ppermute | solution.py:483
  14.9 1.5 %collective-permute-start.9 = (bf16[4,64,128]{2,1,0:T(8,128)(2,1)S(1)}, bf16[4,64,128]{2,1,0:T(8,128)(2,1)S(1)}, u32[]{:S(2)}, u32[]{:S(2)}) collective-permute-start(bf16[4,64,128]{2,1,0:T(8,128)(2,1)S(1)} %collective-permute-done.8.refs_10_), channel_id=1, source_target_pairs={{0,4},{4,0},{8,12},{12,8},{16,20},{20,16},{24,28},{28,24},{1,5},{5... | collective-permute-start | bytes 196616 | tf_op jit(solution)/shard_map/ppermute | solution.py:483
  16.8 1.5 %collective-permute-start.7 = (bf16[4,64,128]{2,1,0:T(8,128)(2,1)S(1)}, bf16[4,64,128]{2,1,0:T(8,128)(2,1)S(1)}, u32[]{:S(2)}, u32[]{:S(2)}) collective-permute-start(bf16[4,64,128]{2,1,0:T(8,128)(2,1)S(1)} %collective-permute-done.6.refs_8_), channel_id=1, source_target_pairs={{0,4},{4,0},{8,12},{12,8},{16,20},{20,16},{24,28},{28,24},{1,5},{5... | collective-permute-start | bytes 196616 | tf_op jit(solution)/shard_map/ppermute | solution.py:483
  19.1 3.7 %collective-permute-start.13 = (bf16[8,64,128]{2,1,0:T(8,128)(2,1)S(1)}, bf16[8,64,128]{2,1,0:T(8,128)(2,1)S(1)}, u32[]{:S(2)}, u32[]{:S(2)}) collective-permute-start(bf16[8,64,128]{2,1,0:T(8,128)(2,1)S(1)} %constant_dynamic-update-slice_fusion.refs_4_), channel_id=1, source_target_pairs={{0,24},{4,28},{8,16},{12,20},{16,8},{20,12},{24,0},{28,4},{1,25},{... | collective-permute-start | bytes 393224 | tf_op jit(solution)/shard_map/ppermute | solution.py:479
  23.5 5.1 %shard_map.94 = (bf16[4,832,512]{2,1,0:T(8,128)(2,1)S(1)}, bf16[4,832,128]{2,1,0:T(8,128)(2,1)S(1)}, f32[4,4,64,128]{3,2,1,0:T(8,128)S(1)}, bf16[4,4,64,128]{3,2...) custom-call(s32[4,8]{1,0:T(4,128)} %refs_0_.3, ...), custom_call_target="tpu_custom_call" | custom-call | flops 1744830464 | bytes 6815744 | tf_op jit(solution)/shard_map/pallas_call | solution.py:508
  28.6 1.3 %collective-permute-start.18 = (bf16[4,4,64,128]{3,2,1,0:T(8,128)(2,1)S(1)}, bf16[4,4,64,128]{3,2,1,0:T(8,128)(2,1)S(1)}, u32[]{:S(2)}, u32[]{:S(2)}) collective-permute-start(bf16[4,4,64,128]{3,2,1,0:T(8,128)(2,1)S(1)} %get-tuple-element.44), channel_id=1, source_target_pairs={{0,4},{4,0},{8,12},{12,8},{16,20},{20,16},{24,28},{28,24},{1,5},{5... | collective-permute-start | bytes 786440 | tf_op jit(solution)/shard_map/ppermute | solution.py:530
  30.0 2.1 %collective-permute-done.11.refs_5_ = bf16[8,64,128]{2,1,0:T(8,128)(2,1)S(1)} collective-permute-done((bf16[8,64,128]{2,1,0:T(8,128)(2,1)S(1)}, bf16[8,64,128]{2,1,0:T(8,128)(2,1)S(1)}, u32[]{:S(2)}, u32[]{:S(2)}) %collective-permute-start.11) | collective-permute-done | bytes 131104 | tf_op jit(solution)/shard_map/ppermute | solution.py:479
  32.0 4.3 %shard_map.95 = (bf16[256,1024]{1,0:T(8,128)(2,1)}, bf16[4,832,512]{2,1,0:T(8,128)(2,1)S(1)}, f32[4,4,64,128]{3,2,1,0:T(8,128)S(1)}, bf16[4,4,64,128]{3,2,1,0:T(8,128)(2,1)S(1)}) custom-call(s32[4,13]{1,0:T(4,128)S(1)} %get-tuple-element.35.refs_0_, bf16[256,1024]{1,0:T(8,128)(2,1)S(1)} %get-tuple-element.36.refs_1_, ...), custom_call_target="tpu_custom_call" | custom-call | flops 2617245696 | bytes 6815744 | tf_op jit(solution)/shard_map/pallas_call | solution.py:531
  36.4 1.5 %collective-permute-start.14 = (bf16[4,4,64,128]{3,2,1,0:T(8,128)(2,1)S(1)}, bf16[4,4,64,128]{3,2,1,0:T(8,128)(2,1)S(1)}, u32[]{:S(2)}, u32[]{:S(2)}) collective-permute-start(bf16[4,4,64,128]{3,2,1,0:T(8,128)(2,1)S(1)} %get-tuple-element.42), channel_id=1, source_target_pairs={{0,4},{4,0},{8,12},{12,8},{16,20},{20,16},{24,28},{28,24},{1,5},{5... | collective-permute-start | bytes 786440 | tf_op jit(solution)/shard_map/ppermute | solution.py:539
  37.9 2.1 %collective-permute-start.21 = (bf16[4,64,128]{2,1,0:T(8,128)(2,1)S(1)}, bf16[4,64,128]{2,1,0:T(8,128)(2,1)S(1)}, u32[]{:S(2)}, u32[]{:S(2)}) collective-permute-start(bf16[4,64,128]{2,1,0:T(8,128)(2,1)S(1)} %get-tuple-element.62), channel_id=1, source_target_pairs={{0,24},{4,28},{8,16},{12,20},{16,8},{20,12},{24,0},{28,4},{1,25},{... | collective-permute-start | bytes 196616 | tf_op jit(solution)/shard_map/ppermute | solution.py:547
  40.0 2.4 %collective-permute-start.19 = (bf16[4,64,128]{2,1,0:T(8,128)(2,1)S(1)}, bf16[4,64,128]{2,1,0:T(8,128)(2,1)S(1)}, u32[]{:S(2)}, u32[]{:S(2)}) collective-permute-start(bf16[4,64,128]{2,1,0:T(8,128)(2,1)S(1)} %get-tuple-element.64), channel_id=1, source_target_pairs={{0,16},{4,20},{8,24},{12,28},{16,0},{20,4},{24,8},{28,12},{1,17},{... | collective-permute-start | bytes 196616 | tf_op jit(solution)/shard_map/ppermute | solution.py:547
  42.4 1.2 %collective-permute-done.14 = bf16[4,4,64,128]{3,2,1,0:T(8,128)(2,1)S(1)} collective-permute-done((bf16[4,4,64,128]{3,2,1,0:T(8,128)(2,1)S(1)}, bf16[4,4,64,128]{3,2,1,0:T(8,128)(2,1)S(1)}, u32[]{:S(2)}, u32[]{:S(2)}) %collective-permute-start.14) | collective-permute-done | bytes 262176 | tf_op jit(solution)/shard_map/ppermute | solution.py:539
  43.7 2.1 %collective-permute-start.17 = (bf16[4,64,128]{2,1,0:T(8,128)(2,1)S(1)}, bf16[4,64,128]{2,1,0:T(8,128)(2,1)S(1)}, u32[]{:S(2)}, u32[]{:S(2)}) collective-permute-start(bf16[4,64,128]{2,1,0:T(8,128)(2,1)S(1)} %get-tuple-element.65), channel_id=1, source_target_pairs={{0,24},{4,28},{8,16},{12,20},{16,8},{20,12},{24,0},{28,4},{1,25},{... | collective-permute-start | bytes 196616 | tf_op jit(solution)/shard_map/ppermute | solution.py:547
  45.8 2.4 %collective-permute-start.15 = (bf16[4,64,128]{2,1,0:T(8,128)(2,1)S(1)}, bf16[4,64,128]{2,1,0:T(8,128)(2,1)S(1)}, u32[]{:S(2)}, u32[]{:S(2)}) collective-permute-start(bf16[4,64,128]{2,1,0:T(8,128)(2,1)S(1)} %get-tuple-element.67), channel_id=1, source_target_pairs={{0,16},{4,20},{8,24},{12,28},{16,0},{20,4},{24,8},{28,12},{1,17},{... | collective-permute-start | bytes 196616 | tf_op jit(solution)/shard_map/ppermute | solution.py:547
  48.2 1.5 %shard_map.96 = bf16[256,1024]{1,0:T(8,128)(2,1)} custom-call(bf16[4,832,512]{2,1,0:T(8,128)(2,1)S(1)} %get-tuple-element.47.refs_0_, bf16[4,832,128]{2,1,0:T(8,128)(2,1)S(1)} %get-tuple-element.48.refs_1_), custom_call_target="tpu_custom_call" | custom-call | flops 872415232 | bytes 6815744 | tf_op jit(solution)/shard_map/pallas_call | solution.py:560
  49.9 1.5 %collective-permute-done.16 = bf16[4,64,128]{2,1,0:T(8,128)(2,1)S(1)} collective-permute-done((bf16[4,64,128]{2,1,0:T(8,128)(2,1)S(1)}, bf16[4,64,128]{2,1,0:T(8,128)(2,1)S(1)}, u32[]{:S(2)}, u32[]{:S(2)}) %collective-permute-start.16) | collective-permute-done | bytes 65568 | tf_op jit(solution)/shard_map/ppermute | solution.py:547
  51.6 1.0 %collective-permute-start.22 = (bf16[128,128]{1,0:T(8,128)(2,1)S(1)}, bf16[128,128]{1,0:T(8,128)(2,1)S(1)}, u32[]{:S(2)}, u32[]{:S(2)}) collective-permute-start(bf16[128,128]{1,0:T(8,128)(2,1)S(1)} %get-tuple-element.70), channel_id=1, source_target_pairs={{0,1},{1,0},{2,3},{3,2},{4,5},{5,4},{6,7},{7,6},{8,9},{9,8},{10,11... | collective-permute-start | bytes 98312 | tf_op jit(solution)/shard_map/ppermute | solution.py:574
  52.6 1.1 %collective-permute-start.23 = (bf16[128,128]{1,0:T(8,128)(2,1)S(1)}, bf16[128,128]{1,0:T(8,128)(2,1)S(1)}, u32[]{:S(2)}, u32[]{:S(2)}) collective-permute-start(bf16[128,128]{1,0:T(8,128)(2,1)S(1)} %get-tuple-element.71), channel_id=1, source_target_pairs={{0,2},{1,3},{2,0},{3,1},{4,6},{5,7},{6,4},{7,5},{8,10},{9,11},{10,... | collective-permute-start | bytes 98312 | tf_op jit(solution)/shard_map/ppermute | solution.py:574
  53.7 1.2 %collective-permute-done.24.refs_3_ = bf16[128,128]{1,0:T(8,128)(2,1)S(1)} collective-permute-done((bf16[128,128]{1,0:T(8,128)(2,1)S(1)}, bf16[128,128]{1,0:T(8,128)(2,1)S(1)}, u32[]{:S(2)}, u32[]{:S(2)}) %collective-permute-start.24) | collective-permute-done | bytes 32800 | tf_op jit(solution)/shard_map/ppermute | solution.py:574
  54.9 1.6 %collective-permute-done.23.refs_2_ = bf16[128,128]{1,0:T(8,128)(2,1)S(1)} collective-permute-done((bf16[128,128]{1,0:T(8,128)(2,1)S(1)}, bf16[128,128]{1,0:T(8,128)(2,1)S(1)}, u32[]{:S(2)}, u32[]{:S(2)}) %collective-permute-start.23) | collective-permute-done | bytes 32800 | tf_op jit(solution)/shard_map/ppermute | solution.py:574
  (48 shorter events, 6.4 us)
Async XLA Ops:
  2.1 4.5 %collective-permute-start.1 = (bf16[128,128]{1,0:T(8,128)(2,1)S(1)}, bf16[128,128]{1,0:T(8,128)(2,1)S(1)}, u32[]{:S(2)}, u32[]{:S(2)}) collective-permute-start(bf16[128,128]{1,0:T(8,128)(2,1)S(1)} %get-tuple-element.33), channel_id=1, source_target_pairs={{0,2},{1,3},{2,0},{3,1},{4,6},{5,7},{6,4},{7,5},{8,10},{9,11},{10,... | collective-permute-start | bytes 98312 | tf_op jit(solution)/shard_map/ppermute | solution.py:473
  4.6 3.3 %collective-permute-start.2 = (bf16[128,128]{1,0:T(8,128)(2,1)S(1)}, bf16[128,128]{1,0:T(8,128)(2,1)S(1)}, u32[]{:S(2)}, u32[]{:S(2)}) collective-permute-start(bf16[128,128]{1,0:T(8,128)(2,1)S(1)} %get-tuple-element.34), channel_id=1, source_target_pairs={{0,3},{1,2},{2,1},{3,0},{4,7},{5,6},{6,5},{7,4},{8,11},{9,10},{10,... | collective-permute-start | bytes 98312 | tf_op jit(solution)/shard_map/ppermute | solution.py:473
  8.0 6.8 %collective-permute-start.8 = (bf16[4,64,128]{2,1,0:T(8,128)(2,1)S(1)}, bf16[4,64,128]{2,1,0:T(8,128)(2,1)S(1)}, u32[]{:S(2)}, u32[]{:S(2)}) collective-permute-start(bf16[4,64,128]{2,1,0:T(8,128)(2,1)S(1)} %pad_maximum_fusion.refs_4_), channel_id=1, source_target_pairs={{0,24},{4,28},{8,16},{12,20},{16,8},{20,12},{24,0},{28,4},{1,25},{... | collective-permute-start | bytes 196616 | tf_op jit(solution)/shard_map/ppermute | solution.py:479
  11.7 5.1 %collective-permute-start.6 = (bf16[4,64,128]{2,1,0:T(8,128)(2,1)S(1)}, bf16[4,64,128]{2,1,0:T(8,128)(2,1)S(1)}, u32[]{:S(2)}, u32[]{:S(2)}) collective-permute-start(bf16[4,64,128]{2,1,0:T(8,128)(2,1)S(1)} %pad_maximum_fusion.refs_4_), channel_id=1, source_target_pairs={{0,8},{4,12},{8,0},{12,4},{16,24},{20,28},{24,16},{28,20},{1,9},{5... | collective-permute-start | bytes 196616 | tf_op jit(solution)/shard_map/ppermute | solution.py:479
  11.7 6.6 %collective-permute-start.4 = (bf16[4,64,128]{2,1,0:T(8,128)(2,1)S(1)}, bf16[4,64,128]{2,1,0:T(8,128)(2,1)S(1)}, u32[]{:S(2)}, u32[]{:S(2)}) collective-permute-start(bf16[4,64,128]{2,1,0:T(8,128)(2,1)S(1)} %pad_maximum_fusion.refs_4_), channel_id=1, source_target_pairs={{0,16},{4,20},{8,24},{12,28},{16,0},{20,4},{24,8},{28,12},{1,17},{... | collective-permute-start | bytes 196616 | tf_op jit(solution)/shard_map/ppermute | solution.py:479
  12.5 10.3 %collective-permute-start.3 = (bf16[4,64,128]{2,1,0:T(8,128)(2,1)S(1)}, bf16[4,64,128]{2,1,0:T(8,128)(2,1)S(1)}, u32[]{:S(2)}, u32[]{:S(2)}) collective-permute-start(bf16[4,64,128]{2,1,0:T(8,128)(2,1)S(1)} %pad_maximum_fusion.refs_4_), channel_id=1, source_target_pairs={{0,4},{4,0},{8,12},{12,8},{16,20},{20,16},{24,28},{28,24},{1,5},{5... | collective-permute-start | bytes 196616 | tf_op jit(solution)/shard_map/ppermute | solution.py:483
  14.0 5.1 %collective-permute-start.10 = (bf16[4,64,128]{2,1,0:T(8,128)(2,1)S(1)}, bf16[4,64,128]{2,1,0:T(8,128)(2,1)S(1)}, u32[]{:S(2)}, u32[]{:S(2)}) collective-permute-start(bf16[4,64,128]{2,1,0:T(8,128)(2,1)S(1)} %pad_maximum_fusion.1), channel_id=1, source_target_pairs={{0,4},{4,0},{8,12},{12,8},{16,20},{20,16},{24,28},{28,24},{1,5},{5... | collective-permute-start | bytes 196616 | tf_op jit(solution)/shard_map/ppermute | solution.py:483
  14.9 7.9 %collective-permute-start.9 = (bf16[4,64,128]{2,1,0:T(8,128)(2,1)S(1)}, bf16[4,64,128]{2,1,0:T(8,128)(2,1)S(1)}, u32[]{:S(2)}, u32[]{:S(2)}) collective-permute-start(bf16[4,64,128]{2,1,0:T(8,128)(2,1)S(1)} %collective-permute-done.8.refs_10_), channel_id=1, source_target_pairs={{0,4},{4,0},{8,12},{12,8},{16,20},{20,16},{24,28},{28,24},{1,5},{5... | collective-permute-start | bytes 196616 | tf_op jit(solution)/shard_map/ppermute | solution.py:483
  16.8 6.8 %collective-permute-start.7 = (bf16[4,64,128]{2,1,0:T(8,128)(2,1)S(1)}, bf16[4,64,128]{2,1,0:T(8,128)(2,1)S(1)}, u32[]{:S(2)}, u32[]{:S(2)}) collective-permute-start(bf16[4,64,128]{2,1,0:T(8,128)(2,1)S(1)} %collective-permute-done.6.refs_8_), channel_id=1, source_target_pairs={{0,4},{4,0},{8,12},{12,8},{16,20},{20,16},{24,28},{28,24},{1,5},{5... | collective-permute-start | bytes 196616 | tf_op jit(solution)/shard_map/ppermute | solution.py:483
  18.3 5.2 %collective-permute-start.5 = (bf16[4,64,128]{2,1,0:T(8,128)(2,1)S(1)}, bf16[4,64,128]{2,1,0:T(8,128)(2,1)S(1)}, u32[]{:S(2)}, u32[]{:S(2)}) collective-permute-start(bf16[4,64,128]{2,1,0:T(8,128)(2,1)S(1)} %collective-permute-done.4.refs_6_), channel_id=1, source_target_pairs={{0,4},{4,0},{8,12},{12,8},{16,20},{20,16},{24,28},{28,24},{1,5},{5... | collective-permute-start | bytes 196616 | tf_op jit(solution)/shard_map/ppermute | solution.py:483
  19.1 10.9 %collective-permute-start.13 = (bf16[8,64,128]{2,1,0:T(8,128)(2,1)S(1)}, bf16[8,64,128]{2,1,0:T(8,128)(2,1)S(1)}, u32[]{:S(2)}, u32[]{:S(2)}) collective-permute-start(bf16[8,64,128]{2,1,0:T(8,128)(2,1)S(1)} %constant_dynamic-update-slice_fusion.refs_4_), channel_id=1, source_target_pairs={{0,24},{4,28},{8,16},{12,20},{16,8},{20,12},{24,0},{28,4},{1,25},{... | collective-permute-start | bytes 393224 | tf_op jit(solution)/shard_map/ppermute | solution.py:479
  22.8 7.2 %collective-permute-start.12 = (bf16[8,64,128]{2,1,0:T(8,128)(2,1)S(1)}, bf16[8,64,128]{2,1,0:T(8,128)(2,1)S(1)}, u32[]{:S(2)}, u32[]{:S(2)}) collective-permute-start(bf16[8,64,128]{2,1,0:T(8,128)(2,1)S(1)} %constant_dynamic-update-slice_fusion.refs_4_), channel_id=1, source_target_pairs={{0,8},{4,12},{8,0},{12,4},{16,24},{20,28},{24,16},{28,20},{1,9},{5... | collective-permute-start | bytes 393224 | tf_op jit(solution)/shard_map/ppermute | solution.py:479
  22.8 9.3 %collective-permute-start.11 = (bf16[8,64,128]{2,1,0:T(8,128)(2,1)S(1)}, bf16[8,64,128]{2,1,0:T(8,128)(2,1)S(1)}, u32[]{:S(2)}, u32[]{:S(2)}) collective-permute-start(bf16[8,64,128]{2,1,0:T(8,128)(2,1)S(1)} %constant_dynamic-update-slice_fusion.refs_4_), channel_id=1, source_target_pairs={{0,16},{4,20},{8,24},{12,28},{16,0},{20,4},{24,8},{28,12},{1,17},{... | collective-permute-start | bytes 393224 | tf_op jit(solution)/shard_map/ppermute | solution.py:479
  28.6 9.2 %collective-permute-start.18 = (bf16[4,4,64,128]{3,2,1,0:T(8,128)(2,1)S(1)}, bf16[4,4,64,128]{3,2,1,0:T(8,128)(2,1)S(1)}, u32[]{:S(2)}, u32[]{:S(2)}) collective-permute-start(bf16[4,4,64,128]{3,2,1,0:T(8,128)(2,1)S(1)} %get-tuple-element.44), channel_id=1, source_target_pairs={{0,4},{4,0},{8,12},{12,8},{16,20},{20,16},{24,28},{28,24},{1,5},{5... | collective-permute-start | bytes 786440 | tf_op jit(solution)/shard_map/ppermute | solution.py:530
  36.4 7.2 %collective-permute-start.14 = (bf16[4,4,64,128]{3,2,1,0:T(8,128)(2,1)S(1)}, bf16[4,4,64,128]{3,2,1,0:T(8,128)(2,1)S(1)}, u32[]{:S(2)}, u32[]{:S(2)}) collective-permute-start(bf16[4,4,64,128]{3,2,1,0:T(8,128)(2,1)S(1)} %get-tuple-element.42), channel_id=1, source_target_pairs={{0,4},{4,0},{8,12},{12,8},{16,20},{20,16},{24,28},{28,24},{1,5},{5... | collective-permute-start | bytes 786440 | tf_op jit(solution)/shard_map/ppermute | solution.py:539
  37.9 7.9 %collective-permute-start.21 = (bf16[4,64,128]{2,1,0:T(8,128)(2,1)S(1)}, bf16[4,64,128]{2,1,0:T(8,128)(2,1)S(1)}, u32[]{:S(2)}, u32[]{:S(2)}) collective-permute-start(bf16[4,64,128]{2,1,0:T(8,128)(2,1)S(1)} %get-tuple-element.62), channel_id=1, source_target_pairs={{0,24},{4,28},{8,16},{12,20},{16,8},{20,12},{24,0},{28,4},{1,25},{... | collective-permute-start | bytes 196616 | tf_op jit(solution)/shard_map/ppermute | solution.py:547
  40.0 9.7 %collective-permute-start.20 = (bf16[4,64,128]{2,1,0:T(8,128)(2,1)S(1)}, bf16[4,64,128]{2,1,0:T(8,128)(2,1)S(1)}, u32[]{:S(2)}, u32[]{:S(2)}) collective-permute-start(bf16[4,64,128]{2,1,0:T(8,128)(2,1)S(1)} %get-tuple-element.63), channel_id=1, source_target_pairs={{0,8},{4,12},{8,0},{12,4},{16,24},{20,28},{24,16},{28,20},{1,9},{5... | collective-permute-start | bytes 196616 | tf_op jit(solution)/shard_map/ppermute | solution.py:547
  40.0 9.7 %collective-permute-start.19 = (bf16[4,64,128]{2,1,0:T(8,128)(2,1)S(1)}, bf16[4,64,128]{2,1,0:T(8,128)(2,1)S(1)}, u32[]{:S(2)}, u32[]{:S(2)}) collective-permute-start(bf16[4,64,128]{2,1,0:T(8,128)(2,1)S(1)} %get-tuple-element.64), channel_id=1, source_target_pairs={{0,16},{4,20},{8,24},{12,28},{16,0},{20,4},{24,8},{28,12},{1,17},{... | collective-permute-start | bytes 196616 | tf_op jit(solution)/shard_map/ppermute | solution.py:547
  43.7 6.2 %collective-permute-start.17 = (bf16[4,64,128]{2,1,0:T(8,128)(2,1)S(1)}, bf16[4,64,128]{2,1,0:T(8,128)(2,1)S(1)}, u32[]{:S(2)}, u32[]{:S(2)}) collective-permute-start(bf16[4,64,128]{2,1,0:T(8,128)(2,1)S(1)} %get-tuple-element.65), channel_id=1, source_target_pairs={{0,24},{4,28},{8,16},{12,20},{16,8},{20,12},{24,0},{28,4},{1,25},{... | collective-permute-start | bytes 196616 | tf_op jit(solution)/shard_map/ppermute | solution.py:547
  45.8 5.6 %collective-permute-start.16 = (bf16[4,64,128]{2,1,0:T(8,128)(2,1)S(1)}, bf16[4,64,128]{2,1,0:T(8,128)(2,1)S(1)}, u32[]{:S(2)}, u32[]{:S(2)}) collective-permute-start(bf16[4,64,128]{2,1,0:T(8,128)(2,1)S(1)} %get-tuple-element.66), channel_id=1, source_target_pairs={{0,8},{4,12},{8,0},{12,4},{16,24},{20,28},{24,16},{28,20},{1,9},{5... | collective-permute-start | bytes 196616 | tf_op jit(solution)/shard_map/ppermute | solution.py:547
  45.8 5.6 %collective-permute-start.15 = (bf16[4,64,128]{2,1,0:T(8,128)(2,1)S(1)}, bf16[4,64,128]{2,1,0:T(8,128)(2,1)S(1)}, u32[]{:S(2)}, u32[]{:S(2)}) collective-permute-start(bf16[4,64,128]{2,1,0:T(8,128)(2,1)S(1)} %get-tuple-element.67), channel_id=1, source_target_pairs={{0,16},{4,20},{8,24},{12,28},{16,0},{20,4},{24,8},{28,12},{1,17},{... | collective-permute-start | bytes 196616 | tf_op jit(solution)/shard_map/ppermute | solution.py:547
  51.5 3.4 %collective-permute-start.24 = (bf16[128,128]{1,0:T(8,128)(2,1)S(1)}, bf16[128,128]{1,0:T(8,128)(2,1)S(1)}, u32[]{:S(2)}, u32[]{:S(2)}) collective-permute-start(bf16[128,128]{1,0:T(8,128)(2,1)S(1)} %get-tuple-element.68), channel_id=1, source_target_pairs={{0,3},{1,2},{2,1},{3,0},{4,7},{5,6},{6,5},{7,4},{8,11},{9,10},{10,... | collective-permute-start | bytes 98312 | tf_op jit(solution)/shard_map/ppermute | solution.py:574
  51.6 3.3 %collective-permute-start.22 = (bf16[128,128]{1,0:T(8,128)(2,1)S(1)}, bf16[128,128]{1,0:T(8,128)(2,1)S(1)}, u32[]{:S(2)}, u32[]{:S(2)}) collective-permute-start(bf16[128,128]{1,0:T(8,128)(2,1)S(1)} %get-tuple-element.70), channel_id=1, source_target_pairs={{0,1},{1,0},{2,3},{3,2},{4,5},{5,4},{6,7},{7,6},{8,9},{9,8},{10,11... | collective-permute-start | bytes 98312 | tf_op jit(solution)/shard_map/ppermute | solution.py:574
  52.6 3.9 %collective-permute-start.23 = (bf16[128,128]{1,0:T(8,128)(2,1)S(1)}, bf16[128,128]{1,0:T(8,128)(2,1)S(1)}, u32[]{:S(2)}, u32[]{:S(2)}) collective-permute-start(bf16[128,128]{1,0:T(8,128)(2,1)S(1)} %get-tuple-element.71), channel_id=1, source_target_pairs={{0,2},{1,3},{2,0},{3,1},{4,6},{5,7},{6,4},{7,5},{8,10},{9,11},{10,... | collective-permute-start | bytes 98312 | tf_op jit(solution)/shard_map/ppermute | solution.py:574
  (1 other events, 3.2 us)

commit v7 on v6

--- a/solution.py
+++ b/solution.py
@@ -234,6 +234,10 @@
     return [(i, i ^ bits) for i in range(count)]
 
 
+def head_order(count):
+    return [n ^ (n >> 1) for n in range(count)]
+
+
 def head_columns(head, offset):
     return pl.ds(pl.multiple_of((head ^ offset) * DH, DH), DH)
 
@@ -261,7 +265,7 @@
     piece_refs, (keys_ref, values_ref) = refs[:-2], refs[-2:]
     head = lax.axis_index("head")
     short = keys_ref.shape[0]
-    for offset, piece in enumerate(piece_refs):
+    for offset, piece in zip(head_order(len(piece_refs)), piece_refs):
         columns = head_columns(head, offset)
         keys_ref[:, columns] = piece[:short, :]
         values_ref[:, columns] = piece[short:, :]
@@ -570,8 +574,9 @@
     packed = jnp.concatenate(
         [added(key_own, key_far), added(value_own, value_terms)], axis=1
     ).astype(jnp.bfloat16)
-    back = [packed[0]] + [
-        lax.ppermute(packed[k], "head", flips(head_count, k)) for k in range(1, head_count)
+    back = [
+        lax.ppermute(packed[k], "head", flips(head_count, k)) if k else packed[0]
+        for k in head_order(head_count)
     ]
     flat = jax.ShapeDtypeStruct(keys.shape, jnp.bfloat16)
     d_keys, d_values = pl.pallas_call(

time: 57.4 us -> 56.8 us (0.990)
  waiting for transfers between devices: 11.7 us -> 11 us
    ppermute x3, waiting for transfers between devices: 2.77 us -> 2.12 us  [whole_body(): lax.ppermute(packed[k], 'head', flips(head_count, k))]
where the time goes in v7:
time: 56.8 us; the launch traced here: 56.5 us
  starting transfers between devices  31.8 us (56%)
  Pallas kernels  12.5 us (22%)
  waiting for transfers between devices  11 us (19%)
  between operations  0.77 us (1%)
    ppermute x6, starting transfers between devices, from_far(): lax.ppermute(sums[pair - 1], 'seq', flips(seq_count, 2 * pair))  8.91 us
    ppermute x6, starting transfers between devices, along_far(): parts.append(lax.ppermute(own, 'seq', flips(seq_count, k)))  8.9 us
    ppermute x5, starting transfers between devices, to_near(): return lax.ppermute(part, 'seq', flips(seq_count, 1))  5.89 us
    pallas_call x1, Pallas kernels, whole_body(): pl.pallas_call(lambda *refs: probs_kernel(seq_count, key_starts, size, *r...  5.09 us
    pallas_call x1, Pallas kernels, whole_body(): pl.pallas_call(lambda *refs: dscores_kernel(value_starts, size, *refs), i...  4.33 us
    ppermute x3, waiting for transfers between devices, whole_body(): lax.ppermute(pieces[k], 'head', flips(head_count, k))  3.25 us
    ppermute x3, starting transfers between devices, whole_body(): lax.ppermute(pieces[k], 'head', flips(head_count, k))  3.15 us
    ppermute x6, waiting for transfers between devices, along_far(): parts.append(lax.ppermute(own, 'seq', flips(seq_count, k)))  2.73 us
  transfers between devices with their start and end apart: 25, of which 10 were waited for; matrix products, arithmetic and copies ran while one was open for 0% of the time, Pallas kernels for 19%

profile of v7, /device:TPU:0, one launch (start us, length us, event | category | flops | bytes accessed | tf_op | source)
XLA Modules:
  0.0 56.5 jit_solution(167281950468541276)
XLA Ops:
  0.6 0.9 %shard_map.93 = (bf16[128,128]{1,0:T(8,128)(2,1)S(1)}, bf16[128,128]{1,0:T(8,128)(2,1)S(1)}, bf16[128,128]{1,0:T(8,128)(2,1)S(1)}, bf16[128,128]{1,0:T(8,128)(2,1)S(1)}) custom-call(bf16[64,512]{1,0:T(8,128)(2,1)} %refs_0_.2, bf16[64,512]{1,0:T(8,128)(2,1)} %refs_1_.2), custom_call_target="tpu_custom_call" | custom-call | tf_op jit(solution)/shard_map/pallas_call | solution.py:468
  2.1 2.6 %collective-permute-start.1 = (bf16[128,128]{1,0:T(8,128)(2,1)S(1)}, bf16[128,128]{1,0:T(8,128)(2,1)S(1)}, u32[]{:S(2)}, u32[]{:S(2)}) collective-permute-start(bf16[128,128]{1,0:T(8,128)(2,1)S(1)} %get-tuple-element.33), channel_id=1, source_target_pairs={{0,2},{1,3},{2,0},{3,1},{4,6},{5,7},{6,4},{7,5},{8,10},{9,11},{10,... | collective-permute-start | bytes 98312 | tf_op jit(solution)/shard_map/ppermute | solution.py:477
  4.7 1.9 %collective-permute-done.1 = bf16[128,128]{1,0:T(8,128)(2,1)S(1)} collective-permute-done((bf16[128,128]{1,0:T(8,128)(2,1)S(1)}, bf16[128,128]{1,0:T(8,128)(2,1)S(1)}, u32[]{:S(2)}, u32[]{:S(2)}) %collective-permute-start.1) | collective-permute-done | bytes 32800 | tf_op jit(solution)/shard_map/ppermute | solution.py:477
  6.6 1.4 %collective-permute-done.2 = bf16[128,128]{1,0:T(8,128)(2,1)S(1)} collective-permute-done((bf16[128,128]{1,0:T(8,128)(2,1)S(1)}, bf16[128,128]{1,0:T(8,128)(2,1)S(1)}, u32[]{:S(2)}, u32[]{:S(2)}) %collective-permute-start.2) | collective-permute-done | bytes 32800 | tf_op jit(solution)/shard_map/ppermute | solution.py:477
  8.0 3.7 %collective-permute-start.8 = (bf16[4,64,128]{2,1,0:T(8,128)(2,1)S(1)}, bf16[4,64,128]{2,1,0:T(8,128)(2,1)S(1)}, u32[]{:S(2)}, u32[]{:S(2)}) collective-permute-start(bf16[4,64,128]{2,1,0:T(8,128)(2,1)S(1)} %pad_maximum_fusion.refs_4_), channel_id=1, source_target_pairs={{0,24},{4,28},{8,16},{12,20},{16,8},{20,12},{24,0},{28,4},{1,25},{... | collective-permute-start | bytes 196616 | tf_op jit(solution)/shard_map/ppermute | solution.py:483
  12.5 1.5 %collective-permute-start.3 = (bf16[4,64,128]{2,1,0:T(8,128)(2,1)S(1)}, bf16[4,64,128]{2,1,0:T(8,128)(2,1)S(1)}, u32[]{:S(2)}, u32[]{:S(2)}) collective-permute-start(bf16[4,64,128]{2,1,0:T(8,128)(2,1)S(1)} %pad_maximum_fusion.refs_4_), channel_id=1, source_target_pairs={{0,4},{4,0},{8,12},{12,8},{16,20},{20,16},{24,28},{28,24},{1,5},{5... | collective-permute-start | bytes 196616 | tf_op jit(solution)/shard_map/ppermute | solution.py:487
  14.9 1.5 %collective-permute-start.9 = (bf16[4,64,128]{2,1,0:T(8,128)(2,1)S(1)}, bf16[4,64,128]{2,1,0:T(8,128)(2,1)S(1)}, u32[]{:S(2)}, u32[]{:S(2)}) collective-permute-start(bf16[4,64,128]{2,1,0:T(8,128)(2,1)S(1)} %collective-permute-done.8.refs_10_), channel_id=1, source_target_pairs={{0,4},{4,0},{8,12},{12,8},{16,20},{20,16},{24,28},{28,24},{1,5},{5... | collective-permute-start | bytes 196616 | tf_op jit(solution)/shard_map/ppermute | solution.py:487
  16.8 1.5 %collective-permute-start.7 = (bf16[4,64,128]{2,1,0:T(8,128)(2,1)S(1)}, bf16[4,64,128]{2,1,0:T(8,128)(2,1)S(1)}, u32[]{:S(2)}, u32[]{:S(2)}) collective-permute-start(bf16[4,64,128]{2,1,0:T(8,128)(2,1)S(1)} %collective-permute-done.6.refs_8_), channel_id=1, source_target_pairs={{0,4},{4,0},{8,12},{12,8},{16,20},{20,16},{24,28},{28,24},{1,5},{5... | collective-permute-start | bytes 196616 | tf_op jit(solution)/shard_map/ppermute | solution.py:487
  19.1 3.7 %collective-permute-start.13 = (bf16[8,64,128]{2,1,0:T(8,128)(2,1)S(1)}, bf16[8,64,128]{2,1,0:T(8,128)(2,1)S(1)}, u32[]{:S(2)}, u32[]{:S(2)}) collective-permute-start(bf16[8,64,128]{2,1,0:T(8,128)(2,1)S(1)} %constant_dynamic-update-slice_fusion.refs_4_), channel_id=1, source_target_pairs={{0,24},{4,28},{8,16},{12,20},{16,8},{20,12},{24,0},{28,4},{1,25},{... | collective-permute-start | bytes 393224 | tf_op jit(solution)/shard_map/ppermute | solution.py:483
  23.5 5.1 %shard_map.94 = (bf16[4,832,512]{2,1,0:T(8,128)(2,1)S(1)}, bf16[4,832,128]{2,1,0:T(8,128)(2,1)S(1)}, f32[4,4,64,128]{3,2,1,0:T(8,128)S(1)}, bf16[4,4,64,128]{3,2...) custom-call(s32[4,8]{1,0:T(4,128)} %refs_0_.3, ...), custom_call_target="tpu_custom_call" | custom-call | flops 1744830464 | bytes 6815744 | tf_op jit(solution)/shard_map/pallas_call | solution.py:512
  28.6 1.3 %collective-permute-start.18 = (bf16[4,4,64,128]{3,2,1,0:T(8,128)(2,1)S(1)}, bf16[4,4,64,128]{3,2,1,0:T(8,128)(2,1)S(1)}, u32[]{:S(2)}, u32[]{:S(2)}) collective-permute-start(bf16[4,4,64,128]{3,2,1,0:T(8,128)(2,1)S(1)} %get-tuple-element.44), channel_id=1, source_target_pairs={{0,4},{4,0},{8,12},{12,8},{16,20},{20,16},{24,28},{28,24},{1,5},{5... | collective-permute-start | bytes 786440 | tf_op jit(solution)/shard_map/ppermute | solution.py:534
  30.0 2.1 %collective-permute-done.11.refs_5_ = bf16[8,64,128]{2,1,0:T(8,128)(2,1)S(1)} collective-permute-done((bf16[8,64,128]{2,1,0:T(8,128)(2,1)S(1)}, bf16[8,64,128]{2,1,0:T(8,128)(2,1)S(1)}, u32[]{:S(2)}, u32[]{:S(2)}) %collective-permute-start.11) | collective-permute-done | bytes 131104 | tf_op jit(solution)/shard_map/ppermute | solution.py:483
  32.0 4.3 %shard_map.95 = (bf16[256,1024]{1,0:T(8,128)(2,1)}, bf16[4,832,512]{2,1,0:T(8,128)(2,1)S(1)}, f32[4,4,64,128]{3,2,1,0:T(8,128)S(1)}, bf16[4,4,64,128]{3,2,1,0:T(8,128)(2,1)S(1)}) custom-call(s32[4,13]{1,0:T(4,128)S(1)} %get-tuple-element.35.refs_0_, bf16[256,1024]{1,0:T(8,128)(2,1)S(1)} %get-tuple-element.36.refs_1_, ...), custom_call_target="tpu_custom_call" | custom-call | flops 2617245696 | bytes 6815744 | tf_op jit(solution)/shard_map/pallas_call | solution.py:535
  36.4 1.5 %collective-permute-start.14 = (bf16[4,4,64,128]{3,2,1,0:T(8,128)(2,1)S(1)}, bf16[4,4,64,128]{3,2,1,0:T(8,128)(2,1)S(1)}, u32[]{:S(2)}, u32[]{:S(2)}) collective-permute-start(bf16[4,4,64,128]{3,2,1,0:T(8,128)(2,1)S(1)} %get-tuple-element.42), channel_id=1, source_target_pairs={{0,4},{4,0},{8,12},{12,8},{16,20},{20,16},{24,28},{28,24},{1,5},{5... | collective-permute-start | bytes 786440 | tf_op jit(solution)/shard_map/ppermute | solution.py:543
  38.0 2.1 %collective-permute-start.21 = (bf16[4,64,128]{2,1,0:T(8,128)(2,1)S(1)}, bf16[4,64,128]{2,1,0:T(8,128)(2,1)S(1)}, u32[]{:S(2)}, u32[]{:S(2)}) collective-permute-start(bf16[4,64,128]{2,1,0:T(8,128)(2,1)S(1)} %get-tuple-element.62), channel_id=1, source_target_pairs={{0,24},{4,28},{8,16},{12,20},{16,8},{20,12},{24,0},{28,4},{1,25},{... | collective-permute-start | bytes 196616 | tf_op jit(solution)/shard_map/ppermute | solution.py:551
  40.0 2.4 %collective-permute-start.19 = (bf16[4,64,128]{2,1,0:T(8,128)(2,1)S(1)}, bf16[4,64,128]{2,1,0:T(8,128)(2,1)S(1)}, u32[]{:S(2)}, u32[]{:S(2)}) collective-permute-start(bf16[4,64,128]{2,1,0:T(8,128)(2,1)S(1)} %get-tuple-element.64), channel_id=1, source_target_pairs={{0,16},{4,20},{8,24},{12,28},{16,0},{20,4},{24,8},{28,12},{1,17},{... | collective-permute-start | bytes 196616 | tf_op jit(solution)/shard_map/ppermute | solution.py:551
  42.4 1.2 %collective-permute-done.14 = bf16[4,4,64,128]{3,2,1,0:T(8,128)(2,1)S(1)} collective-permute-done((bf16[4,4,64,128]{3,2,1,0:T(8,128)(2,1)S(1)}, bf16[4,4,64,128]{3,2,1,0:T(8,128)(2,1)S(1)}, u32[]{:S(2)}, u32[]{:S(2)}) %collective-permute-start.14) | collective-permute-done | bytes 262176 | tf_op jit(solution)/shard_map/ppermute | solution.py:543
  43.7 2.1 %collective-permute-start.17 = (bf16[4,64,128]{2,1,0:T(8,128)(2,1)S(1)}, bf16[4,64,128]{2,1,0:T(8,128)(2,1)S(1)}, u32[]{:S(2)}, u32[]{:S(2)}) collective-permute-start(bf16[4,64,128]{2,1,0:T(8,128)(2,1)S(1)} %get-tuple-element.65), channel_id=1, source_target_pairs={{0,24},{4,28},{8,16},{12,20},{16,8},{20,12},{24,0},{28,4},{1,25},{... | collective-permute-start | bytes 196616 | tf_op jit(solution)/shard_map/ppermute | solution.py:551
  45.8 2.4 %collective-permute-start.15 = (bf16[4,64,128]{2,1,0:T(8,128)(2,1)S(1)}, bf16[4,64,128]{2,1,0:T(8,128)(2,1)S(1)}, u32[]{:S(2)}, u32[]{:S(2)}) collective-permute-start(bf16[4,64,128]{2,1,0:T(8,128)(2,1)S(1)} %get-tuple-element.67), channel_id=1, source_target_pairs={{0,16},{4,20},{8,24},{12,28},{16,0},{20,4},{24,8},{28,12},{1,17},{... | collective-permute-start | bytes 196616 | tf_op jit(solution)/shard_map/ppermute | solution.py:551
  48.2 1.5 %shard_map.96 = bf16[256,1024]{1,0:T(8,128)(2,1)} custom-call(bf16[4,832,512]{2,1,0:T(8,128)(2,1)S(1)} %get-tuple-element.47.refs_0_, bf16[4,832,128]{2,1,0:T(8,128)(2,1)S(1)} %get-tuple-element.48.refs_1_), custom_call_target="tpu_custom_call" | custom-call | flops 872415232 | bytes 6815744 | tf_op jit(solution)/shard_map/pallas_call | solution.py:564
  49.9 1.5 %collective-permute-done.16 = bf16[4,64,128]{2,1,0:T(8,128)(2,1)S(1)} collective-permute-done((bf16[4,64,128]{2,1,0:T(8,128)(2,1)S(1)}, bf16[4,64,128]{2,1,0:T(8,128)(2,1)S(1)}, u32[]{:S(2)}, u32[]{:S(2)}) %collective-permute-start.16) | collective-permute-done | bytes 65568 | tf_op jit(solution)/shard_map/ppermute | solution.py:551
  51.5 0.9 %collective-permute-start.24 = (bf16[128,128]{1,0:T(8,128)(2,1)S(1)}, bf16[128,128]{1,0:T(8,128)(2,1)S(1)}, u32[]{:S(2)}, u32[]{:S(2)}) collective-permute-start(bf16[128,128]{1,0:T(8,128)(2,1)S(1)} %get-tuple-element.68), channel_id=1, source_target_pairs={{0,2},{1,3},{2,0},{3,1},{4,6},{5,7},{6,4},{7,5},{8,10},{9,11},{10,... | collective-permute-start | bytes 98312 | tf_op jit(solution)/shard_map/ppermute | solution.py:578
  52.5 1.3 %collective-permute-start.23 = (bf16[128,128]{1,0:T(8,128)(2,1)S(1)}, bf16[128,128]{1,0:T(8,128)(2,1)S(1)}, u32[]{:S(2)}, u32[]{:S(2)}) collective-permute-start(bf16[128,128]{1,0:T(8,128)(2,1)S(1)} %get-tuple-element.71), channel_id=1, source_target_pairs={{0,3},{1,2},{2,1},{3,0},{4,7},{5,6},{6,5},{7,4},{8,11},{9,10},{10,... | collective-permute-start | bytes 98312 | tf_op jit(solution)/shard_map/ppermute | solution.py:578
  53.7 1.8 %collective-permute-done.24.refs_3_ = bf16[128,128]{1,0:T(8,128)(2,1)S(1)} collective-permute-done((bf16[128,128]{1,0:T(8,128)(2,1)S(1)}, bf16[128,128]{1,0:T(8,128)(2,1)S(1)}, u32[]{:S(2)}, u32[]{:S(2)}) %collective-permute-start.24) | collective-permute-done | bytes 32800 | tf_op jit(solution)/shard_map/ppermute | solution.py:578
  (48 shorter events, 5.7 us)
Async XLA Ops:
  1.6 3.2 %collective-permute-start = (bf16[128,128]{1,0:T(8,128)(2,1)S(1)}, bf16[128,128]{1,0:T(8,128)(2,1)S(1)}, u32[]{:S(2)}, u32[]{:S(2)}) collective-permute-start(bf16[128,128]{1,0:T(8,128)(2,1)S(1)} %get-tuple-element.32), channel_id=1, source_target_pairs={{0,1},{1,0},{2,3},{3,2},{4,5},{5,4},{6,7},{7,6},{8,9},{9,8},{10,11... | collective-permute-start | bytes 98312 | tf_op jit(solution)/shard_map/ppermute | solution.py:477
  2.1 4.5 %collective-permute-start.1 = (bf16[128,128]{1,0:T(8,128)(2,1)S(1)}, bf16[128,128]{1,0:T(8,128)(2,1)S(1)}, u32[]{:S(2)}, u32[]{:S(2)}) collective-permute-start(bf16[128,128]{1,0:T(8,128)(2,1)S(1)} %get-tuple-element.33), channel_id=1, source_target_pairs={{0,2},{1,3},{2,0},{3,1},{4,6},{5,7},{6,4},{7,5},{8,10},{9,11},{10,... | collective-permute-start | bytes 98312 | tf_op jit(solution)/shard_map/ppermute | solution.py:477
  4.6 3.3 %collective-permute-start.2 = (bf16[128,128]{1,0:T(8,128)(2,1)S(1)}, bf16[128,128]{1,0:T(8,128)(2,1)S(1)}, u32[]{:S(2)}, u32[]{:S(2)}) collective-permute-start(bf16[128,128]{1,0:T(8,128)(2,1)S(1)} %get-tuple-element.34), channel_id=1, source_target_pairs={{0,3},{1,2},{2,1},{3,0},{4,7},{5,6},{6,5},{7,4},{8,11},{9,10},{10,... | collective-permute-start | bytes 98312 | tf_op jit(solution)/shard_map/ppermute | solution.py:477
  8.0 6.8 %collective-permute-start.8 = (bf16[4,64,128]{2,1,0:T(8,128)(2,1)S(1)}, bf16[4,64,128]{2,1,0:T(8,128)(2,1)S(1)}, u32[]{:S(2)}, u32[]{:S(2)}) collective-permute-start(bf16[4,64,128]{2,1,0:T(8,128)(2,1)S(1)} %pad_maximum_fusion.refs_4_), channel_id=1, source_target_pairs={{0,24},{4,28},{8,16},{12,20},{16,8},{20,12},{24,0},{28,4},{1,25},{... | collective-permute-start | bytes 196616 | tf_op jit(solution)/shard_map/ppermute | solution.py:483
  11.7 5.1 %collective-permute-start.6 = (bf16[4,64,128]{2,1,0:T(8,128)(2,1)S(1)}, bf16[4,64,128]{2,1,0:T(8,128)(2,1)S(1)}, u32[]{:S(2)}, u32[]{:S(2)}) collective-permute-start(bf16[4,64,128]{2,1,0:T(8,128)(2,1)S(1)} %pad_maximum_fusion.refs_4_), channel_id=1, source_target_pairs={{0,8},{4,12},{8,0},{12,4},{16,24},{20,28},{24,16},{28,20},{1,9},{5... | collective-permute-start | bytes 196616 | tf_op jit(solution)/shard_map/ppermute | solution.py:483
  11.7 6.6 %collective-permute-start.4 = (bf16[4,64,128]{2,1,0:T(8,128)(2,1)S(1)}, bf16[4,64,128]{2,1,0:T(8,128)(2,1)S(1)}, u32[]{:S(2)}, u32[]{:S(2)}) collective-permute-start(bf16[4,64,128]{2,1,0:T(8,128)(2,1)S(1)} %pad_maximum_fusion.refs_4_), channel_id=1, source_target_pairs={{0,16},{4,20},{8,24},{12,28},{16,0},{20,4},{24,8},{28,12},{1,17},{... | collective-permute-start | bytes 196616 | tf_op jit(solution)/shard_map/ppermute | solution.py:483
  12.5 10.3 %collective-permute-start.3 = (bf16[4,64,128]{2,1,0:T(8,128)(2,1)S(1)}, bf16[4,64,128]{2,1,0:T(8,128)(2,1)S(1)}, u32[]{:S(2)}, u32[]{:S(2)}) collective-permute-start(bf16[4,64,128]{2,1,0:T(8,128)(2,1)S(1)} %pad_maximum_fusion.refs_4_), channel_id=1, source_target_pairs={{0,4},{4,0},{8,12},{12,8},{16,20},{20,16},{24,28},{28,24},{1,5},{5... | collective-permute-start | bytes 196616 | tf_op jit(solution)/shard_map/ppermute | solution.py:487
  14.0 5.1 %collective-permute-start.10 = (bf16[4,64,128]{2,1,0:T(8,128)(2,1)S(1)}, bf16[4,64,128]{2,1,0:T(8,128)(2,1)S(1)}, u32[]{:S(2)}, u32[]{:S(2)}) collective-permute-start(bf16[4,64,128]{2,1,0:T(8,128)(2,1)S(1)} %pad_maximum_fusion.1), channel_id=1, source_target_pairs={{0,4},{4,0},{8,12},{12,8},{16,20},{20,16},{24,28},{28,24},{1,5},{5... | collective-permute-start | bytes 196616 | tf_op jit(solution)/shard_map/ppermute | solution.py:487
  14.9 7.9 %collective-permute-start.9 = (bf16[4,64,128]{2,1,0:T(8,128)(2,1)S(1)}, bf16[4,64,128]{2,1,0:T(8,128)(2,1)S(1)}, u32[]{:S(2)}, u32[]{:S(2)}) collective-permute-start(bf16[4,64,128]{2,1,0:T(8,128)(2,1)S(1)} %collective-permute-done.8.refs_10_), channel_id=1, source_target_pairs={{0,4},{4,0},{8,12},{12,8},{16,20},{20,16},{24,28},{28,24},{1,5},{5... | collective-permute-start | bytes 196616 | tf_op jit(solution)/shard_map/ppermute | solution.py:487
  16.8 6.8 %collective-permute-start.7 = (bf16[4,64,128]{2,1,0:T(8,128)(2,1)S(1)}, bf16[4,64,128]{2,1,0:T(8,128)(2,1)S(1)}, u32[]{:S(2)}, u32[]{:S(2)}) collective-permute-start(bf16[4,64,128]{2,1,0:T(8,128)(2,1)S(1)} %collective-permute-done.6.refs_8_), channel_id=1, source_target_pairs={{0,4},{4,0},{8,12},{12,8},{16,20},{20,16},{24,28},{28,24},{1,5},{5... | collective-permute-start | bytes 196616 | tf_op jit(solution)/shard_map/ppermute | solution.py:487
  18.3 5.2 %collective-permute-start.5 = (bf16[4,64,128]{2,1,0:T(8,128)(2,1)S(1)}, bf16[4,64,128]{2,1,0:T(8,128)(2,1)S(1)}, u32[]{:S(2)}, u32[]{:S(2)}) collective-permute-start(bf16[4,64,128]{2,1,0:T(8,128)(2,1)S(1)} %collective-permute-done.4.refs_6_), channel_id=1, source_target_pairs={{0,4},{4,0},{8,12},{12,8},{16,20},{20,16},{24,28},{28,24},{1,5},{5... | collective-permute-start | bytes 196616 | tf_op jit(solution)/shard_map/ppermute | solution.py:487
  19.1 10.9 %collective-permute-start.13 = (bf16[8,64,128]{2,1,0:T(8,128)(2,1)S(1)}, bf16[8,64,128]{2,1,0:T(8,128)(2,1)S(1)}, u32[]{:S(2)}, u32[]{:S(2)}) collective-permute-start(bf16[8,64,128]{2,1,0:T(8,128)(2,1)S(1)} %constant_dynamic-update-slice_fusion.refs_4_), channel_id=1, source_target_pairs={{0,24},{4,28},{8,16},{12,20},{16,8},{20,12},{24,0},{28,4},{1,25},{... | collective-permute-start | bytes 393224 | tf_op jit(solution)/shard_map/ppermute | solution.py:483
  22.8 7.2 %collective-permute-start.12 = (bf16[8,64,128]{2,1,0:T(8,128)(2,1)S(1)}, bf16[8,64,128]{2,1,0:T(8,128)(2,1)S(1)}, u32[]{:S(2)}, u32[]{:S(2)}) collective-permute-start(bf16[8,64,128]{2,1,0:T(8,128)(2,1)S(1)} %constant_dynamic-update-slice_fusion.refs_4_), channel_id=1, source_target_pairs={{0,8},{4,12},{8,0},{12,4},{16,24},{20,28},{24,16},{28,20},{1,9},{5... | collective-permute-start | bytes 393224 | tf_op jit(solution)/shard_map/ppermute | solution.py:483
  22.8 9.3 %collective-permute-start.11 = (bf16[8,64,128]{2,1,0:T(8,128)(2,1)S(1)}, bf16[8,64,128]{2,1,0:T(8,128)(2,1)S(1)}, u32[]{:S(2)}, u32[]{:S(2)}) collective-permute-start(bf16[8,64,128]{2,1,0:T(8,128)(2,1)S(1)} %constant_dynamic-update-slice_fusion.refs_4_), channel_id=1, source_target_pairs={{0,16},{4,20},{8,24},{12,28},{16,0},{20,4},{24,8},{28,12},{1,17},{... | collective-permute-start | bytes 393224 | tf_op jit(solution)/shard_map/ppermute | solution.py:483
  28.6 9.2 %collective-permute-start.18 = (bf16[4,4,64,128]{3,2,1,0:T(8,128)(2,1)S(1)}, bf16[4,4,64,128]{3,2,1,0:T(8,128)(2,1)S(1)}, u32[]{:S(2)}, u32[]{:S(2)}) collective-permute-start(bf16[4,4,64,128]{3,2,1,0:T(8,128)(2,1)S(1)} %get-tuple-element.44), channel_id=1, source_target_pairs={{0,4},{4,0},{8,12},{12,8},{16,20},{20,16},{24,28},{28,24},{1,5},{5... | collective-permute-start | bytes 786440 | tf_op jit(solution)/shard_map/ppermute | solution.py:534
  36.4 7.2 %collective-permute-start.14 = (bf16[4,4,64,128]{3,2,1,0:T(8,128)(2,1)S(1)}, bf16[4,4,64,128]{3,2,1,0:T(8,128)(2,1)S(1)}, u32[]{:S(2)}, u32[]{:S(2)}) collective-permute-start(bf16[4,4,64,128]{3,2,1,0:T(8,128)(2,1)S(1)} %get-tuple-element.42), channel_id=1, source_target_pairs={{0,4},{4,0},{8,12},{12,8},{16,20},{20,16},{24,28},{28,24},{1,5},{5... | collective-permute-start | bytes 786440 | tf_op jit(solution)/shard_map/ppermute | solution.py:543
  38.0 7.8 %collective-permute-start.21 = (bf16[4,64,128]{2,1,0:T(8,128)(2,1)S(1)}, bf16[4,64,128]{2,1,0:T(8,128)(2,1)S(1)}, u32[]{:S(2)}, u32[]{:S(2)}) collective-permute-start(bf16[4,64,128]{2,1,0:T(8,128)(2,1)S(1)} %get-tuple-element.62), channel_id=1, source_target_pairs={{0,24},{4,28},{8,16},{12,20},{16,8},{20,12},{24,0},{28,4},{1,25},{... | collective-permute-start | bytes 196616 | tf_op jit(solution)/shard_map/ppermute | solution.py:551
  40.0 9.7 %collective-permute-start.20 = (bf16[4,64,128]{2,1,0:T(8,128)(2,1)S(1)}, bf16[4,64,128]{2,1,0:T(8,128)(2,1)S(1)}, u32[]{:S(2)}, u32[]{:S(2)}) collective-permute-start(bf16[4,64,128]{2,1,0:T(8,128)(2,1)S(1)} %get-tuple-element.63), channel_id=1, source_target_pairs={{0,8},{4,12},{8,0},{12,4},{16,24},{20,28},{24,16},{28,20},{1,9},{5... | collective-permute-start | bytes 196616 | tf_op jit(solution)/shard_map/ppermute | solution.py:551
  40.0 9.7 %collective-permute-start.19 = (bf16[4,64,128]{2,1,0:T(8,128)(2,1)S(1)}, bf16[4,64,128]{2,1,0:T(8,128)(2,1)S(1)}, u32[]{:S(2)}, u32[]{:S(2)}) collective-permute-start(bf16[4,64,128]{2,1,0:T(8,128)(2,1)S(1)} %get-tuple-element.64), channel_id=1, source_target_pairs={{0,16},{4,20},{8,24},{12,28},{16,0},{20,4},{24,8},{28,12},{1,17},{... | collective-permute-start | bytes 196616 | tf_op jit(solution)/shard_map/ppermute | solution.py:551
  43.7 6.2 %collective-permute-start.17 = (bf16[4,64,128]{2,1,0:T(8,128)(2,1)S(1)}, bf16[4,64,128]{2,1,0:T(8,128)(2,1)S(1)}, u32[]{:S(2)}, u32[]{:S(2)}) collective-permute-start(bf16[4,64,128]{2,1,0:T(8,128)(2,1)S(1)} %get-tuple-element.65), channel_id=1, source_target_pairs={{0,24},{4,28},{8,16},{12,20},{16,8},{20,12},{24,0},{28,4},{1,25},{... | collective-permute-start | bytes 196616 | tf_op jit(solution)/shard_map/ppermute | solution.py:551
  45.8 5.6 %collective-permute-start.16 = (bf16[4,64,128]{2,1,0:T(8,128)(2,1)S(1)}, bf16[4,64,128]{2,1,0:T(8,128)(2,1)S(1)}, u32[]{:S(2)}, u32[]{:S(2)}) collective-permute-start(bf16[4,64,128]{2,1,0:T(8,128)(2,1)S(1)} %get-tuple-element.66), channel_id=1, source_target_pairs={{0,8},{4,12},{8,0},{12,4},{16,24},{20,28},{24,16},{28,20},{1,9},{5... | collective-permute-start | bytes 196616 | tf_op jit(solution)/shard_map/ppermute | solution.py:551
  45.8 5.6 %collective-permute-start.15 = (bf16[4,64,128]{2,1,0:T(8,128)(2,1)S(1)}, bf16[4,64,128]{2,1,0:T(8,128)(2,1)S(1)}, u32[]{:S(2)}, u32[]{:S(2)}) collective-permute-start(bf16[4,64,128]{2,1,0:T(8,128)(2,1)S(1)} %get-tuple-element.67), channel_id=1, source_target_pairs={{0,16},{4,20},{8,24},{12,28},{16,0},{20,4},{24,8},{28,12},{1,17},{... | collective-permute-start | bytes 196616 | tf_op jit(solution)/shard_map/ppermute | solution.py:551
  51.5 4.0 %collective-permute-start.24 = (bf16[128,128]{1,0:T(8,128)(2,1)S(1)}, bf16[128,128]{1,0:T(8,128)(2,1)S(1)}, u32[]{:S(2)}, u32[]{:S(2)}) collective-permute-start(bf16[128,128]{1,0:T(8,128)(2,1)S(1)} %get-tuple-element.68), channel_id=1, source_target_pairs={{0,2},{1,3},{2,0},{3,1},{4,6},{5,7},{6,4},{7,5},{8,10},{9,11},{10,... | collective-permute-start | bytes 98312 | tf_op jit(solution)/shard_map/ppermute | solution.py:578
  52.5 3.4 %collective-permute-start.23 = (bf16[128,128]{1,0:T(8,128)(2,1)S(1)}, bf16[128,128]{1,0:T(8,128)(2,1)S(1)}, u32[]{:S(2)}, u32[]{:S(2)}) collective-permute-start(bf16[128,128]{1,0:T(8,128)(2,1)S(1)} %get-tuple-element.71), channel_id=1, source_target_pairs={{0,3},{1,2},{2,1},{3,0},{4,7},{5,6},{6,5},{7,4},{8,11},{9,10},{10,... | collective-permute-start | bytes 98312 | tf_op jit(solution)/shard_map/ppermute | solution.py:578
  (1 other events, 3.1 us)
